TPU v7x, 32 devices: a whole 2x2x4 slice. The times are simulated.
32 devices in a mesh: ent: 8 (over z, y), sec: 4 (over x, core).
Axes of the slice: x: 2, y: 2, z: 4, core: 2. Of those that a mesh axis runs over, the one named last changes fastest.
Arguments:
- features: bfloat16 [1024, 256], P('ent'), may hold values from -6 to 6
- theta: bfloat16 [256, 256], replicated, may hold values from -3 to 3
- section_weight: float32 [16384], P(('ent', 'sec')), may hold values from 0.5 to 2
- pair_rows: int32 [32, 8, 512], P(('ent', 'sec')), may hold values from 0 to 511
- pair_cols: int32 [32, 8, 512], P(('ent', 'sec')), may hold values from 0 to 127
- pair_counts: int32 [32, 8], P(('ent', 'sec')), may hold values from 0 to 512, as said below
- cotangent: bfloat16 [1024, 256], P('ent'), may hold values from -24 to 24
Outputs:
- activated: bfloat16 [1024, 256], P('ent')
- grad_features: bfloat16 [1024, 256], P('ent')
- grad_theta: float32 [256, 256], replicated
- grad_weight: float32 [16384], P(('ent', 'sec'))
Inputs may be any that keep to these rules, and one draw needn't show every extreme that they name: Only the first pair_counts[k, j] slots of shard k and block j are used; some shard uses all 512 slots of some block.
All inputs are finite; a program needn't handle non-finite values.
Results may differ from a plain program's by a relative error of at most 0.0059.
Values may be sent and summed in bfloat16 or wider, within the bound.
No kernel may reach another device: no remote copies, remote signals or barrier semaphores. Data moves between devices by JAX's collectives and lax.ppermute only.
A program may use at most 64 MiB of HBM per device.

v0:
```python
import jax
import jax.numpy as jnp
from jax import lax
from jax.sharding import PartitionSpec as P


def hot_table(indices, live_slots, offset, table_width):
    hits = (indices - offset)[:, None] == jnp.arange(table_width, dtype=jnp.int32)[None, :]
    return (hits & live_slots[:, None]).astype(jnp.bfloat16)


def body(features, theta, section_weight, pair_rows, pair_cols, pair_counts, cotangent):
    ent_dev = features.shape[0]
    feature_width = features.shape[1]
    sec_dev = section_weight.shape[0]
    blocks_count = pair_rows.shape[1]
    slot_count = pair_rows.shape[2]
    own_block = lax.axis_index("ent")
    row_lists = pair_rows[0]
    col_lists = pair_cols[0]
    usable = jnp.arange(slot_count, dtype=jnp.int32)[None, :] < pair_counts[0][:, None]
    usable_float = usable.astype(jnp.float32)
    entity_index = jnp.arange(blocks_count, dtype=jnp.int32)[:, None] * ent_dev + col_lists
    local_degree = jax.ops.segment_sum(
        usable_float.reshape(-1), entity_index.reshape(-1), num_segments=blocks_count * ent_dev
    )
    entity_degree = lax.psum(local_degree, ("ent", "sec"))
    own_degree = lax.dynamic_slice_in_dim(entity_degree, own_block * ent_dev, ent_dev)
    entity_scale = lax.rsqrt(1.0 + own_degree)[:, None]
    sec_count = jax.ops.segment_sum(
        usable_float.reshape(-1), row_lists.reshape(-1), num_segments=sec_dev
    )
    section_scale = (section_weight / (1.0 + sec_count))[:, None]

    def entity_fold(running, incoming, start_row):
        row_count = incoming.shape[0]
        span_width = min(row_count, ent_dev)
        block_span = max(row_count // ent_dev, 1)
        offset = start_row

        def add_block(turn_index, accum):
            row_slots = lax.dynamic_index_in_dim(row_lists, turn_index, 0, keepdims=False)
            col_slots = lax.dynamic_index_in_dim(col_lists, turn_index, 0, keepdims=False)
            live_slots = lax.dynamic_index_in_dim(usable, turn_index, 0, keepdims=False)
            values = lax.dynamic_slice_in_dim(incoming, turn_index * span_width, span_width, 0)
            col_hot = hot_table(col_slots, live_slots, offset, span_width)
            row_hot = hot_table(row_slots, live_slots, 0, sec_dev)
            picked = jnp.dot(col_hot, values, preferred_element_type=jnp.float32).astype(
                jnp.bfloat16
            )
            return accum + jnp.einsum(
                "ps,pf->sf", row_hot, picked, preferred_element_type=jnp.float32
            )

        return lax.fori_loop(0, block_span, add_block, running)

    def entity_terms(messages, start_row):
        span_width = min(lax.axis_size("ent") * ent_dev, ent_dev)
        block_span = max(lax.axis_size("ent") * ent_dev // ent_dev, 1)
        offset = start_row

        def block_term(turn_index):
            row_slots = lax.dynamic_index_in_dim(row_lists, turn_index, 0, keepdims=False)
            col_slots = lax.dynamic_index_in_dim(col_lists, turn_index, 0, keepdims=False)
            live_slots = lax.dynamic_index_in_dim(usable, turn_index, 0, keepdims=False)
            row_hot = hot_table(row_slots, live_slots, 0, sec_dev)
            col_hot = hot_table(col_slots, live_slots, offset, span_width)
            picked = jnp.dot(row_hot, messages, preferred_element_type=jnp.float32).astype(
                jnp.bfloat16
            )
            return jnp.einsum("pw,pf->wf", col_hot, picked, preferred_element_type=jnp.float32)

        pieces = lax.map(block_term, jnp.arange(block_span, dtype=jnp.int32))
        return pieces.reshape(block_span * span_width, feature_width)

    def collect(messages):
        partial_sum = lax.psum_scatter(
            entity_terms(messages, jnp.int32(0)), "ent", scatter_dimension=0, tiled=True
        )
        return lax.psum(partial_sum, "sec")

    zero_sections = jnp.zeros((sec_dev, feature_width), jnp.float32)
    projected = jnp.dot(features, theta, preferred_element_type=jnp.float32)
    scaled = (entity_scale * projected).astype(jnp.bfloat16)
    gathered = entity_fold(
        zero_sections, lax.all_gather(scaled, "ent", axis=0, tiled=True), jnp.int32(0)
    )
    messages = (section_scale * gathered).astype(jnp.bfloat16)
    collected = collect(messages)
    preact = entity_scale * collected
    activated = jax.nn.silu(preact).astype(jnp.bfloat16)
    sigmoid_pre = jax.nn.sigmoid(preact)
    grad_pre = cotangent.astype(jnp.float32) * sigmoid_pre * (1.0 + preact * (1.0 - sigmoid_pre))
    back_scaled = (entity_scale * grad_pre).astype(jnp.bfloat16)
    back_gathered = entity_fold(
        zero_sections, lax.all_gather(back_scaled, "ent", axis=0, tiled=True), jnp.int32(0)
    )
    grad_weight = jnp.sum(gathered * back_gathered, axis=1) / (1.0 + sec_count)
    back_messages = (section_scale * back_gathered).astype(jnp.bfloat16)
    back_collected = collect(back_messages)
    grad_proj = (entity_scale * back_collected).astype(jnp.bfloat16)
    grad_features = lax.dot_general(
        grad_proj, theta, (((1,), (1,)), ((), ())), preferred_element_type=jnp.float32
    ).astype(jnp.bfloat16)
    local_theta = lax.dot_general(
        features, grad_proj, (((0,), (0,)), ((), ())), preferred_element_type=jnp.float32
    )
    grad_theta = lax.psum(local_theta, "ent")
    return (activated, grad_features, grad_theta, grad_weight)


def solution(mesh):
    placed = (
        P("ent", None),
        P(),
        P(("ent", "sec")),
        P(("ent", "sec"), None, None),
        P(("ent", "sec"), None, None),
        P(("ent", "sec"), None),
        P("ent", None),
    )
    return jax.shard_map(
        body,
        mesh=mesh,
        in_specs=placed,
        out_specs=(P("ent", None), P("ent", None), P(), P(("ent", "sec"))),
        check_vma=False,
    )
```

profile of v0, /device:TPU:0, one launch (start us, length us, event | category | flops | bytes accessed | tf_op | source)
XLA Modules:
  0.0 517.0 jit_solution(3613104768004372445)
XLA Ops:
  8.8 28.8 %scatter_custom_fusion = f32[1024]{0:T(1024)S(1)} fusion(s32[4096]{0:T(1024)S(1)} %bitcast.89, f32[4096]{0:T(1024)S(1)} %bitcast.90, f32[]{:T(128)} %constant.131.clone.1), kind=kCustom, calls=%fused_computation.76 | custom fusion | flops 4096 | bytes 4100 | tf_op jit(solution)/shard_map/scatter-add | solution.py:24
  37.6 42.0 %psum.28 = f32[1024]{0:T(1024)S(1)} all-reduce(f32[1024]{0:T(1024)S(1)} %scatter_custom_fusion), channel_id=1, replica_groups=mesh['ent'=8,'sec'=4] {'ent','sec'}, use_global_device_ids=true, to_apply=%region_1.0 | all-reduce | flops 1024 | bytes 8192 | tf_op jit(solution)/shard_map/psum | solution.py:27
  79.9 31.5 %all_gather.6 = bf16[1024,256]{1,0:T(8,128)(2,1)S(1)} all-gather(bf16[128,256]{1,0:T(8,128)(2,1)S(1)} %fusion.58), channel_id=1, replica_groups=mesh['ent'=8,'sec'=4] {'ent'}, dimensions={0}, use_global_device_ids=true | all-gather | bytes 589824 | tf_op jit(solution)/shard_map/all_gather | solution.py:86
  111.4 7.5 %while.50 = (s32[]{:T(128)}, f32[512,256]{1,0:T(8,128)S(1)}, s32[8,512]{1,0:T(8,128)S(1)}, pred[8,512]{1,0:T(8,128)(4,1)S(1)}, s32[8,512]{1,0:T(8,128)S(1)}, /*i...) while((s32[]{:T(128)}, f32[512,256]{1,0:T(8,128)S(1)}, ...), condition=%wide.region_4.5_spmd.clone, body=%wide.region_3.4_spmd.clone.sunk | while | flops 168820736 | bytes 1128617 | solution.py:55
  111.4 0.9 convolution_add_fusion.4
  112.4 0.9 convolution_add_fusion.4
  113.3 0.9 convolution_add_fusion.4
  114.2 0.9 convolution_add_fusion.4
  115.2 0.9 convolution_add_fusion.4
  116.1 0.9 convolution_add_fusion.4
  117.0 0.9 convolution_add_fusion.4
  118.0 0.9 convolution_add_fusion.4
  118.9 28.8 %scatter_custom_fusion.1 = f32[512]{0:T(512)S(1)} fusion(s32[4096]{0:T(1024)S(1)} %bitcast.92, f32[4096]{0:T(1024)S(1)} %bitcast.91, f32[]{:T(128)} %constant.137.clone.1), kind=kCustom, calls=%fused_computation.78 | custom fusion | flops 4096 | bytes 2052 | tf_op jit(solution)/shard_map/scatter-add | solution.py:30
  147.9 25.2 %while.48 = (s32[]{:T(128)}, f32[8,128,256]{2,1,0:T(8,128)S(1)}, s32[8]{0:T(128)S(1)}, s32[8,512]{1,0:T(8,128)S(1)}, pred[8,512]{1,0:T(8,128)(4,1)S(1)}, /*index...) while((s32[]{:T(128)}, f32[8,128,256]{2,1,0:T(8,128)S(1)}, ...), condition=%wide.region_6.7_spmd, body=%wide.region_5.6_spmd.sunk | while | flops 168558592 | bytes 407711 | solution.py:73
  173.2 1.0 copy-done.2
  174.2 63.6 %reduce-scatter.3.cloned.1.call-done = f32[128,256]{1,0:T(8,128)} async-done(((f32[1024,256]{1,0:T(8,128)}), f32[128,256]{1,0:T(8,128)}) %reduce-scatter.3.cloned.1.call-update) | async-done | bytes 131088 | tf_op jit(solution)/shard_map/reduce_scatter | solution.py:77
  237.9 32.8 %all-reduce.4.cloned.1.call-done = f32[128,256]{1,0:T(8,128)} async-done(((f32[128,256]{1,0:T(8,128)}), f32[128,256]{1,0:T(8,128)}) %all-reduce.4.cloned.1.call-update) | async-done | bytes 131088 | tf_op jit(solution)/shard_map/psum | solution.py:80
  270.7 1.7 multiply_convert_fusion.3
  272.4 31.4 %all_gather.7 = bf16[1024,256]{1,0:T(8,128)(2,1)S(1)} all-gather(bf16[128,256]{1,0:T(8,128)(2,1)S(1)} %get-tuple-element.408), channel_id=1, replica_groups=mesh['ent'=8,'sec'=4] {'ent'}, dimensions={0}, use_global_device_ids=true | all-gather | bytes 589824 | tf_op jit(solution)/shard_map/all_gather | solution.py:96
  303.7 7.4 %while.51 = (s32[]{:T(128)}, f32[512,256]{1,0:T(8,128)S(1)}, s32[8,512]{1,0:T(8,128)S(1)}, pred[8,512]{1,0:T(8,128)(4,1)S(1)}, s32[8,512]{1,0:T(8,128)S(1)}, /*i...) while((s32[]{:T(128)}, f32[512,256]{1,0:T(8,128)S(1)}, ...), condition=%wide.region_10.11_spmd.clone, body=%wide.region_9.10_spmd.clone.sunk | while | flops 168820736 | bytes 1128617 | solution.py:55
  304.7 0.9 convolution_add_fusion.5
  305.6 0.9 convolution_add_fusion.5
  307.5 0.9 convolution_add_fusion.5
  309.3 0.9 convolution_add_fusion.5
  310.3 0.9 convolution_add_fusion.5
  311.5 25.2 %while.49 = (s32[]{:T(128)}, f32[8,128,256]{2,1,0:T(8,128)S(1)}, s32[8]{0:T(128)S(1)}, s32[8,512]{1,0:T(8,128)S(1)}, pred[8,512]{1,0:T(8,128)(4,1)S(1)}, /*index...) while((s32[]{:T(128)}, f32[8,128,256]{2,1,0:T(8,128)S(1)}, ...), condition=%wide.region_12.13_spmd, body=%wide.region_11.12_spmd.sunk | while | flops 168558592 | bytes 407711 | solution.py:73
  336.7 1.0 copy-done.1
  337.8 63.8 %reduce-scatter.5.cloned.1.call-done = f32[128,256]{1,0:T(8,128)} async-done(((f32[1024,256]{1,0:T(8,128)}), f32[128,256]{1,0:T(8,128)}) %reduce-scatter.5.cloned.1.call-update) | async-done | bytes 131088 | tf_op jit(solution)/shard_map/reduce_scatter | solution.py:77
  401.7 32.7 %all-reduce.6.cloned.1.call-done = f32[128,256]{1,0:T(8,128)} async-done(((f32[128,256]{1,0:T(8,128)}), f32[128,256]{1,0:T(8,128)}) %all-reduce.6.cloned.1.call-update) | async-done | bytes 131088 | tf_op jit(solution)/shard_map/psum | solution.py:80
  434.3 1.9 convolution_bitcast_fusion
  438.0 70.7 %all-reduce.8.cloned.1.call-done = f32[256,256]{0,1:T(8,128)} async-done(((f32[256,256]{0,1:T(8,128)}), f32[256,256]{0,1:T(8,128)}) %all-reduce.8.cloned.1.call-update) | async-done | bytes 262160 | tf_op jit(solution)/shard_map/psum | solution.py:108
  508.7 1.8 copy.11
  (148 shorter events, 26.4 us)
Async XLA Ops:
  7.2 72.5 %copy-start = (bf16[256,256]{1,0:T(8,128)(2,1)S(1)}, bf16[256,256]{1,0:T(8,128)(2,1)}, u32[]{:S(2)}) copy-start(bf16[256,256]{1,0:T(8,128)(2,1)} %param.16) | copy-start | bytes 393220
  7.2 230.6 %reduce-scatter.3.cloned.1.call-start = ((), (), s32[]{:S(2)}) async-start(), calls=%async_computation.2 | async-start | bytes 1179648 | tf_op jit(solution)/shard_map/reduce_scatter | solution.py:77
  7.3 0.7 copy-start.9
  8.0 0.7 copy-start.5
  8.1 71.6 %copy-start.4 = (bf16[128,256]{1,0:T(8,128)(2,1)S(1)}, bf16[128,256]{1,0:T(8,128)(2,1)}, u32[]{:S(2)}) copy-start(bf16[128,256]{1,0:T(8,128)(2,1)} %param.15) | copy-start | bytes 196612
  79.8 31.5 %copy-start.6 = (s32[1,8,512]{2,1,0:T(8,128)S(1)}, s32[1,8,512]{2,1,0:T(8,128)}, u32[]{:S(2)}) copy-start(s32[1,8,512]{2,1,0:T(8,128)} %param.18) | copy-start | bytes 49156
  118.9 28.8 %copy-start.8 = (f32[512]{0:T(512)S(1)}, f32[512]{0:T(512)}, u32[]{:S(2)}) copy-start(f32[512]{0:T(512)} %param.17) | copy-start | bytes 6148
  173.2 1.0 copy-start.2
  174.2 96.5 %all-reduce.4.cloned.1.call-start = ((), (), s32[]{:S(2)}) async-start(), calls=%async_computation.3 | async-start | bytes 262144 | tf_op jit(solution)/shard_map/psum | solution.py:80
  237.8 32.9 %copy-start.7 = (bf16[128,256]{1,0:T(8,128)(2,1)S(1)}, bf16[128,256]{1,0:T(8,128)(2,1)}, u32[]{:S(2)}) copy-start(bf16[128,256]{1,0:T(8,128)(2,1)} %param.21) | copy-start | bytes 196612
  237.9 163.8 %reduce-scatter.5.cloned.1.call-start = ((), (), s32[]{:S(2)}) async-start(), calls=%async_computation.4 | async-start | bytes 1179648 | tf_op jit(solution)/shard_map/reduce_scatter | solution.py:77
  336.7 1.0 copy-start.1
  337.7 96.6 %all-reduce.6.cloned.1.call-start = ((), (), s32[]{:S(2)}) async-start(), calls=%async_computation.5 | async-start | bytes 262144 | tf_op jit(solution)/shard_map/psum | solution.py:80
  401.6 107.1 %all-reduce.8.cloned.1.call-start = ((), (), s32[]{:S(2)}) async-start(), calls=%async_computation.6 | async-start | bytes 524288 | tf_op jit(solution)/shard_map/psum | solution.py:108
  436.2 0.9 copy-start.3
Sparse Core Ops, SparseCore 0:
  174.3 63.4 reduce-scatter.2
  240.2 30.3 all-reduce.3
  337.9 63.6 reduce-scatter.4
  403.9 30.4 all-reduce.5
  438.1 70.5 all-reduce.7
where the time goes:
time: 518 us; the launch traced here: 517 us
  waiting for transfers between devices  264 us (51%)
  blocking collectives  105 us (20%)
  other arithmetic  60.4 us (12%)
  loops' own time  32.1 us (6%)
  matrix products  25.6 us (5%)
  local copies, waits for them, and re-layouts  16.2 us (3%)
  between operations  14 us (3%)
    reduce_scatter x2, waiting for transfers between devices, collect(): lax.psum_scatter(entity_terms(messages, jnp.int32(0)), 'ent', scatter_dim...  127 us
    psum x1, waiting for transfers between devices, body(): grad_theta = lax.psum(local_theta, 'ent')  70.7 us
    psum x2, waiting for transfers between devices, collect(): return lax.psum(partial_sum, 'sec')  65.4 us
    psum x1, blocking collectives, body(): entity_degree = lax.psum(local_degree, ('ent', 'sec'))  42 us
    another operation x2, loops' own time, entity_terms(): pieces = lax.map(block_term, jnp.arange(block_span, dtype=jnp.int32))  31.5 us
    all_gather x1, blocking collectives, body(): lax.all_gather(scaled, 'ent', axis=0, tiled=True)  31.5 us
    all_gather x1, blocking collectives, body(): lax.all_gather(back_scaled, 'ent', axis=0, tiled=True)  31.4 us
    scatter-add x1, other arithmetic, body(): jax.ops.segment_sum(usable_float.reshape(-1), entity_index.reshape(-1), n...  28.8 us
  transfers between devices with their start and end apart: 5, of which 5 were waited for; matrix products, arithmetic and copies ran while one was open for 0% of the time, Pallas kernels for 0%

commit v1 on v0

--- a/solution.py
+++ b/solution.py
@@ -1,7 +1,9 @@
 import jax
 import jax.numpy as jnp
 from jax import lax
-from jax.sharding import PartitionSpec as P
+from jax.experimental import pallas as pl
+from jax.experimental.pallas import tpu as pltpu
+from jax.sharding import Mesh, PartitionSpec as P
 
 
 def hot_table(indices, live_slots, offset, table_width):
@@ -109,20 +111,274 @@
     return (activated, grad_features, grad_theta, grad_weight)
 
 
+BF = jnp.bfloat16
+F32 = jnp.float32
+TILE = 256
+NT = (((1,), (1,)), ((), ()))
+TN = (((0,), (0,)), ((), ()))
+
+
+def params():
+    return pltpu.CompilerParams(vmem_limit_bytes=48 * 2**20)
+
+
+def vmem():
+    return pl.BlockSpec(memory_space=pltpu.VMEM)
+
+
+def dot(a, b, dims=(((1,), (0,)), ((), ()))):
+    return lax.dot_general(a, b, dims, preferred_element_type=F32)
+
+
+def one_hot(index_row):
+    ids = lax.broadcasted_iota(jnp.int32, (TILE, index_row.shape[1]), 0).astype(BF)
+    return jnp.where(ids == index_row, jnp.ones((), BF), jnp.zeros((), BF))
+
+
+def column_to_row(column):
+    wide = jnp.broadcast_to(column, (column.shape[0], 128))
+    return wide.T[0:1, :]
+
+
+def row_to_column(row):
+    return jnp.broadcast_to(row, (128, 128)).T
+
+
+def prep_kernel(counts, rows, cols, weight, payload, incidence, inverse):
+    copies, _, slots = payload.shape
+    blocks = rows.shape[1]
+    ent_dev = incidence.shape[1] // blocks
+    row_ids = rows[0]
+    col_ids = cols[0]
+    sub = lax.broadcasted_iota(jnp.int32, (blocks, slots), 0)
+    lane = lax.broadcasted_iota(jnp.int32, (blocks, slots), 1)
+    limit = jnp.zeros((blocks, slots), jnp.int32)
+    for j in range(blocks):
+        limit = jnp.where(sub == j, counts[0, j], limit)
+    live = lane < limit
+    high = jnp.where(live, (row_ids // TILE) * ent_dev + col_ids, -1).astype(F32)
+    low = jnp.where(live, row_ids % TILE, -1).astype(F32)
+    totals = [jnp.zeros((TILE, ent_dev), F32) for _ in range(2)]
+    for j in range(blocks):
+        high_hot = one_hot(high[j : j + 1].astype(BF))
+        low_hot = one_hot(low[j : j + 1].astype(BF))
+        block = dot(low_hot, high_hot, NT)
+        for half in range(2):
+            part = block[:, half * ent_dev : (half + 1) * ent_dev]
+            totals[half] = totals[half] + part
+            incidence[half * TILE : (half + 1) * TILE, j * ent_dev : (j + 1) * ent_dev] = part.astype(BF)
+    degree = jnp.concatenate(
+        [column_to_row(jnp.sum(t, axis=1, keepdims=True)) for t in totals], axis=1
+    )
+    inv = 1.0 / (1.0 + degree)
+    inverse[...] = inv
+    scale = weight[...] / (1.0 + degree)
+    message = jnp.concatenate(
+        [high, low, jnp.broadcast_to(scale, (blocks, slots))], axis=0
+    ).astype(BF)
+    for n in range(copies):
+        payload[n] = message
+
+
+def gram_kernel(lists, gram, table, scaled, *sums):
+    shards, _, slots = lists.shape
+    ents = table.shape[0]
+    blocks = (lists.shape[1]) // 3
+    ent_dev = ents // blocks
+    tiles = ents // TILE
+    for acc in sums:
+        acc[...] = jnp.zeros_like(acc)
+    scaled[ents:, :] = jnp.ones((scaled.shape[0] - ents, scaled.shape[1]), BF)
+
+    def shard(k, carry):
+        indices = lists[k]
+        for j in range(blocks):
+            high_hot = one_hot(indices[j : j + 1])
+            low_hot = one_hot(indices[blocks + j : blocks + j + 1])
+            block = dot(high_hot, low_hot, NT).astype(BF)
+            for half in range(2):
+                table[j * ent_dev : (j + 1) * ent_dev, half * TILE : (half + 1) * TILE] = block[
+                    half * ent_dev : (half + 1) * ent_dev, :
+                ]
+        scale = indices[2 * blocks : 2 * blocks + 1]
+        scaled[0:ents, :] = table[...] * scale
+        for b in range(tiles):
+            sums[b][...] += dot(
+                scaled[b * TILE :, :], table[b * TILE : (b + 1) * TILE, :], NT
+            )
+        return carry
+
+    lax.fori_loop(0, shards, shard, 0)
+    start = 0
+    degrees = []
+    for b in range(tiles):
+        size = ents - b * TILE
+        gram[start : start + size, :] = sums[b][0:size, :].astype(BF)
+        start += size
+        degree = sums[b][size : size + 1, :]
+        top = degree.astype(BF)
+        degrees.append(top.astype(F32))
+        degrees.append(degree - top.astype(F32))
+    degrees.append(jnp.zeros((16 - 2 * tiles, TILE), F32))
+    gram[start : start + 16, :] = jnp.concatenate(degrees, axis=0).astype(BF)
+
+
+def tail_kernel(
+    own, other, gathered, theta, incidence, inverse,
+    activated, grad_features, grad_theta, grad_weight,
+    full, scale, values, backs, acts, projs,
+):
+    ents = full.shape[0]
+    tiles = ents // TILE
+    ent_dev = activated.shape[0]
+    groups = ents // ent_dev
+    width = theta.shape[0]
+    core = lax.axis_index("core")
+    mine = lax.axis_index("ent")
+    base = sum(ents - b * TILE for b in range(tiles))
+    degree_rows = own[base : base + 16, :].astype(F32) + other[base : base + 16, :].astype(F32)
+    for b in range(tiles):
+        row = lax.rsqrt(1.0 + (degree_rows[2 * b : 2 * b + 1] + degree_rows[2 * b + 1 : 2 * b + 2]))
+        for h in range(TILE // 128):
+            at = b * TILE + h * 128
+            scale[at : at + 128, :] = row_to_column(row[:, h * 128 : (h + 1) * 128])
+    for which, source in enumerate((own, other)):
+        column = (core if which == 0 else 1 - core) * ents
+        start = 0
+        for b in range(tiles):
+            for a in range(b, tiles):
+                piece = source[start : start + TILE, :]
+                full[a * TILE : (a + 1) * TILE, pl.ds(pl.multiple_of(column + b * TILE, TILE), TILE)] = piece
+                if a != b:
+                    full[b * TILE : (b + 1) * TILE, pl.ds(pl.multiple_of(column + a * TILE, TILE), TILE)] = piece.T
+                start += TILE
+
+    def es(at, size):
+        part = scale[at : at + size, :]
+        return jnp.concatenate([part] * (width // 128), axis=1)
+
+    for g in range(groups):
+        at = g * ent_dev
+        proj = dot(gathered[g, 0:ent_dev, :], theta[...])
+        part = (es(at, ent_dev) * proj).astype(BF)
+        values[at : at + ent_dev, :] = part
+        values[ents + at : ents + at + ent_dev, :] = part
+    for g in range(groups):
+        at = g * ent_dev
+        preact = es(at, ent_dev) * dot(full[at : at + ent_dev, :], values[...])
+        gate = jax.nn.sigmoid(preact)
+        acts[at : at + ent_dev, :] = (preact * gate).astype(BF)
+        cot = gathered[g, ent_dev:, :].astype(F32)
+        grad = cot * gate * (1.0 + preact * (1.0 - gate))
+        part = (es(at, ent_dev) * grad).astype(BF)
+        backs[at : at + ent_dev, :] = part
+        backs[ents + at : ents + at + ent_dev, :] = part
+    own_rows = pl.ds(pl.multiple_of(mine * ent_dev, ent_dev), ent_dev)
+    activated[...] = acts[own_rows, :]
+    total = jnp.zeros((width, width), F32)
+    for g in range(groups):
+        at = g * ent_dev
+        part = (es(at, ent_dev) * dot(full[at : at + ent_dev, :], backs[...])).astype(BF)
+        projs[at : at + ent_dev, :] = part
+        total = total + dot(gathered[g, 0:ent_dev, :], part, TN)
+    grad_theta[...] = total
+    grad_features[...] = dot(projs[own_rows, :], theta[...], NT).astype(BF)
+    sections = incidence.shape[0]
+    for q in range(sections // 128):
+        piece = incidence[q * 128 : (q + 1) * 128, :]
+        ahead = dot(piece, values[0:ents, :])
+        back = dot(piece, backs[0:ents, :])
+        sums = column_to_row(jnp.sum(ahead * back, axis=1, keepdims=True))
+        lanes = slice(q * 128, (q + 1) * 128)
+        grad_weight[:, lanes] = sums * inverse[:, lanes]
+
+
+def dense_body(features, theta, section_weight, pair_rows, pair_cols, pair_counts, cotangent):
+    ent_dev, width = features.shape
+    sec_dev = section_weight.shape[0]
+    _, blocks, slots = pair_rows.shape
+    ents = blocks * ent_dev
+    tiles = ents // TILE
+    chips = lax.axis_size("ent") * lax.axis_size("x")
+    gathered = lax.all_gather(
+        jnp.concatenate([features, cotangent], axis=0), "ent", axis=0, tiled=False
+    )
+    with jax.named_scope("lists"):
+        payload, incidence, inverse = pl.pallas_call(
+            prep_kernel,
+            out_shape=(
+                jax.ShapeDtypeStruct((chips, 3 * blocks, slots), BF),
+                jax.ShapeDtypeStruct((sec_dev, ents), BF),
+                jax.ShapeDtypeStruct((1, sec_dev), F32),
+            ),
+            in_specs=[pl.BlockSpec(memory_space=pltpu.SMEM), vmem(), vmem(), vmem()],
+            out_specs=(vmem(), vmem(), vmem()),
+            compiler_params=params(),
+        )(pair_counts, pair_rows, pair_cols, section_weight.reshape(1, sec_dev))
+        lists = lax.all_to_all(payload, ("ent", "x"), 0, 0, tiled=True)
+    with jax.named_scope("gram"):
+        heights = [ents - b * TILE for b in range(tiles)]
+        gram_rows = sum(heights) + 16
+        own = pl.pallas_call(
+            gram_kernel,
+            out_shape=jax.ShapeDtypeStruct((gram_rows, TILE), BF),
+            in_specs=[vmem()],
+            out_specs=vmem(),
+            scratch_shapes=[
+                pltpu.VMEM((ents, sec_dev), BF),
+                pltpu.VMEM((ents + 16, sec_dev), BF),
+            ]
+            + [pltpu.VMEM((h + 16, TILE), F32) for h in heights],
+            compiler_params=params(),
+        )(lists)
+        other = lax.ppermute(own, "core", [(0, 1), (1, 0)])
+    with jax.named_scope("tail"):
+        activated, grad_features, grad_theta, grad_weight = pl.pallas_call(
+            tail_kernel,
+            out_shape=(
+                jax.ShapeDtypeStruct((ent_dev, width), BF),
+                jax.ShapeDtypeStruct((ent_dev, width), BF),
+                jax.ShapeDtypeStruct((width, width), F32),
+                jax.ShapeDtypeStruct((1, sec_dev), F32),
+            ),
+            in_specs=[vmem()] * 6,
+            out_specs=(vmem(),) * 4,
+            scratch_shapes=[
+                pltpu.VMEM((ents, 2 * ents), BF),
+                pltpu.VMEM((ents, 128), F32),
+                pltpu.VMEM((2 * ents, width), BF),
+                pltpu.VMEM((2 * ents, width), BF),
+                pltpu.VMEM((ents, width), BF),
+                pltpu.VMEM((ents, width), BF),
+            ],
+            compiler_params=params(),
+        )(own, other, gathered, theta, incidence, inverse)
+    return activated, grad_features, grad_theta, grad_weight.reshape(sec_dev)
+
+
 def solution(mesh):
+    ent, sec = mesh.shape["ent"], mesh.shape["sec"]
+    cores = 2
+    dense = ent <= 8 and sec % cores == 0
+    if dense:
+        grid = Mesh(mesh.devices.reshape(ent, sec // cores, cores), ("ent", "x", "core"))
+        split = ("ent", "x", "core")
+    else:
+        grid = mesh
+        split = ("ent", "sec")
     placed = (
         P("ent", None),
         P(),
-        P(("ent", "sec")),
-        P(("ent", "sec"), None, None),
-        P(("ent", "sec"), None, None),
-        P(("ent", "sec"), None),
+        P(split),
+        P(split, None, None),
+        P(split, None, None),
+        P(split, None),
         P("ent", None),
     )
     return jax.shard_map(
-        body,
-        mesh=mesh,
+        dense_body if dense else body,
+        mesh=grid,
         in_specs=placed,
-        out_specs=(P("ent", None), P("ent", None), P(), P(("ent", "sec"))),
+        out_specs=(P("ent", None), P("ent", None), P(), P(split)),
         check_vma=False,
     )

time: 518 us -> 82.2 us (0.16)
  waiting for transfers between devices: 264 us -> 19.9 us
  blocking collectives: 105 us -> 0 us
  other arithmetic: 60.4 us -> 1.54 us
  loops' own time: 32.1 us -> 0 us
  Pallas kernels: 0 us -> 31.4 us
  matrix products: 25.6 us -> 0 us
  local copies, waits for them, and re-layouts: 16.2 us -> 6.21 us
  starting transfers between devices: 0.2 us -> 8.56 us
    psum x3 -> x0, waiting for transfers between devices: 136 us -> none  [the longest x1 70.7 us: body(): grad_theta = lax.psum(local_theta, 'ent')]
    reduce_scatter x2 -> x0, waiting for transfers between devices: 127 us -> none  [collect(): lax.psum_scatter(entity_terms(messages, jnp.int32(0)), 'ent', scatter_dim...]
    all_gather x2 -> x0, blocking collectives: 62.9 us -> none  [the longest x1 31.5 us: body(): lax.all_gather(scaled, 'ent', axis=0, tiled=True)]
    scatter-add x2 -> x0, other arithmetic: 57.6 us -> none  [the longest x1 28.8 us: body(): jax.ops.segment_sum(usable_float.reshape(-1), entity_index.reshape(-1), n...]
    psum x1 -> x0, blocking collectives: 42 us -> none  [body(): entity_degree = lax.psum(local_degree, ('ent', 'sec'))]
    another operation x4 -> x0, loops' own time: 32.1 us -> none  [the longest x2 31.5 us: entity_terms(): pieces = lax.map(block_term, jnp.arange(block_span, dtype=jnp.int32))]
    pallas_call x0 -> x3, Pallas kernels: none -> 31.4 us  [the longest x1 23.5 us: dense_body(): pl.pallas_call(gram_kernel, out_shape=jax.ShapeDtypeStruct((gram_rows, TI...]
    dot_general x35 -> x0, matrix products: 25.6 us -> none  [the longest x16 13.7 us: add_block(): jnp.einsum('ps,pf->sf', row_hot, picked, preferred_element_type=jnp.float32)]
  transfers between devices with their start and end apart: 5 -> 3, of which waited for: 5 -> 2; matrix products, arithmetic and copies ran while one was open for 0% -> 2% of each run, Pallas kernels for 0% -> 29%
where the time goes in v1:
time: 82.2 us; the launch traced here: 81.7 us
  Pallas kernels  31.4 us (38%)
  waiting for transfers between devices  19.9 us (24%)
  between operations  14.1 us (17%)
  starting transfers between devices  8.56 us (10%)
  local copies, waits for them, and re-layouts  6.21 us (8%)
  other arithmetic  1.54 us (2%)
    pallas_call x1, Pallas kernels, dense_body(): pl.pallas_call(gram_kernel, out_shape=jax.ShapeDtypeStruct((gram_rows, TI...  23.5 us
    all_to_all x1, waiting for transfers between devices, dense_body(): lists = lax.all_to_all(payload, ('ent', 'x'), 0, 0, tiled=True)  11 us
    all_gather x1, waiting for transfers between devices, dense_body(): lax.all_gather(jnp.concatenate([features, cotangent], axis=0), 'ent', axi...  8.86 us
    all_to_all x1, starting transfers between devices, dense_body(): lists = lax.all_to_all(payload, ('ent', 'x'), 0, 0, tiled=True)  8.44 us
    unnamed x16, local copies, waits for them, and re-layouts  6.21 us
    pallas_call x1, Pallas kernels, dense_body(): pl.pallas_call(tail_kernel, out_shape=(jax.ShapeDtypeStruct((ent_dev, wid...  5.7 us
    pallas_call x1, Pallas kernels, dense_body(): pl.pallas_call(prep_kernel, out_shape=(jax.ShapeDtypeStruct((chips, 3 * b...  2.23 us
  transfers between devices with their start and end apart: 3, of which 2 were waited for; matrix products, arithmetic and copies ran while one was open for 2% of the time, Pallas kernels for 29%

profile of v1, /device:TPU:0, one launch (start us, length us, event | category | flops | bytes accessed | tf_op | source)
XLA Modules:
  0.0 81.7 jit_solution(11724323740691914951)
XLA Ops:
  7.2 0.0 copy-start.4
  7.2 0.7 copy-done.4
  7.9 0.0 copy-start.5
  7.9 0.7 copy-done.5
  8.6 0.0 copy-start.6
  8.6 0.7 copy-done.6
  9.3 0.0 copy-start.7
  9.3 0.7 copy-done.7
  9.9 2.2 %lists.1 = (bf16[16,24,512]{2,1,0:T(8,128)(2,1)}, bf16[512,1024]{1,0:T(8,128)(2,1)S(1)}, f32[1,512]{1,0:T(1,128)S(1)}) custom-call(s32[1,8]{1,0:T(1,128)S(1)} %copy-done.7, s32[1,8,512]{2,1,0:T(8,128)S(1)} %copy-done.4, s32[1,8,512]{2,1,0:T(8,128)S(1)} %copy-done.5, f32[1,512]{1,0:T(1,128)S(1)} %bitcast.4), custom_call_target="tpu_custom_call" | custom-call | tf_op jit(solution)/shard_map/lists/pallas_call | solution.py:307
  12.2 0.0 copy-start
  12.2 1.0 %copy-done = bf16[512,1024]{1,0:T(8,128)(2,1)} copy-done((bf16[512,1024]{1,0:T(8,128)(2,1)}, bf16[512,1024]{1,0:T(8,128)(2,1)S(1)}, u32[]{:S(2)}) %copy-start) | copy-done | bytes 1048600
  13.2 0.0 copy-start.3
  13.2 8.4 %all-to-all-start = ((bf16[16,24,512]{2,1,0:T(8,128)(2,1)}), bf16[16,24,512]{2,1,0:T(8,128)(2,1)S(1)}, u32[]{:S(2)}, u32[]{:S(2)}) async-start(bf16[16,24,512]{2,1,0:T(8,128)(2,1)} %get-tuple-element.11), calls=%async_computation | async-start | bytes 786432 | tf_op jit(solution)/shard_map/lists/all_to_all | solution.py:318
  21.6 0.0 all-gather.3.cloned.1.call-start
  21.7 1.5 %pad_maximum_fusion = bf16[256,256]{1,0:T(8,128)(2,1)} fusion(bf16[128,256]{1,0:T(8,128)(2,1)} %param.13, bf16[128,256]{1,0:T(8,128)(2,1)} %param.7), kind=kLoop, calls=%fused_computation | loop fusion | flops 262144 | bytes 262144 | tf_op jit(solution)/shard_map/concatenate | solution.py:304
  23.2 0.0 all-gather.3.cloned.1.call-update
  23.2 11.0 %all-to-all-done.lists = bf16[16,24,512]{2,1,0:T(8,128)(2,1)S(1)} async-done(((bf16[16,24,512]{2,1,0:T(8,128)(2,1)}), bf16[16,24,512]{2,1,0:T(8,128)(2,1)S(1)}, u32[]{:S(2)}, u32[]{:S(2)}) %all-to-all-start) | async-done | bytes 393248 | tf_op jit(solution)/shard_map/lists/all_to_all | solution.py:318
  34.3 23.5 %gram.1.own = bf16[2576,256]{1,0:T(8,128)(2,1)S(1)} custom-call(bf16[16,24,512]{2,1,0:T(8,128)(2,1)S(1)} %all-to-all-done.lists), custom_call_target="tpu_custom_call" | custom-call | tf_op jit(solution)/shard_map/gram/pallas_call | solution.py:322
  57.7 0.1 collective-permute-start
  57.8 8.9 %all-gather.3.cloned.1.call-done = bf16[2048,256]{1,0:T(8,128)(2,1)} async-done(((bf16[256,256]{1,0:T(8,128)(2,1)}), bf16[2048,256]{1,0:T(8,128)(2,1)}) %all-gather.3.cloned.1.call-update) | async-done | bytes 1048592 | tf_op jit(solution)/shard_map/all_gather | solution.py:303
  66.7 0.0 collective-permute-done.other
  66.7 0.0 copy-done.3
  66.7 0.0 copy-start.1
  66.7 1.2 %copy-done.1 = bf16[512,1024]{1,0:T(8,128)(2,1)S(1)} copy-done((bf16[512,1024]{1,0:T(8,128)(2,1)S(1)}, bf16[512,1024]{1,0:T(8,128)(2,1)}, u32[]{:S(2)}) %copy-start.1) | copy-done | bytes 1048600
  67.9 0.0 copy-start.2
  67.9 1.2 %copy-done.2 = bf16[2048,256]{1,0:T(8,128)(2,1)S(1)} copy-done((bf16[2048,256]{1,0:T(8,128)(2,1)S(1)}, bf16[2048,256]{1,0:T(8,128)(2,1)}, u32[]{:S(2)}) %copy-start.2) | copy-done | bytes 1048600
  69.1 5.7 %tail.1 = (bf16[128,256]{1,0:T(8,128)(2,1)}, bf16[128,256]{1,0:T(8,128)(2,1)}, f32[256,256]{1,0:T(8,128)}, f32[1,512]{1,0:T(1,128)}) custom-call(bf16[2576,256]{1,0:T(8,128)(2,1)S(1)} %gram.1.own, bf16[2576,256]{1,0:T(8,128)(2,1)S(1)} %collective-permute-done.other, bf16[8,256,256]{2,1,0:T(8,128)(2,1)S(1)} %bitcast.3, bf16[256,256]{1,0:T(8,128)(2,1)S(1)} %copy-done.3, ...), custom_call_target="tpu_custom_call" | custom-call | tf_op jit(solution)/shard_map/tail/pallas_call | solution.py:336
Async XLA Ops:
  7.2 0.7 copy-start.4
  7.9 0.7 copy-start.5
  8.6 0.7 copy-start.6
  9.3 0.7 copy-start.7
  12.2 1.0 %copy-start = (bf16[512,1024]{1,0:T(8,128)(2,1)}, bf16[512,1024]{1,0:T(8,128)(2,1)S(1)}, u32[]{:S(2)}) copy-start(bf16[512,1024]{1,0:T(8,128)(2,1)S(1)} %get-tuple-element.12.incidence) | copy-start | bytes 3145732
  13.2 53.5 %copy-start.3 = (bf16[256,256]{1,0:T(8,128)(2,1)S(1)}, bf16[256,256]{1,0:T(8,128)(2,1)}, u32[]{:S(2)}) copy-start(bf16[256,256]{1,0:T(8,128)(2,1)} %theta.1) | copy-start | bytes 393220
  13.2 21.1 %all-to-all-start = ((bf16[16,24,512]{2,1,0:T(8,128)(2,1)}), bf16[16,24,512]{2,1,0:T(8,128)(2,1)S(1)}, u32[]{:S(2)}, u32[]{:S(2)}) async-start(bf16[16,24,512]{2,1,0:T(8,128)(2,1)} %get-tuple-element.11), calls=%async_computation | async-start | bytes 786432 | tf_op jit(solution)/shard_map/lists/all_to_all | solution.py:318
  21.6 45.1 %all-gather.3.cloned.1.call-start = ((), (), s32[]{:S(2)}) async-start(), calls=%async_computation.1 | async-start | bytes 1179648 | tf_op jit(solution)/shard_map/all_gather | solution.py:303
  57.7 8.9 %collective-permute-start = (bf16[2576,256]{1,0:T(8,128)(2,1)S(1)}, bf16[2576,256]{1,0:T(8,128)(2,1)S(1)}, u32[]{:S(2)}, u32[]{:S(2)}) collective-permute-start(bf16[2576,256]{1,0:T(8,128)(2,1)S(1)} %gram.1.own), channel_id=1, source_target_pairs={{0,1},{1,0},{2,3},{3,2},{4,5},{5,4},{6,7},{7,6},{8,9},{9,8},{10,11... | collective-permute-start | bytes 3956744 | tf_op jit(solution)/shard_map/gram/ppermute | solution.py:334
  66.7 1.2 %copy-start.1 = (bf16[512,1024]{1,0:T(8,128)(2,1)S(1)}, bf16[512,1024]{1,0:T(8,128)(2,1)}, u32[]{:S(2)}) copy-start(bf16[512,1024]{1,0:T(8,128)(2,1)} %copy-done) | copy-start | bytes 3145732
  67.9 1.2 %copy-start.2 = (bf16[2048,256]{1,0:T(8,128)(2,1)S(1)}, bf16[2048,256]{1,0:T(8,128)(2,1)}, u32[]{:S(2)}) copy-start(bf16[2048,256]{1,0:T(8,128)(2,1)} %all-gather.3.cloned.1.call-done) | copy-start | bytes 3145732
Sparse Core Ops, SparseCore 0:
  25.2 41.4 all-gather.2

commit v2 on v1

--- a/solution.py
+++ b/solution.py
@@ -113,26 +113,34 @@
 
 BF = jnp.bfloat16
 F32 = jnp.float32
+BIT = jnp.float8_e4m3fn
 TILE = 256
+SHIFT = TILE.bit_length() - 1
 NT = (((1,), (1,)), ((), ()))
 TN = (((0,), (0,)), ((), ()))
-
-
-def params():
-    return pltpu.CompilerParams(vmem_limit_bytes=48 * 2**20)
+CORES = 2
+STEP = 4
+
+
+def params(mebibytes=32):
+    return pltpu.CompilerParams(vmem_limit_bytes=mebibytes * 2**20)
 
 
 def vmem():
     return pl.BlockSpec(memory_space=pltpu.VMEM)
 
 
+def hbm():
+    return pl.BlockSpec(memory_space=pltpu.HBM)
+
+
 def dot(a, b, dims=(((1,), (0,)), ((), ()))):
     return lax.dot_general(a, b, dims, preferred_element_type=F32)
 
 
-def one_hot(index_row):
-    ids = lax.broadcasted_iota(jnp.int32, (TILE, index_row.shape[1]), 0).astype(BF)
-    return jnp.where(ids == index_row, jnp.ones((), BF), jnp.zeros((), BF))
+def one_hot(index_row, count=TILE):
+    ids = lax.broadcasted_iota(jnp.int32, (count, index_row.shape[1]), 0).astype(BF)
+    return jnp.where(ids == index_row, jnp.ones((), BIT), jnp.zeros((), BIT))
 
 
 def column_to_row(column):
@@ -144,71 +152,113 @@
     return jnp.broadcast_to(row, (128, 128)).T
 
 
-def prep_kernel(counts, rows, cols, weight, payload, incidence, inverse):
-    copies, _, slots = payload.shape
+def prep_kernel(
+    counts, rows, cols, weight, features, cotangent,
+    payload, shares, message, inverse,
+    counts_here, rows_here, cols_here, weight_here, share_here, in_sems, out_sems, share_sems,
+):
+    copies, height, slots = payload.shape
     blocks = rows.shape[1]
-    ent_dev = incidence.shape[1] // blocks
-    row_ids = rows[0]
-    col_ids = cols[0]
+    ent_dev = features.shape[0]
+    share = shares.shape[1] // 2
+    quarter = lax.axis_index("x") * CORES + lax.axis_index("core")
+    here = pl.ds(pl.multiple_of(quarter * share, share), share)
+    reads = [
+        pltpu.make_async_copy(source, target, in_sems.at[n])
+        for n, (source, target) in enumerate(
+            (
+                (counts, counts_here),
+                (rows.at[0], rows_here),
+                (cols.at[0], cols_here),
+                (weight, weight_here),
+                (features.at[here, :], share_here.at[0:share, :]),
+                (cotangent.at[here, :], share_here.at[share : 2 * share, :]),
+            )
+        )
+    ]
+    for read in reads:
+        read.start()
+    for read in reads:
+        read.wait()
+    sends = [
+        pltpu.make_async_copy(share_here, shares.at[n], share_sems.at[n]) for n in range(copies)
+    ]
+    for send in sends:
+        send.start()
+    row_ids = rows_here[...]
     sub = lax.broadcasted_iota(jnp.int32, (blocks, slots), 0)
     lane = lax.broadcasted_iota(jnp.int32, (blocks, slots), 1)
     limit = jnp.zeros((blocks, slots), jnp.int32)
     for j in range(blocks):
-        limit = jnp.where(sub == j, counts[0, j], limit)
+        limit = jnp.where(sub == j, counts_here[0, j], limit)
     live = lane < limit
-    high = jnp.where(live, (row_ids // TILE) * ent_dev + col_ids, -1).astype(F32)
-    low = jnp.where(live, row_ids % TILE, -1).astype(F32)
-    totals = [jnp.zeros((TILE, ent_dev), F32) for _ in range(2)]
+    part = lax.shift_right_logical(row_ids, SHIFT)
+    high = jnp.where(live, part * ent_dev + cols_here[...], -1).astype(F32)
+    low = jnp.where(live, row_ids & (TILE - 1), -1).astype(F32)
+    part = part.astype(F32)
+    degree = jnp.zeros((16, TILE), F32)
     for j in range(blocks):
-        high_hot = one_hot(high[j : j + 1].astype(BF))
-        low_hot = one_hot(low[j : j + 1].astype(BF))
-        block = dot(low_hot, high_hot, NT)
+        degree = degree + dot(
+            one_hot(part[j : j + 1].astype(BF), 16), one_hot(low[j : j + 1].astype(BF)), NT
+        )
+    degree = jnp.concatenate([degree[0:1], degree[1:2]], axis=1)
+    inverse[...] = 1.0 / (1.0 + degree)
+    scale = weight_here[...] / (1.0 + degree)
+    message[...] = jnp.concatenate(
+        [high, low, jnp.broadcast_to(scale, (height - 2 * blocks, slots))], axis=0
+    ).astype(BF)
+    writes = [
+        pltpu.make_async_copy(message, payload.at[n], out_sems.at[n]) for n in range(copies)
+    ]
+    for write in writes:
+        write.start()
+    for write in writes + sends:
+        write.wait()
+
+
+def own_kernel(message, incidence):
+    blocks = message.shape[0] // 3
+    ent_dev = incidence.shape[1] // blocks
+    for j in range(blocks):
+        block = dot(
+            one_hot(message[blocks + j : blocks + j + 1, :]), one_hot(message[j : j + 1, :]), NT
+        ).astype(BF)
         for half in range(2):
-            part = block[:, half * ent_dev : (half + 1) * ent_dev]
-            totals[half] = totals[half] + part
-            incidence[half * TILE : (half + 1) * TILE, j * ent_dev : (j + 1) * ent_dev] = part.astype(BF)
-    degree = jnp.concatenate(
-        [column_to_row(jnp.sum(t, axis=1, keepdims=True)) for t in totals], axis=1
-    )
-    inv = 1.0 / (1.0 + degree)
-    inverse[...] = inv
-    scale = weight[...] / (1.0 + degree)
-    message = jnp.concatenate(
-        [high, low, jnp.broadcast_to(scale, (blocks, slots))], axis=0
-    ).astype(BF)
-    for n in range(copies):
-        payload[n] = message
+            incidence[half * TILE : (half + 1) * TILE, j * ent_dev : (j + 1) * ent_dev] = block[
+                :, half * ent_dev : (half + 1) * ent_dev
+            ]
 
 
 def gram_kernel(lists, gram, table, scaled, *sums):
-    shards, _, slots = lists.shape
+    shards, height, slots = lists.shape
     ents = table.shape[0]
-    blocks = (lists.shape[1]) // 3
+    blocks = height // 3
     ent_dev = ents // blocks
     tiles = ents // TILE
+    sections = table.shape[1] // STEP
     for acc in sums:
         acc[...] = jnp.zeros_like(acc)
     scaled[ents:, :] = jnp.ones((scaled.shape[0] - ents, scaled.shape[1]), BF)
 
-    def shard(k, carry):
-        indices = lists[k]
-        for j in range(blocks):
-            high_hot = one_hot(indices[j : j + 1])
-            low_hot = one_hot(indices[blocks + j : blocks + j + 1])
-            block = dot(high_hot, low_hot, NT).astype(BF)
-            for half in range(2):
-                table[j * ent_dev : (j + 1) * ent_dev, half * TILE : (half + 1) * TILE] = block[
-                    half * ent_dev : (half + 1) * ent_dev, :
-                ]
-        scale = indices[2 * blocks : 2 * blocks + 1]
-        scaled[0:ents, :] = table[...] * scale
+    def step(i, carry):
+        for q in range(STEP):
+            indices = lists[i * STEP + q]
+            scale = indices[2 * blocks : 2 * blocks + 1]
+            for j in range(blocks):
+                block = dot(
+                    one_hot(indices[j : j + 1]), one_hot(indices[blocks + j : blocks + j + 1]), NT
+                ).astype(BF)
+                rows = slice(j * ent_dev, (j + 1) * ent_dev)
+                for half in range(2):
+                    at = q * sections + half * TILE
+                    part = block[half * ent_dev : (half + 1) * ent_dev, :]
+                    table[rows, at : at + TILE] = part
+                    scaled[rows, at : at + TILE] = part * scale[:, half * TILE : (half + 1) * TILE]
         for b in range(tiles):
-            sums[b][...] += dot(
-                scaled[b * TILE :, :], table[b * TILE : (b + 1) * TILE, :], NT
-            )
+            sums[b][...] += dot(scaled[b * TILE :, :], table[b * TILE : (b + 1) * TILE, :], NT)
         return carry
 
-    lax.fori_loop(0, shards, shard, 0)
+    lax.fori_loop(0, shards // STEP, step, 0)
     start = 0
     degrees = []
     for b in range(tiles):
@@ -216,25 +266,35 @@
         gram[start : start + size, :] = sums[b][0:size, :].astype(BF)
         start += size
         degree = sums[b][size : size + 1, :]
-        top = degree.astype(BF)
-        degrees.append(top.astype(F32))
-        degrees.append(degree - top.astype(F32))
+        top = degree.astype(BF).astype(F32)
+        degrees += [top, degree - top]
     degrees.append(jnp.zeros((16 - 2 * tiles, TILE), F32))
     gram[start : start + 16, :] = jnp.concatenate(degrees, axis=0).astype(BF)
 
 
 def tail_kernel(
-    own, other, gathered, theta, incidence, inverse,
+    own, other, own_share, other_share, theta, incidence, inverse,
     activated, grad_features, grad_theta, grad_weight,
-    full, scale, values, backs, acts, projs,
+    full, scale, values, backs, acts, projs, feats, cots, sems,
 ):
     ents = full.shape[0]
     tiles = ents // TILE
     ent_dev = activated.shape[0]
     groups = ents // ent_dev
     width = theta.shape[0]
+    share = feats.shape[2]
+    per_group = feats.shape[0] // groups
     core = lax.axis_index("core")
     mine = lax.axis_index("ent")
+    loads = []
+    for n, source in enumerate((own_share, other_share)):
+        at = core if n == 0 else 1 - core
+        loads.append(pltpu.make_async_copy(source.at[:, 0:share, :], feats.at[:, at], sems.at[2 * n]))
+        loads.append(
+            pltpu.make_async_copy(source.at[:, share : 2 * share, :], cots.at[:, at], sems.at[2 * n + 1])
+        )
+    for load in loads:
+        load.start()
     base = sum(ents - b * TILE for b in range(tiles))
     degree_rows = own[base : base + 16, :].astype(F32) + other[base : base + 16, :].astype(F32)
     for b in range(tiles):
@@ -242,8 +302,8 @@
         for h in range(TILE // 128):
             at = b * TILE + h * 128
             scale[at : at + 128, :] = row_to_column(row[:, h * 128 : (h + 1) * 128])
-    for which, source in enumerate((own, other)):
-        column = (core if which == 0 else 1 - core) * ents
+    for n, source in enumerate((own, other)):
+        column = (core if n == 0 else 1 - core) * ents
         start = 0
         for b in range(tiles):
             for a in range(b, tiles):
@@ -252,14 +312,19 @@
                 if a != b:
                     full[b * TILE : (b + 1) * TILE, pl.ds(pl.multiple_of(column + a * TILE, TILE), TILE)] = piece.T
                 start += TILE
+    for load in loads:
+        load.wait()
 
     def es(at, size):
         part = scale[at : at + size, :]
         return jnp.concatenate([part] * (width // 128), axis=1)
 
+    def rows_of(stack, g):
+        return stack[g * per_group : (g + 1) * per_group].reshape(ent_dev, width)
+
     for g in range(groups):
         at = g * ent_dev
-        proj = dot(gathered[g, 0:ent_dev, :], theta[...])
+        proj = dot(rows_of(feats, g), theta[...])
         part = (es(at, ent_dev) * proj).astype(BF)
         values[at : at + ent_dev, :] = part
         values[ents + at : ents + at + ent_dev, :] = part
@@ -268,8 +333,7 @@
         preact = es(at, ent_dev) * dot(full[at : at + ent_dev, :], values[...])
         gate = jax.nn.sigmoid(preact)
         acts[at : at + ent_dev, :] = (preact * gate).astype(BF)
-        cot = gathered[g, ent_dev:, :].astype(F32)
-        grad = cot * gate * (1.0 + preact * (1.0 - gate))
+        grad = rows_of(cots, g).astype(F32) * gate * (1.0 + preact * (1.0 - gate))
         part = (es(at, ent_dev) * grad).astype(BF)
         backs[at : at + ent_dev, :] = part
         backs[ents + at : ents + at + ent_dev, :] = part
@@ -280,7 +344,7 @@
         at = g * ent_dev
         part = (es(at, ent_dev) * dot(full[at : at + ent_dev, :], backs[...])).astype(BF)
         projs[at : at + ent_dev, :] = part
-        total = total + dot(gathered[g, 0:ent_dev, :], part, TN)
+        total = total + dot(rows_of(feats, g), part, TN)
     grad_theta[...] = total
     grad_features[...] = dot(projs[own_rows, :], theta[...], NT).astype(BF)
     sections = incidence.shape[0]
@@ -299,69 +363,98 @@
     _, blocks, slots = pair_rows.shape
     ents = blocks * ent_dev
     tiles = ents // TILE
-    chips = lax.axis_size("ent") * lax.axis_size("x")
-    gathered = lax.all_gather(
-        jnp.concatenate([features, cotangent], axis=0), "ent", axis=0, tiled=False
-    )
-    with jax.named_scope("lists"):
-        payload, incidence, inverse = pl.pallas_call(
-            prep_kernel,
-            out_shape=(
-                jax.ShapeDtypeStruct((chips, 3 * blocks, slots), BF),
-                jax.ShapeDtypeStruct((sec_dev, ents), BF),
-                jax.ShapeDtypeStruct((1, sec_dev), F32),
-            ),
-            in_specs=[pl.BlockSpec(memory_space=pltpu.SMEM), vmem(), vmem(), vmem()],
-            out_specs=(vmem(), vmem(), vmem()),
-            compiler_params=params(),
-        )(pair_counts, pair_rows, pair_cols, section_weight.reshape(1, sec_dev))
-        lists = lax.all_to_all(payload, ("ent", "x"), 0, 0, tiled=True)
-    with jax.named_scope("gram"):
-        heights = [ents - b * TILE for b in range(tiles)]
-        gram_rows = sum(heights) + 16
-        own = pl.pallas_call(
-            gram_kernel,
-            out_shape=jax.ShapeDtypeStruct((gram_rows, TILE), BF),
-            in_specs=[vmem()],
-            out_specs=vmem(),
-            scratch_shapes=[
-                pltpu.VMEM((ents, sec_dev), BF),
-                pltpu.VMEM((ents + 16, sec_dev), BF),
-            ]
-            + [pltpu.VMEM((h + 16, TILE), F32) for h in heights],
-            compiler_params=params(),
-        )(lists)
-        other = lax.ppermute(own, "core", [(0, 1), (1, 0)])
-    with jax.named_scope("tail"):
-        activated, grad_features, grad_theta, grad_weight = pl.pallas_call(
-            tail_kernel,
-            out_shape=(
-                jax.ShapeDtypeStruct((ent_dev, width), BF),
-                jax.ShapeDtypeStruct((ent_dev, width), BF),
-                jax.ShapeDtypeStruct((width, width), F32),
-                jax.ShapeDtypeStruct((1, sec_dev), F32),
-            ),
-            in_specs=[vmem()] * 6,
-            out_specs=(vmem(),) * 4,
-            scratch_shapes=[
-                pltpu.VMEM((ents, 2 * ents), BF),
-                pltpu.VMEM((ents, 128), F32),
-                pltpu.VMEM((2 * ents, width), BF),
-                pltpu.VMEM((2 * ents, width), BF),
-                pltpu.VMEM((ents, width), BF),
-                pltpu.VMEM((ents, width), BF),
-            ],
-            compiler_params=params(),
-        )(own, other, gathered, theta, incidence, inverse)
+    lanes = lax.axis_size("x")
+    chips = lax.axis_size("ent") * lanes
+    share = ent_dev // (lanes * CORES)
+    height = 3 * blocks
+    dma = pltpu.SemaphoreType.DMA
+    swap = [(0, 1), (1, 0)]
+    payload, shares, message, inverse = pl.pallas_call(
+        prep_kernel,
+        out_shape=(
+            jax.ShapeDtypeStruct((chips, height, slots), BF),
+            jax.ShapeDtypeStruct((chips, 2 * share, width), BF),
+            jax.ShapeDtypeStruct((height, slots), BF),
+            jax.ShapeDtypeStruct((1, sec_dev), F32),
+        ),
+        in_specs=[hbm()] * 6,
+        out_specs=(hbm(), hbm(), vmem(), vmem()),
+        scratch_shapes=[
+            pltpu.SMEM((1, blocks), jnp.int32),
+            pltpu.VMEM((blocks, slots), jnp.int32),
+            pltpu.VMEM((blocks, slots), jnp.int32),
+            pltpu.VMEM((1, sec_dev), F32),
+            pltpu.VMEM((2 * share, width), BF),
+            dma((6,)),
+            dma((chips,)),
+            dma((chips,)),
+        ],
+        compiler_params=params(63),
+        name="prep",
+    )(pair_counts, pair_rows, pair_cols, section_weight.reshape(1, sec_dev), features, cotangent)
+    lists = lax.all_to_all(payload, ("ent", "x"), 0, 0, tiled=True)
+    incidence = pl.pallas_call(
+        own_kernel,
+        out_shape=jax.ShapeDtypeStruct((sec_dev, ents), BF),
+        in_specs=[vmem()],
+        out_specs=vmem(),
+        compiler_params=params(),
+        cost_estimate=pl.CostEstimate(flops=2 * sec_dev * ents * slots, bytes_accessed=2**20, transcendentals=0),
+        name="own_incidence",
+    )(message)
+    lists, shares = lax.optimization_barrier((lists, shares))
+    own_share = lax.all_to_all(shares, ("ent", "x"), 0, 0, tiled=True)
+    heights = [ents - b * TILE for b in range(tiles)]
+    own = pl.pallas_call(
+        gram_kernel,
+        out_shape=jax.ShapeDtypeStruct((sum(heights) + 16, TILE), BF),
+        in_specs=[vmem()],
+        out_specs=vmem(),
+        scratch_shapes=[
+            pltpu.VMEM((ents, STEP * sec_dev), BF),
+            pltpu.VMEM((ents + 16, STEP * sec_dev), BF),
+        ]
+        + [pltpu.VMEM((h + 16, TILE), F32) for h in heights],
+        compiler_params=params(),
+        cost_estimate=pl.CostEstimate(
+            flops=2 * chips * sec_dev * (sum(heights) * TILE + ents * slots), bytes_accessed=2**21, transcendentals=0
+        ),
+        name="gram",
+    )(lists)
+    other = lax.ppermute(own, "core", swap)
+    other_share = lax.ppermute(own_share, "core", swap)
+    activated, grad_features, grad_theta, grad_weight = pl.pallas_call(
+        tail_kernel,
+        out_shape=(
+            jax.ShapeDtypeStruct((ent_dev, width), BF),
+            jax.ShapeDtypeStruct((ent_dev, width), BF),
+            jax.ShapeDtypeStruct((width, width), F32),
+            jax.ShapeDtypeStruct((1, sec_dev), F32),
+        ),
+        in_specs=[vmem(), vmem(), hbm(), hbm(), vmem(), vmem(), vmem()],
+        out_specs=(vmem(),) * 4,
+        scratch_shapes=[
+            pltpu.VMEM((ents, 2 * ents), BF),
+            pltpu.VMEM((ents, 128), F32),
+            pltpu.VMEM((2 * ents, width), BF),
+            pltpu.VMEM((2 * ents, width), BF),
+            pltpu.VMEM((ents, width), BF),
+            pltpu.VMEM((ents, width), BF),
+            pltpu.VMEM((chips, CORES, share, width), BF),
+            pltpu.VMEM((chips, CORES, share, width), BF),
+            dma((4,)),
+        ],
+        compiler_params=params(),
+        name="tail",
+    )(own, other, own_share, other_share, theta, incidence, inverse)
     return activated, grad_features, grad_theta, grad_weight.reshape(sec_dev)
 
 
 def solution(mesh):
     ent, sec = mesh.shape["ent"], mesh.shape["sec"]
-    cores = 2
-    dense = ent <= 8 and sec % cores == 0
+    dense = ent <= 8 and sec % CORES == 0
     if dense:
-        grid = Mesh(mesh.devices.reshape(ent, sec // cores, cores), ("ent", "x", "core"))
+        grid = Mesh(mesh.devices.reshape(ent, sec // CORES, CORES), ("ent", "x", "core"))
         split = ("ent", "x", "core")
     else:
         grid = mesh

time: 82.2 us -> 56 us (0.68)
  blocking collectives: 0 us -> 21 us
  waiting for transfers between devices: 19.9 us -> 2.83 us
  between operations: 14.1 us -> 0.71 us
  local copies, waits for them, and re-layouts: 6.21 us -> 0.02 us
  Pallas kernels: 31.4 us -> 26.9 us
  starting transfers between devices: 8.56 us -> 4.15 us
  other arithmetic: 1.54 us -> 0 us
    all_to_all x0 -> x1, blocking collectives: none -> 21 us  [dense_body(): lists = lax.all_to_all(payload, ('ent', 'x'), 0, 0, tiled=True)]
    all_to_all x1, waiting for transfers between devices: 11 us -> 0.01 us  [dense_body(): own_share = lax.all_to_all(shares, ('ent', 'x'), 0, 0, tiled=True)]
    all_gather x1 -> x0, waiting for transfers between devices: 8.86 us -> none  [dense_body(): lax.all_gather(jnp.concatenate([features, cotangent], axis=0), 'ent', axi...]
    unnamed x16 -> x6, local copies, waits for them, and re-layouts: 6.21 us -> 0.02 us
    all_to_all x1, starting transfers between devices: 8.44 us -> 3.59 us  [dense_body(): own_share = lax.all_to_all(shares, ('ent', 'x'), 0, 0, tiled=True)]
    pallas_call x2 -> x3, Pallas kernels: 25.7 us -> 21.1 us  [the longest x1 17.7 us: dense_body(): pl.pallas_call(gram_kernel, out_shape=jax.ShapeDtypeStruct((sum(heights)...]
    ppermute x1 -> x2, waiting for transfers between devices: 0.01 us -> 2.83 us  [the longest x1 2.08 us: dense_body(): other = lax.ppermute(own, 'core', swap)]
    concatenate x1 -> x0, other arithmetic: 1.54 us -> none  [dense_body(): jnp.concatenate([features, cotangent], axis=0)]
  transfers between devices with their start and end apart: 3 -> 3, of which waited for: 2 -> 2; matrix products, arithmetic and copies ran while one was open for 2% -> 0% of each run, Pallas kernels for 29% -> 33%
where the time goes in v2:
time: 56 us; the launch traced here: 55.6 us
  Pallas kernels  26.9 us (48%)
  blocking collectives  21 us (38%)
  starting transfers between devices  4.15 us (7%)
  waiting for transfers between devices  2.83 us (5%)
  between operations  0.71 us (1%)
    all_to_all x1, blocking collectives, dense_body(): lists = lax.all_to_all(payload, ('ent', 'x'), 0, 0, tiled=True)  21 us
    pallas_call x1, Pallas kernels, dense_body(): pl.pallas_call(gram_kernel, out_shape=jax.ShapeDtypeStruct((sum(heights)...  17.7 us
    pallas_call x1, Pallas kernels, dense_body(): pl.pallas_call(tail_kernel, out_shape=(jax.ShapeDtypeStruct((ent_dev, wid...  5.86 us
    all_to_all x1, starting transfers between devices, dense_body(): own_share = lax.all_to_all(shares, ('ent', 'x'), 0, 0, tiled=True)  3.59 us
    pallas_call x1, Pallas kernels, dense_body(): pl.pallas_call(prep_kernel, out_shape=(jax.ShapeDtypeStruct((chips, heigh...  2.92 us
    ppermute x1, waiting for transfers between devices, dense_body(): other = lax.ppermute(own, 'core', swap)  2.08 us
  transfers between devices with their start and end apart: 3, of which 2 were waited for; matrix products, arithmetic and copies ran while one was open for 0% of the time, Pallas kernels for 33%

profile of v2, /device:TPU:0, one launch (start us, length us, event | category | flops | bytes accessed | tf_op | source)
XLA Modules:
  0.0 55.6 jit_solution(298793511544444602)
XLA Ops:
  0.6 2.9 %prep.1 = (bf16[16,24,512]{2,1,0:T(8,128)(2,1)}, bf16[16,64,256]{2,1,0:T(8,128)(2,1)}, bf16[24,512]{1,0:T(8,128)(2,1)}, f32[1,512]{1,0:T(1,128)}) custom-call(s32[1,8]{1,0:T(1,128)} %counts.1, s32[1,8,512]{2,1,0:T(8,128)} %rows.1, s32[1,8,512]{2,1,0:T(8,128)} %cols.1, f32[1,512]{1,0:T(1,128)} %bitcast.2, bf16[128,256]{1,0:T(8,128)(2,1)} %features.1, ...), custom_call_target="tpu_custom_call" | custom-call | tf_op jit(solution)/shard_map/prep/pallas_call | solution.py:372
  3.6 21.0 %all_to_all.10.lists = bf16[16,24,512]{2,1,0:T(8,128)(2,1)S(1)} all-to-all(bf16[16,24,512]{2,1,0:T(8,128)(2,1)} %get-tuple-element.14), channel_id=1, replica_groups=mesh['ent'=8,'x'=2,'core'=2] {'ent','x'}, dimensions={0} | all-to-all | bytes 786432 | tf_op jit(solution)/shard_map/all_to_all | solution.py:395
  24.5 3.6 %all-to-all-start.1 = ((bf16[16,64,256]{2,1,0:T(8,128)(2,1)}), bf16[16,64,256]{2,1,0:T(8,128)(2,1)S(1)}, u32[]{:S(2)}, u32[]{:S(2)}) async-start(bf16[16,64,256]{2,1,0:T(8,128)(2,1)} %get-tuple-element.17), calls=%async_computation.1 | async-start | bytes 1048576 | tf_op jit(solution)/shard_map/all_to_all | solution.py:406
  28.1 0.0 copy-start.2
  28.1 17.7 %gram.1.own = bf16[2576,256]{1,0:T(8,128)(2,1)S(1)} custom-call(bf16[16,24,512]{2,1,0:T(8,128)(2,1)S(1)} %all_to_all.10.lists), custom_call_target="tpu_custom_call" | custom-call | flops 19327352832 | bytes 2097152 | tf_op jit(solution)/shard_map/gram/pallas_call | solution.py:408
  45.8 0.0 copy-start
  45.9 0.0 copy-start.1
  45.9 0.1 collective-permute-start
  45.9 0.0 all-to-all-done.1.own_share
  46.0 0.5 collective-permute-start.1
  46.5 0.0 copy-done.2
  46.5 0.4 own_incidence.1.incidence
  46.9 2.1 %collective-permute-done.other = bf16[2576,256]{1,0:T(8,128)(2,1)S(1)} collective-permute-done((bf16[2576,256]{1,0:T(8,128)(2,1)S(1)}, bf16[2576,256]{1,0:T(8,128)(2,1)S(1)}, u32[]{:S(2)}, u32[]{:S(2)}) %collective-permute-start) | collective-permute-done | bytes 1318944 | tf_op jit(solution)/shard_map/ppermute | solution.py:424
  49.0 0.7 %collective-permute-done.1.other_share = bf16[16,64,256]{2,1,0:T(8,128)(2,1)S(1)} collective-permute-done((bf16[16,64,256]{2,1,0:T(8,128)(2,1)S(1)}, bf16[16,64,256]{2,1,0:T(8,128)(2,1)S(1)}, u32[]{:S(2)}, u32[]{:S(2)}) %collective-permute-start.1) | collective-permute-done | bytes 524320 | tf_op jit(solution)/shard_map/ppermute | solution.py:425
  49.7 0.0 copy-done
  49.7 0.0 copy-done.1
  49.7 5.9 %tail.1 = (bf16[128,256]{1,0:T(8,128)(2,1)}, bf16[128,256]{1,0:T(8,128)(2,1)}, f32[256,256]{1,0:T(8,128)}, f32[1,512]{1,0:T(1,128)}) custom-call(bf16[2576,256]{1,0:T(8,128)(2,1)S(1)} %gram.1.own, bf16[2576,256]{1,0:T(8,128)(2,1)S(1)} %collective-permute-done.other, bf16[16,64,256]{2,1,0:T(8,128)(2,1)S(1)} %all-to-all-done.1.own_share, ...), custom_call_target="tpu_custom_call" | custom-call | tf_op jit(solution)/shard_map/tail/pallas_call | solution.py:426
Async XLA Ops:
  24.5 21.4 %all-to-all-start.1 = ((bf16[16,64,256]{2,1,0:T(8,128)(2,1)}), bf16[16,64,256]{2,1,0:T(8,128)(2,1)S(1)}, u32[]{:S(2)}, u32[]{:S(2)}) async-start(bf16[16,64,256]{2,1,0:T(8,128)(2,1)} %get-tuple-element.17), calls=%async_computation.1 | async-start | bytes 1048576 | tf_op jit(solution)/shard_map/all_to_all | solution.py:406
  28.1 18.3 %copy-start.2 = (bf16[24,512]{1,0:T(8,128)(2,1)S(1)}, bf16[24,512]{1,0:T(8,128)(2,1)}, u32[]{:S(2)}) copy-start(bf16[24,512]{1,0:T(8,128)(2,1)} %get-tuple-element.18.message) | copy-start | bytes 73732
  45.8 3.9 %copy-start = (bf16[256,256]{1,0:T(8,128)(2,1)S(1)}, bf16[256,256]{1,0:T(8,128)(2,1)}, u32[]{:S(2)}) copy-start(bf16[256,256]{1,0:T(8,128)(2,1)} %theta.1) | copy-start | bytes 393220
  45.9 3.9 %copy-start.1 = (f32[1,512]{1,0:T(1,128)S(1)}, f32[1,512]{1,0:T(1,128)}, u32[]{:S(2)}) copy-start(f32[1,512]{1,0:T(1,128)} %get-tuple-element.19.inverse) | copy-start | bytes 6148
  45.9 3.1 %collective-permute-start = (bf16[2576,256]{1,0:T(8,128)(2,1)S(1)}, bf16[2576,256]{1,0:T(8,128)(2,1)S(1)}, u32[]{:S(2)}, u32[]{:S(2)}) collective-permute-start(bf16[2576,256]{1,0:T(8,128)(2,1)S(1)} %gram.1.own), channel_id=1, source_target_pairs={{0,1},{1,0},{2,3},{3,2},{4,5},{5,4},{6,7},{7,6},{8,9},{9,8},{10,11... | collective-permute-start | bytes 3956744 | tf_op jit(solution)/shard_map/ppermute | solution.py:424
  46.0 3.8 %collective-permute-start.1 = (bf16[16,64,256]{2,1,0:T(8,128)(2,1)S(1)}, bf16[16,64,256]{2,1,0:T(8,128)(2,1)S(1)}, u32[]{:S(2)}, u32[]{:S(2)}) collective-permute-start(bf16[16,64,256]{2,1,0:T(8,128)(2,1)S(1)} %all-to-all-done.1.own_share), channel_id=1, source_target_pairs={{0,1},{1,0},{2,3},{3,2},{4,5},{5,4},{6,7},{7,6},{8,9},{9,8},{10,11... | collective-permute-start | bytes 1572872 | tf_op jit(solution)/shard_map/ppermute | solution.py:425

commit v3 on v2

--- a/solution.py
+++ b/solution.py
@@ -119,7 +119,7 @@
 NT = (((1,), (1,)), ((), ()))
 TN = (((0,), (0,)), ((), ()))
 CORES = 2
-STEP = 4
+CHUNKS = 4
 
 
 def params(mebibytes=32):
@@ -143,6 +143,11 @@
     return jnp.where(ids == index_row, jnp.ones((), BIT), jnp.zeros((), BIT))
 
 
+def index_hot(lists, j, chunks):
+    parts = [one_hot(lists[16 * c + j : 16 * c + j + 1, :]) for c in range(chunks)]
+    return jnp.concatenate(parts, axis=1)
+
+
 def column_to_row(column):
     wide = jnp.broadcast_to(column, (column.shape[0], 128))
     return wide.T[0:1, :]
@@ -153,18 +158,17 @@
 
 
 def prep_kernel(
-    counts, rows, cols, weight, features, cotangent,
-    payload, shares, message, inverse,
-    counts_here, rows_here, cols_here, weight_here, share_here, in_sems, out_sems, share_sems,
+    counts, rows, cols, weight, features, cotangent, payload, shares, inverse,
+    counts_here, rows_here, cols_here, weight_here, share_here, sems, share_sems,
 ):
-    copies, height, slots = payload.shape
-    blocks = rows.shape[1]
+    _, blocks, slots = rows.shape
+    chunks = slots // 128
     ent_dev = features.shape[0]
-    share = shares.shape[1] // 2
+    share = share_here.shape[0] // 2
     quarter = lax.axis_index("x") * CORES + lax.axis_index("core")
     here = pl.ds(pl.multiple_of(quarter * share, share), share)
     reads = [
-        pltpu.make_async_copy(source, target, in_sems.at[n])
+        pltpu.make_async_copy(source, target, sems.at[n])
         for n, (source, target) in enumerate(
             (
                 (counts, counts_here),
@@ -181,7 +185,8 @@
     for read in reads:
         read.wait()
     sends = [
-        pltpu.make_async_copy(share_here, shares.at[n], share_sems.at[n]) for n in range(copies)
+        pltpu.make_async_copy(share_here, shares.at[n], share_sems.at[n])
+        for n in range(shares.shape[0])
     ]
     for send in sends:
         send.start()
@@ -204,78 +209,108 @@
     degree = jnp.concatenate([degree[0:1], degree[1:2]], axis=1)
     inverse[...] = 1.0 / (1.0 + degree)
     scale = weight_here[...] / (1.0 + degree)
-    message[...] = jnp.concatenate(
-        [high, low, jnp.broadcast_to(scale, (height - 2 * blocks, slots))], axis=0
-    ).astype(BF)
-    writes = [
-        pltpu.make_async_copy(message, payload.at[n], out_sems.at[n]) for n in range(copies)
-    ]
-    for write in writes:
-        write.start()
-    for write in writes + sends:
-        write.wait()
-
-
-def own_kernel(message, incidence):
-    blocks = message.shape[0] // 3
-    ent_dev = incidence.shape[1] // blocks
-    for j in range(blocks):
-        block = dot(
-            one_hot(message[blocks + j : blocks + j + 1, :]), one_hot(message[j : j + 1, :]), NT
-        ).astype(BF)
+    indices = jnp.concatenate([high, low], axis=0).astype(BF)
+    for c in range(chunks):
+        payload[16 * c : 16 * (c + 1), :] = indices[:, 128 * c : 128 * (c + 1)]
+    ends = [scale[:, 128 * c : 128 * (c + 1)] for c in range(chunks)]
+    ends.append(jnp.zeros((8 - chunks, 128), F32))
+    at = 16 * chunks
+    payload[at : at + 8, :] = jnp.concatenate(ends, axis=0).astype(BF)
+    for send in sends:
+        send.wait()
+
+
+def hold_kernel(source, target):
+    target[...] = source[...]
+
+
+def own_kernel(payload, incidence):
+    ents = incidence.shape[1]
+    ent_dev = TILE // (incidence.shape[0] // TILE)
+    chunks = CHUNKS
+    for j in range(ents // ent_dev):
+        block = dot(index_hot(payload, 8 + j, chunks), index_hot(payload, j, chunks), NT).astype(BF)
         for half in range(2):
             incidence[half * TILE : (half + 1) * TILE, j * ent_dev : (j + 1) * ent_dev] = block[
                 :, half * ent_dev : (half + 1) * ent_dev
             ]
 
 
-def gram_kernel(lists, gram, table, scaled, *sums):
-    shards, height, slots = lists.shape
+def collect_kernel(own, by_x, by_y, by_both, group):
+    mine = lax.axis_index("y") * 2 + lax.axis_index("x")
+    for d, source in enumerate((own, by_x, by_y, by_both)):
+        group[jnp.bitwise_xor(mine, d)] = source[...]
+
+
+def column_rows(ents):
+    spans, start = [], 0
+    for b in range(ents // TILE):
+        end = start + ents - b * TILE + 16
+        spans.append((start, end))
+        start = end
+    return spans
+
+
+def fill(lists, table, scaled):
+    shards = lists.shape[0]
+    chunks = CHUNKS
     ents = table.shape[0]
-    blocks = height // 3
-    ent_dev = ents // blocks
-    tiles = ents // TILE
-    sections = table.shape[1] // STEP
-    for acc in sums:
-        acc[...] = jnp.zeros_like(acc)
+    sections = table.shape[1] // shards
+    ent_dev = TILE // (sections // TILE)
     scaled[ents:, :] = jnp.ones((scaled.shape[0] - ents, scaled.shape[1]), BF)
-
-    def step(i, carry):
-        for q in range(STEP):
-            indices = lists[i * STEP + q]
-            scale = indices[2 * blocks : 2 * blocks + 1]
-            for j in range(blocks):
-                block = dot(
-                    one_hot(indices[j : j + 1]), one_hot(indices[blocks + j : blocks + j + 1]), NT
-                ).astype(BF)
-                rows = slice(j * ent_dev, (j + 1) * ent_dev)
-                for half in range(2):
-                    at = q * sections + half * TILE
-                    part = block[half * ent_dev : (half + 1) * ent_dev, :]
-                    table[rows, at : at + TILE] = part
-                    scaled[rows, at : at + TILE] = part * scale[:, half * TILE : (half + 1) * TILE]
-        for b in range(tiles):
-            sums[b][...] += dot(scaled[b * TILE :, :], table[b * TILE : (b + 1) * TILE, :], NT)
-        return carry
-
-    lax.fori_loop(0, shards // STEP, step, 0)
-    start = 0
+    for q in range(shards):
+        indices = lists.at[q]
+        scale = jnp.concatenate(
+            [indices[16 * chunks + c : 16 * chunks + c + 1, :] for c in range(chunks)], axis=1
+        )
+        for j in range(ents // ent_dev):
+            block = dot(index_hot(indices, j, chunks), index_hot(indices, 8 + j, chunks), NT).astype(BF)
+            rows = slice(j * ent_dev, (j + 1) * ent_dev)
+            for half in range(2):
+                at = q * sections + half * TILE
+                part = block[half * ent_dev : (half + 1) * ent_dev, :]
+                table[rows, at : at + TILE] = part
+                scaled[rows, at : at + TILE] = part * scale[:, half * TILE : (half + 1) * TILE]
+
+
+def column(b, table, scaled):
+    return dot(scaled[b * TILE :, :], table[b * TILE : (b + 1) * TILE, :], NT)
+
+
+def first_kernel(lists, sums, table, scaled):
+    fill(lists, table, scaled)
+    for b, (start, end) in enumerate(column_rows(table.shape[0])):
+        sums[start:end, :] = column(b, table, scaled)
+
+
+def second_kernel(lists, before, sums, table, scaled):
+    fill(lists, table, scaled)
+    for b, (start, end) in enumerate(column_rows(table.shape[0])):
+        sums[start:end, :] = before[start:end, :] + column(b, table, scaled)
+
+
+def last_kernel(lists, pair, single, gram, table, scaled):
+    ents = table.shape[0]
+    spans = column_rows(ents)
+    fill(lists, table, scaled)
+    at = 0
     degrees = []
-    for b in range(tiles):
-        size = ents - b * TILE
-        gram[start : start + size, :] = sums[b][0:size, :].astype(BF)
-        start += size
-        degree = sums[b][size : size + 1, :]
+    for b, (start, end) in enumerate(spans):
+        size = end - start - 16
+        total = pair[start:end, :] + (single[start:end, :] + column(b, table, scaled))
+        gram[at : at + size, :] = total[0:size].astype(BF)
+        at += size
+        degree = total[size : size + 1]
         top = degree.astype(BF).astype(F32)
         degrees += [top, degree - top]
-    degrees.append(jnp.zeros((16 - 2 * tiles, TILE), F32))
-    gram[start : start + 16, :] = jnp.concatenate(degrees, axis=0).astype(BF)
+    degrees.append(jnp.zeros((16 - 2 * len(spans), TILE), F32))
+    gram[at : at + 16, :] = jnp.concatenate(degrees, axis=0).astype(BF)
 
 
 def tail_kernel(
     own, other, own_share, other_share, theta, incidence, inverse,
     activated, grad_features, grad_theta, grad_weight,
-    full, scale, values, backs, acts, projs, feats, cots, sems,
+    full, scale, values, backs, acts, projs, feats, cots,
 ):
     ents = full.shape[0]
     tiles = ents // TILE
@@ -285,17 +320,13 @@
     share = feats.shape[2]
     per_group = feats.shape[0] // groups
     core = lax.axis_index("core")
-    mine = lax.axis_index("ent")
-    loads = []
+    mine = lax.axis_index("z") * 2 + lax.axis_index("y")
+    base = sum(ents - b * TILE for b in range(tiles))
     for n, source in enumerate((own_share, other_share)):
-        at = core if n == 0 else 1 - core
-        loads.append(pltpu.make_async_copy(source.at[:, 0:share, :], feats.at[:, at], sems.at[2 * n]))
-        loads.append(
-            pltpu.make_async_copy(source.at[:, share : 2 * share, :], cots.at[:, at], sems.at[2 * n + 1])
-        )
-    for load in loads:
-        load.start()
-    base = sum(ents - b * TILE for b in range(tiles))
+        which = core if n == 0 else 1 - core
+        for q in range(source.shape[0]):
+            feats[q, which] = source[q, 0:share, :]
+            cots[q, which] = source[q, share : 2 * share, :]
     degree_rows = own[base : base + 16, :].astype(F32) + other[base : base + 16, :].astype(F32)
     for b in range(tiles):
         row = lax.rsqrt(1.0 + (degree_rows[2 * b : 2 * b + 1] + degree_rows[2 * b + 1 : 2 * b + 2]))
@@ -312,8 +343,6 @@
                 if a != b:
                     full[b * TILE : (b + 1) * TILE, pl.ds(pl.multiple_of(column + a * TILE, TILE), TILE)] = piece.T
                 start += TILE
-    for load in loads:
-        load.wait()
 
     def es(at, size):
         part = scale[at : at + size, :]
@@ -363,36 +392,35 @@
     _, blocks, slots = pair_rows.shape
     ents = blocks * ent_dev
     tiles = ents // TILE
-    lanes = lax.axis_size("x")
-    chips = lax.axis_size("ent") * lanes
-    share = ent_dev // (lanes * CORES)
-    height = 3 * blocks
-    dma = pltpu.SemaphoreType.DMA
+    group = lax.axis_size("y") * lax.axis_size("x")
+    layers = lax.axis_size("z")
+    share = ent_dev // (lax.axis_size("x") * CORES)
+    height = CHUNKS * 16 + 8
     swap = [(0, 1), (1, 0)]
-    payload, shares, message, inverse = pl.pallas_call(
+    payload, shares, inverse = pl.pallas_call(
         prep_kernel,
         out_shape=(
-            jax.ShapeDtypeStruct((chips, height, slots), BF),
-            jax.ShapeDtypeStruct((chips, 2 * share, width), BF),
-            jax.ShapeDtypeStruct((height, slots), BF),
+            jax.ShapeDtypeStruct((height, 128), BF),
+            jax.ShapeDtypeStruct((layers * group, 2 * share, width), BF),
             jax.ShapeDtypeStruct((1, sec_dev), F32),
         ),
         in_specs=[hbm()] * 6,
-        out_specs=(hbm(), hbm(), vmem(), vmem()),
+        out_specs=(vmem(), hbm(), vmem()),
         scratch_shapes=[
             pltpu.SMEM((1, blocks), jnp.int32),
             pltpu.VMEM((blocks, slots), jnp.int32),
             pltpu.VMEM((blocks, slots), jnp.int32),
             pltpu.VMEM((1, sec_dev), F32),
             pltpu.VMEM((2 * share, width), BF),
-            dma((6,)),
-            dma((chips,)),
-            dma((chips,)),
+            pltpu.SemaphoreType.DMA((6,)),
+            pltpu.SemaphoreType.DMA((layers * group,)),
         ],
         compiler_params=params(63),
         name="prep",
     )(pair_counts, pair_rows, pair_cols, section_weight.reshape(1, sec_dev), features, cotangent)
-    lists = lax.all_to_all(payload, ("ent", "x"), 0, 0, tiled=True)
+    by_x = lax.ppermute(payload, "x", swap)
+    by_y = lax.ppermute(payload, "y", swap)
+    by_both = lax.ppermute(payload, ("y", "x"), [(i, i ^ 3) for i in range(4)])
     incidence = pl.pallas_call(
         own_kernel,
         out_shape=jax.ShapeDtypeStruct((sec_dev, ents), BF),
@@ -401,28 +429,57 @@
         compiler_params=params(),
         cost_estimate=pl.CostEstimate(flops=2 * sec_dev * ents * slots, bytes_accessed=2**20, transcendentals=0),
         name="own_incidence",
-    )(message)
-    lists, shares = lax.optimization_barrier((lists, shares))
-    own_share = lax.all_to_all(shares, ("ent", "x"), 0, 0, tiled=True)
-    heights = [ents - b * TILE for b in range(tiles)]
-    own = pl.pallas_call(
-        gram_kernel,
-        out_shape=jax.ShapeDtypeStruct((sum(heights) + 16, TILE), BF),
+    )(payload)
+    held = pl.pallas_call(
+        hold_kernel,
+        out_shape=jax.ShapeDtypeStruct(payload.shape, BF),
         in_specs=[vmem()],
         out_specs=vmem(),
-        scratch_shapes=[
-            pltpu.VMEM((ents, STEP * sec_dev), BF),
-            pltpu.VMEM((ents + 16, STEP * sec_dev), BF),
-        ]
-        + [pltpu.VMEM((h + 16, TILE), F32) for h in heights],
         compiler_params=params(),
-        cost_estimate=pl.CostEstimate(
-            flops=2 * chips * sec_dev * (sum(heights) * TILE + ents * slots), bytes_accessed=2**21, transcendentals=0
-        ),
-        name="gram",
-    )(lists)
+        name="hold",
+    )(payload)
+    near = pl.pallas_call(
+        collect_kernel,
+        out_shape=jax.ShapeDtypeStruct((group,) + payload.shape, BF),
+        in_specs=[vmem()] * 4,
+        out_specs=vmem(),
+        compiler_params=params(),
+        name="collect",
+    )(held, by_x, by_y, by_both)
+
+    shares, near = lax.optimization_barrier((shares, near))
+
+    def across(d):
+        return lax.ppermute(near, "z", [(i, i ^ d) for i in range(layers)])
+
+    far = [near] + [across(d) for d in range(1, layers)]
+    rows = column_rows(ents)[-1][1]
+    scratch = [pltpu.VMEM((ents, group * sec_dev), BF), pltpu.VMEM((ents + 16, group * sec_dev), BF)]
+
+    def step(kernel, shape, kind, name, inputs):
+        return pl.pallas_call(
+            kernel,
+            out_shape=jax.ShapeDtypeStruct(shape, kind),
+            in_specs=jax.tree.map(lambda _: vmem(), list(inputs)),
+            out_specs=vmem(),
+            scratch_shapes=scratch,
+            compiler_params=params(),
+            cost_estimate=pl.CostEstimate(
+                flops=1000000000, bytes_accessed=1000, transcendentals=0
+            ),
+            name=name,
+        )(*inputs)
+
+    sums = step(first_kernel, (rows, TILE), F32, "gram_first", [far[0]])
+    pair = step(second_kernel, (rows, TILE), F32, "gram_second", [far[1], sums])
+    third, pair = lax.optimization_barrier((far[2], pair))
+    single = step(first_kernel, (rows, TILE), F32, "gram_third", [third])
+    fourth, single = lax.optimization_barrier((far[3], single))
+    own = step(last_kernel, (rows - 16 * tiles + 16, TILE), BF, "gram_last", [fourth, pair, single])
     other = lax.ppermute(own, "core", swap)
+    own_share = lax.all_to_all(shares, ("z", "y", "x"), 0, 0, tiled=True)
     other_share = lax.ppermute(own_share, "core", swap)
+    tail_in = (own, other, own_share, other_share, theta, incidence, inverse)
     activated, grad_features, grad_theta, grad_weight = pl.pallas_call(
         tail_kernel,
         out_shape=(
@@ -431,7 +488,7 @@
             jax.ShapeDtypeStruct((width, width), F32),
             jax.ShapeDtypeStruct((1, sec_dev), F32),
         ),
-        in_specs=[vmem(), vmem(), hbm(), hbm(), vmem(), vmem(), vmem()],
+        in_specs=[vmem()] * len(tail_in),
         out_specs=(vmem(),) * 4,
         scratch_shapes=[
             pltpu.VMEM((ents, 2 * ents), BF),
@@ -440,38 +497,37 @@
             pltpu.VMEM((2 * ents, width), BF),
             pltpu.VMEM((ents, width), BF),
             pltpu.VMEM((ents, width), BF),
-            pltpu.VMEM((chips, CORES, share, width), BF),
-            pltpu.VMEM((chips, CORES, share, width), BF),
-            dma((4,)),
+            pltpu.VMEM((layers * group, CORES, share, width), BF),
+            pltpu.VMEM((layers * group, CORES, share, width), BF),
         ],
         compiler_params=params(),
         name="tail",
-    )(own, other, own_share, other_share, theta, incidence, inverse)
+    )(*tail_in)
     return activated, grad_features, grad_theta, grad_weight.reshape(sec_dev)
 
 
 def solution(mesh):
     ent, sec = mesh.shape["ent"], mesh.shape["sec"]
-    dense = ent <= 8 and sec % CORES == 0
+    dense = ent == 8 and sec == 4
     if dense:
-        grid = Mesh(mesh.devices.reshape(ent, sec // CORES, CORES), ("ent", "x", "core"))
-        split = ("ent", "x", "core")
+        grid = Mesh(mesh.devices.reshape(ent // 2, 2, sec // CORES, CORES), ("z", "y", "x", "core"))
+        whole, split = ("z", "y"), ("z", "y", "x", "core")
     else:
         grid = mesh
-        split = ("ent", "sec")
+        whole, split = "ent", ("ent", "sec")
     placed = (
-        P("ent", None),
+        P(whole, None),
         P(),
         P(split),
         P(split, None, None),
         P(split, None, None),
         P(split, None),
-        P("ent", None),
+        P(whole, None),
     )
     return jax.shard_map(
         dense_body if dense else body,
         mesh=grid,
         in_specs=placed,
-        out_specs=(P("ent", None), P("ent", None), P(), P(split)),
+        out_specs=(P(whole, None), P(whole, None), P(), P(split)),
         check_vma=False,
     )

time: 56 us -> 48.4 us (0.86)
  blocking collectives: 21 us -> 0 us
  starting transfers between devices: 4.15 us -> 14.5 us
  waiting for transfers between devices: 2.83 us -> 6.92 us
  Pallas kernels: 26.9 us -> 25.1 us
  local copies, waits for them, and re-layouts: 0.02 us -> 0.79 us
    all_to_all x1 -> x0, blocking collectives: 21 us -> none  [dense_body(): lists = lax.all_to_all(payload, ('ent', 'x'), 0, 0, tiled=True)]
    ppermute x0 -> x6, starting transfers between devices: none -> 9 us  [the longest x3 4.45 us: across(): return lax.ppermute(near, 'z', [(i, i ^ d) for i in range(layers)])]
    ppermute x0 -> x6, waiting for transfers between devices: none -> 4.08 us  [the longest x1 2.42 us: dense_body(): by_both = lax.ppermute(payload, ('y', 'x'), [(i, i ^ 3) for i in range(4)])]
    pallas_call x2 -> x7, Pallas kernels: 20.6 us -> 19 us  [the longest x4 16.6 us: step(): pl.pallas_call(kernel, out_shape=jax.ShapeDtypeStruct(shape, kind), in_sp...]
    all_to_all x1, starting transfers between devices: 3.59 us -> 4.98 us  [dense_body(): own_share = lax.all_to_all(shares, ('z', 'y', 'x'), 0, 0, tiled=True)]
    unnamed x6 -> x8, local copies, waits for them, and re-layouts: 0.02 us -> 0.79 us
  transfers between devices with their start and end apart: 3 -> 9, of which waited for: 2 -> 4; matrix products, arithmetic and copies ran while one was open for 0% -> 0% of each run, Pallas kernels for 33% -> 35%
where the time goes in v3:
time: 48.4 us; the launch traced here: 48.1 us
  Pallas kernels  25.1 us (52%)
  starting transfers between devices  14.5 us (30%)
  waiting for transfers between devices  6.92 us (14%)
  local copies, waits for them, and re-layouts  0.79 us (2%)
  between operations  0.76 us (2%)
    pallas_call x4, Pallas kernels, step(): pl.pallas_call(kernel, out_shape=jax.ShapeDtypeStruct(shape, kind), in_sp...  16.6 us
    pallas_call x1, Pallas kernels, dense_body(): pl.pallas_call(tail_kernel, out_shape=(jax.ShapeDtypeStruct((ent_dev, wid...  5.66 us
    all_to_all x1, starting transfers between devices, dense_body(): own_share = lax.all_to_all(shares, ('z', 'y', 'x'), 0, 0, tiled=True)  4.98 us
    ppermute x3, starting transfers between devices, across(): return lax.ppermute(near, 'z', [(i, i ^ d) for i in range(layers)])  4.45 us
    ppermute x1, starting transfers between devices, dense_body(): by_x = lax.ppermute(payload, 'x', swap)  3 us
    ppermute x1, waiting for transfers between devices, dense_body(): by_both = lax.ppermute(payload, ('y', 'x'), [(i, i ^ 3) for i in range(4)])  2.42 us
    pallas_call x1, Pallas kernels, dense_body(): pl.pallas_call(prep_kernel, out_shape=(jax.ShapeDtypeStruct((height, 128)...  2.38 us
    ppermute x1, waiting for transfers between devices, dense_body(): other = lax.ppermute(own, 'core', swap)  2.08 us
  transfers between devices with their start and end apart: 9, of which 4 were waited for; matrix products, arithmetic and copies ran while one was open for 0% of the time, Pallas kernels for 35%

profile of v3, /device:TPU:0, one launch (start us, length us, event | category | flops | bytes accessed | tf_op | source)
XLA Modules:
  0.0 48.1 jit_solution(8273197879871121716)
XLA Ops:
  0.6 2.4 %prep.1 = (bf16[72,128]{1,0:T(8,128)(2,1)}, bf16[16,64,256]{2,1,0:T(8,128)(2,1)}, f32[1,512]{1,0:T(1,128)}) custom-call(s32[1,8]{1,0:T(1,128)} %counts.1, s32[1,8,512]{2,1,0:T(8,128)} %rows.1, s32[1,8,512]{2,1,0:T(8,128)} %cols.1, f32[1,512]{1,0:T(1,128)} %bitcast.2, bf16[128,256]{1,0:T(8,128)(2,1)} %features.1, bf16[128,256]{1,0:T(8,128)(2,1)} %cotangent.1), custom_call_target="tpu_custom_call" | custom-call | tf_op jit(solution)/shard_map/prep/pallas_call | solution.py:400
  3.0 3.0 %collective-permute-start = (bf16[72,128]{1,0:T(8,128)(2,1)}, bf16[72,128]{1,0:T(8,128)(2,1)S(1)}, u32[]{:S(2)}, u32[]{:S(2)}) collective-permute-start(bf16[72,128]{1,0:T(8,128)(2,1)} %get-tuple-element.18.source.payload), channel_id=1, source_target_pairs={{0,2},{2,0},{1,3},{3,1},{4,6},{6,4},{5,7},{7,5},{8,10},{10,8},{9,1... | collective-permute-start | bytes 55304 | tf_op jit(solution)/shard_map/ppermute | solution.py:421
  6.0 1.5 %collective-permute-start.1 = (bf16[72,128]{1,0:T(8,128)(2,1)}, bf16[72,128]{1,0:T(8,128)(2,1)S(1)}, u32[]{:S(2)}, u32[]{:S(2)}) collective-permute-start(bf16[72,128]{1,0:T(8,128)(2,1)} %get-tuple-element.18.source.payload), channel_id=1, source_target_pairs={{0,4},{4,0},{1,5},{5,1},{2,6},{6,2},{3,7},{7,3},{8,12},{12,8},{9,1... | collective-permute-start | bytes 55304 | tf_op jit(solution)/shard_map/ppermute | solution.py:422
  7.5 0.0 collective-permute-start.2
  7.6 0.8 %copy-done.1 = bf16[72,128]{1,0:T(8,128)(2,1)S(1)} copy-done((bf16[72,128]{1,0:T(8,128)(2,1)S(1)}, bf16[72,128]{1,0:T(8,128)(2,1)}, u32[]{:S(2)}) %copy-start.1) | copy-done | bytes 18456
  8.3 0.0 collective-permute-done.by_x
  8.3 1.7 %collective-permute-done.1.by_y = bf16[72,128]{1,0:T(8,128)(2,1)S(1)} collective-permute-done((bf16[72,128]{1,0:T(8,128)(2,1)}, bf16[72,128]{1,0:T(8,128)(2,1)S(1)}, u32[]{:S(2)}, u32[]{:S(2)}) %collective-permute-start.1) | collective-permute-done | bytes 18464 | tf_op jit(solution)/shard_map/ppermute | solution.py:422
  10.0 2.4 %collective-permute-done.2.by_both = bf16[72,128]{1,0:T(8,128)(2,1)S(1)} collective-permute-done((bf16[72,128]{1,0:T(8,128)(2,1)}, bf16[72,128]{1,0:T(8,128)(2,1)S(1)}, u32[]{:S(2)}, u32[]{:S(2)}) %collective-permute-start.2) | collective-permute-done | bytes 18464 | tf_op jit(solution)/shard_map/ppermute | solution.py:423
  12.4 1.6 %collective-permute-start.5 = (bf16[4,72,128]{2,1,0:T(8,128)(2,1)S(1)}, bf16[4,72,128]{2,1,0:T(8,128)(2,1)S(1)}, u32[]{:S(2)}, u32[]{:S(2)}) collective-permute-start(bf16[4,72,128]{2,1,0:T(8,128)(2,1)S(1)} %collect.1.lists), channel_id=1, source_target_pairs={{0,8},{8,0},{16,24},{24,16},{1,9},{9,1},{17,25},{25,17},{2,10},{10... | collective-permute-start | bytes 221192 | tf_op jit(solution)/shard_map/ppermute | solution.py:453
  14.1 2.6 %collective-permute-start.4 = (bf16[4,72,128]{2,1,0:T(8,128)(2,1)S(1)}, bf16[4,72,128]{2,1,0:T(8,128)(2,1)S(1)}, u32[]{:S(2)}, u32[]{:S(2)}) collective-permute-start(bf16[4,72,128]{2,1,0:T(8,128)(2,1)S(1)} %collect.1.lists), channel_id=1, source_target_pairs={{0,16},{8,24},{16,0},{24,8},{1,17},{9,25},{17,1},{25,9},{2,18},{10... | collective-permute-start | bytes 221192 | tf_op jit(solution)/shard_map/ppermute | solution.py:453
  16.7 0.2 collective-permute-start.3
  16.9 5.0 %all-to-all-start = ((bf16[16,64,256]{2,1,0:T(8,128)(2,1)}), bf16[16,64,256]{2,1,0:T(8,128)(2,1)S(1)}, u32[]{:S(2)}, u32[]{:S(2)}) async-start(bf16[16,64,256]{2,1,0:T(8,128)(2,1)} %get-tuple-element.24), calls=%async_computation | async-start | bytes 1048576 | tf_op jit(solution)/shard_map/all_to_all | solution.py:480
  21.9 4.1 %gram_first.1.before = f32[2624,256]{1,0:T(8,128)S(1)} custom-call(bf16[4,72,128]{2,1,0:T(8,128)(2,1)S(1)} %collect.1.lists), custom_call_target="tpu_custom_call" | custom-call | flops 1000000000 | bytes 1000 | tf_op jit(solution)/shard_map/gram_first/pallas_call | solution.py:460
  26.0 0.0 collective-permute-done.5.lists
  26.0 4.1 %gram_second.1.pair = f32[2624,256]{1,0:T(8,128)S(1)} custom-call(bf16[4,72,128]{2,1,0:T(8,128)(2,1)S(1)} %collective-permute-done.5.lists, f32[2624,256]{1,0:T(8,128)S(1)} %gram_first.1.before), custom_call_target="tpu_custom_call" | custom-call | flops 1000000000 | bytes 1000 | tf_op jit(solution)/shard_map/gram_second/pallas_call | solution.py:460
  30.1 0.0 collective-permute-done.4.lists
  30.1 4.1 %gram_third.1.single = f32[2624,256]{1,0:T(8,128)S(1)} custom-call(bf16[4,72,128]{2,1,0:T(8,128)(2,1)S(1)} %collective-permute-done.4.lists), custom_call_target="tpu_custom_call" | custom-call | flops 1000000000 | bytes 1000 | tf_op jit(solution)/shard_map/gram_third/pallas_call | solution.py:460
  34.2 0.0 copy-start.2
  34.2 0.0 copy-start
  34.2 0.0 copy-start.3
  34.3 0.0 collective-permute-done.3.lists
  34.3 4.3 %gram_last.1.own = bf16[2576,256]{1,0:T(8,128)(2,1)S(1)} custom-call(bf16[4,72,128]{2,1,0:T(8,128)(2,1)S(1)} %collective-permute-done.3.lists, f32[2624,256]{1,0:T(8,128)S(1)} %gram_second.1.pair, f32[2624,256]{1,0:T(8,128)S(1)} %gram_third.1.single), custom_call_target="tpu_custom_call" | custom-call | flops 1000000000 | bytes 1000 | tf_op jit(solution)/shard_map/gram_last/pallas_call | solution.py:460
  38.6 0.1 collective-permute-start.6
  38.7 0.0 all-to-all-done.own_share
  38.7 0.5 %collective-permute-start.7 = (bf16[16,64,256]{2,1,0:T(8,128)(2,1)S(1)}, bf16[16,64,256]{2,1,0:T(8,128)(2,1)S(1)}, u32[]{:S(2)}, u32[]{:S(2)}) collective-permute-start(bf16[16,64,256]{2,1,0:T(8,128)(2,1)S(1)} %all-to-all-done.own_share), channel_id=1, source_target_pairs={{0,1},{1,0},{2,3},{3,2},{4,5},{5,4},{6,7},{7,6},{8,9},{9,8},{10,11... | collective-permute-start | bytes 1572872 | tf_op jit(solution)/shard_map/ppermute | solution.py:481
  39.2 0.0 copy-done.2
  39.2 0.4 own_incidence.1.incidence
  39.6 2.1 %collective-permute-done.6.other = bf16[2576,256]{1,0:T(8,128)(2,1)S(1)} collective-permute-done((bf16[2576,256]{1,0:T(8,128)(2,1)S(1)}, bf16[2576,256]{1,0:T(8,128)(2,1)S(1)}, u32[]{:S(2)}, u32[]{:S(2)}) %collective-permute-start.6) | collective-permute-done | bytes 1318944 | tf_op jit(solution)/shard_map/ppermute | solution.py:479
  41.7 0.7 %collective-permute-done.7.other_share = bf16[16,64,256]{2,1,0:T(8,128)(2,1)S(1)} collective-permute-done((bf16[16,64,256]{2,1,0:T(8,128)(2,1)S(1)}, bf16[16,64,256]{2,1,0:T(8,128)(2,1)S(1)}, u32[]{:S(2)}, u32[]{:S(2)}) %collective-permute-start.7) | collective-permute-done | bytes 524320 | tf_op jit(solution)/shard_map/ppermute | solution.py:481
  42.4 0.0 copy-done
  42.4 0.0 copy-done.3
  42.4 5.7 %tail.1 = (bf16[128,256]{1,0:T(8,128)(2,1)}, bf16[128,256]{1,0:T(8,128)(2,1)}, f32[256,256]{1,0:T(8,128)}, f32[1,512]{1,0:T(1,128)}) custom-call(bf16[2576,256]{1,0:T(8,128)(2,1)S(1)} %gram_last.1.own, bf16[2576,256]{1,0:T(8,128)(2,1)S(1)} %collective-permute-done.6.other, bf16[16,64,256]{2,1,0:T(8,128)(2,1)S(1)} %all-to-all-done.own_share, ...), custom_call_target="tpu_custom_call" | custom-call | tf_op jit(solution)/shard_map/tail/pallas_call | solution.py:483
  (3 shorter events, 0.0 us)
Async XLA Ops:
  3.0 5.3 %collective-permute-start = (bf16[72,128]{1,0:T(8,128)(2,1)}, bf16[72,128]{1,0:T(8,128)(2,1)S(1)}, u32[]{:S(2)}, u32[]{:S(2)}) collective-permute-start(bf16[72,128]{1,0:T(8,128)(2,1)} %get-tuple-element.18.source.payload), channel_id=1, source_target_pairs={{0,2},{2,0},{1,3},{3,1},{4,6},{6,4},{5,7},{7,5},{8,10},{10,8},{9,1... | collective-permute-start | bytes 55304 | tf_op jit(solution)/shard_map/ppermute | solution.py:421
  6.0 4.0 %collective-permute-start.1 = (bf16[72,128]{1,0:T(8,128)(2,1)}, bf16[72,128]{1,0:T(8,128)(2,1)S(1)}, u32[]{:S(2)}, u32[]{:S(2)}) collective-permute-start(bf16[72,128]{1,0:T(8,128)(2,1)} %get-tuple-element.18.source.payload), channel_id=1, source_target_pairs={{0,4},{4,0},{1,5},{5,1},{2,6},{6,2},{3,7},{7,3},{8,12},{12,8},{9,1... | collective-permute-start | bytes 55304 | tf_op jit(solution)/shard_map/ppermute | solution.py:422
  7.5 4.9 %collective-permute-start.2 = (bf16[72,128]{1,0:T(8,128)(2,1)}, bf16[72,128]{1,0:T(8,128)(2,1)S(1)}, u32[]{:S(2)}, u32[]{:S(2)}) collective-permute-start(bf16[72,128]{1,0:T(8,128)(2,1)} %get-tuple-element.18.source.payload), channel_id=1, source_target_pairs={{0,6},{2,4},{4,2},{6,0},{1,7},{3,5},{5,3},{7,1},{8,14},{10,12},{12... | collective-permute-start | bytes 55304 | tf_op jit(solution)/shard_map/ppermute | solution.py:423
  7.6 0.8 %copy-start.1 = (bf16[72,128]{1,0:T(8,128)(2,1)S(1)}, bf16[72,128]{1,0:T(8,128)(2,1)}, u32[]{:S(2)}) copy-start(bf16[72,128]{1,0:T(8,128)(2,1)} %get-tuple-element.18.source.payload) | copy-start | bytes 55300
  12.4 13.5 %collective-permute-start.5 = (bf16[4,72,128]{2,1,0:T(8,128)(2,1)S(1)}, bf16[4,72,128]{2,1,0:T(8,128)(2,1)S(1)}, u32[]{:S(2)}, u32[]{:S(2)}) collective-permute-start(bf16[4,72,128]{2,1,0:T(8,128)(2,1)S(1)} %collect.1.lists), channel_id=1, source_target_pairs={{0,8},{8,0},{16,24},{24,16},{1,9},{9,1},{17,25},{25,17},{2,10},{10... | collective-permute-start | bytes 221192 | tf_op jit(solution)/shard_map/ppermute | solution.py:453
  14.1 16.0 %collective-permute-start.4 = (bf16[4,72,128]{2,1,0:T(8,128)(2,1)S(1)}, bf16[4,72,128]{2,1,0:T(8,128)(2,1)S(1)}, u32[]{:S(2)}, u32[]{:S(2)}) collective-permute-start(bf16[4,72,128]{2,1,0:T(8,128)(2,1)S(1)} %collect.1.lists), channel_id=1, source_target_pairs={{0,16},{8,24},{16,0},{24,8},{1,17},{9,25},{17,1},{25,9},{2,18},{10... | collective-permute-start | bytes 221192 | tf_op jit(solution)/shard_map/ppermute | solution.py:453
  16.7 17.6 %collective-permute-start.3 = (bf16[4,72,128]{2,1,0:T(8,128)(2,1)S(1)}, bf16[4,72,128]{2,1,0:T(8,128)(2,1)S(1)}, u32[]{:S(2)}, u32[]{:S(2)}) collective-permute-start(bf16[4,72,128]{2,1,0:T(8,128)(2,1)S(1)} %collect.1.lists), channel_id=1, source_target_pairs={{0,24},{8,16},{16,8},{24,0},{1,25},{9,17},{17,9},{25,1},{2,26},{10... | collective-permute-start | bytes 221192 | tf_op jit(solution)/shard_map/ppermute | solution.py:453
  16.9 21.8 %all-to-all-start = ((bf16[16,64,256]{2,1,0:T(8,128)(2,1)}), bf16[16,64,256]{2,1,0:T(8,128)(2,1)S(1)}, u32[]{:S(2)}, u32[]{:S(2)}) async-start(bf16[16,64,256]{2,1,0:T(8,128)(2,1)} %get-tuple-element.24), calls=%async_computation | async-start | bytes 1048576 | tf_op jit(solution)/shard_map/all_to_all | solution.py:480
  34.2 4.9 %copy-start.2 = (bf16[72,128]{1,0:T(8,128)(2,1)S(1)}, bf16[72,128]{1,0:T(8,128)(2,1)}, u32[]{:S(2)}) copy-start(bf16[72,128]{1,0:T(8,128)(2,1)} %get-tuple-element.18.source.payload) | copy-start | bytes 55300
  34.2 8.2 %copy-start = (bf16[256,256]{1,0:T(8,128)(2,1)S(1)}, bf16[256,256]{1,0:T(8,128)(2,1)}, u32[]{:S(2)}) copy-start(bf16[256,256]{1,0:T(8,128)(2,1)} %theta.1) | copy-start | bytes 393220
  34.2 8.2 %copy-start.3 = (f32[1,512]{1,0:T(1,128)S(1)}, f32[1,512]{1,0:T(1,128)}, u32[]{:S(2)}) copy-start(f32[1,512]{1,0:T(1,128)} %get-tuple-element.25.inverse) | copy-start | bytes 6148
  38.6 3.1 %collective-permute-start.6 = (bf16[2576,256]{1,0:T(8,128)(2,1)S(1)}, bf16[2576,256]{1,0:T(8,128)(2,1)S(1)}, u32[]{:S(2)}, u32[]{:S(2)}) collective-permute-start(bf16[2576,256]{1,0:T(8,128)(2,1)S(1)} %gram_last.1.own), channel_id=1, source_target_pairs={{0,1},{1,0},{2,3},{3,2},{4,5},{5,4},{6,7},{7,6},{8,9},{9,8},{10,11... | collective-permute-start | bytes 3956744 | tf_op jit(solution)/shard_map/ppermute | solution.py:479
  38.7 3.8 %collective-permute-start.7 = (bf16[16,64,256]{2,1,0:T(8,128)(2,1)S(1)}, bf16[16,64,256]{2,1,0:T(8,128)(2,1)S(1)}, u32[]{:S(2)}, u32[]{:S(2)}) collective-permute-start(bf16[16,64,256]{2,1,0:T(8,128)(2,1)S(1)} %all-to-all-done.own_share), channel_id=1, source_target_pairs={{0,1},{1,0},{2,3},{3,2},{4,5},{5,4},{6,7},{7,6},{8,9},{9,8},{10,11... | collective-permute-start | bytes 1572872 | tf_op jit(solution)/shard_map/ppermute | solution.py:481

commit v4 on v3

--- a/solution.py
+++ b/solution.py
@@ -158,8 +158,8 @@
 
 
 def prep_kernel(
-    counts, rows, cols, weight, features, cotangent, payload, shares, inverse,
-    counts_here, rows_here, cols_here, weight_here, share_here, sems, share_sems,
+    counts, rows, cols, weight, features, cotangent, payload, inverse,
+    counts_here, rows_here, cols_here, weight_here, share_here, sems,
 ):
     _, blocks, slots = rows.shape
     chunks = slots // 128
@@ -184,12 +184,6 @@
         read.start()
     for read in reads:
         read.wait()
-    sends = [
-        pltpu.make_async_copy(share_here, shares.at[n], share_sems.at[n])
-        for n in range(shares.shape[0])
-    ]
-    for send in sends:
-        send.start()
     row_ids = rows_here[...]
     sub = lax.broadcasted_iota(jnp.int32, (blocks, slots), 0)
     lane = lax.broadcasted_iota(jnp.int32, (blocks, slots), 1)
@@ -216,15 +210,30 @@
     ends.append(jnp.zeros((8 - chunks, 128), F32))
     at = 16 * chunks
     payload[at : at + 8, :] = jnp.concatenate(ends, axis=0).astype(BF)
-    for send in sends:
-        send.wait()
+    at += 8
+    for n in range(2):
+        for half in range(2):
+            payload[at : at + share, :] = share_here[n * share : (n + 1) * share, half * 128 : (half + 1) * 128]
+            at += share
 
 
 def hold_kernel(source, target):
     target[...] = source[...]
 
 
-def own_kernel(payload, incidence):
+def square(gram, full):
+    ents = full.shape[0]
+    start = 0
+    for b in range(0, ents, TILE):
+        for a in range(b, ents, TILE):
+            piece = gram[start : start + TILE, :]
+            full[a : a + TILE, b : b + TILE] = piece
+            if a != b:
+                full[b : b + TILE, a : a + TILE] = piece.T
+            start += TILE
+
+
+def own_kernel(payload, gram, incidence, full):
     ents = incidence.shape[1]
     ent_dev = TILE // (incidence.shape[0] // TILE)
     chunks = CHUNKS
@@ -234,11 +243,12 @@
             incidence[half * TILE : (half + 1) * TILE, j * ent_dev : (j + 1) * ent_dev] = block[
                 :, half * ent_dev : (half + 1) * ent_dev
             ]
-
-
-def collect_kernel(own, by_x, by_y, by_both, group):
-    mine = lax.axis_index("y") * 2 + lax.axis_index("x")
-    for d, source in enumerate((own, by_x, by_y, by_both)):
+    square(gram, full)
+
+
+def collect_kernel(own, first, second, third, group):
+    mine = lax.axis_index("z")
+    for d, source in enumerate((own, first, second, third)):
         group[jnp.bitwise_xor(mine, d)] = source[...]
 
 
@@ -289,7 +299,7 @@
         sums[start:end, :] = before[start:end, :] + column(b, table, scaled)
 
 
-def last_kernel(lists, pair, single, gram, table, scaled):
+def last_kernel(lists, pair, single, near, third, gram, table, scaled):
     ents = table.shape[0]
     spans = column_rows(ents)
     fill(lists, table, scaled)
@@ -305,85 +315,81 @@
         degrees += [top, degree - top]
     degrees.append(jnp.zeros((16 - 2 * len(spans), TILE), F32))
     gram[at : at + 16, :] = jnp.concatenate(degrees, axis=0).astype(BF)
+    at += 16
+    for source in near + (third, lists):
+        shards, height, _ = source.shape
+        top = 16 * CHUNKS + 8
+        share = (height - top) // 4
+        for q in range(shards):
+            for k in range(4):
+                rows = slice(at + k // 2 * share, at + (k // 2 + 1) * share)
+                gram[rows, k % 2 * 128 : k % 2 * 128 + 128] = source[q, top + k * share : top + (k + 1) * share, :]
+            at += 2 * share
 
 
 def tail_kernel(
-    own, other, own_share, other_share, theta, incidence, inverse,
+    own, other, full, theta, incidence, inverse,
     activated, grad_features, grad_theta, grad_weight,
-    full, scale, values, backs, acts, projs, feats, cots,
+    rest, scale, values, backs, acts, feats, cots,
 ):
     ents = full.shape[0]
     tiles = ents // TILE
     ent_dev = activated.shape[0]
-    groups = ents // ent_dev
     width = theta.shape[0]
     share = feats.shape[2]
-    per_group = feats.shape[0] // groups
+    per_group = feats.shape[0] // (ents // ent_dev)
     core = lax.axis_index("core")
     mine = lax.axis_index("z") * 2 + lax.axis_index("y")
     base = sum(ents - b * TILE for b in range(tiles))
-    for n, source in enumerate((own_share, other_share)):
+    columns = lax.axis_size("y") * lax.axis_size("x")
+    column_here = lax.axis_index("y") * 2 + lax.axis_index("x")
+    for n, source in enumerate((own, other)):
         which = core if n == 0 else 1 - core
-        for q in range(source.shape[0]):
-            feats[q, which] = source[q, 0:share, :]
-            cots[q, which] = source[q, share : 2 * share, :]
+        at = base + 16
+        for d in range(columns):
+            there = jnp.bitwise_xor(column_here, d)
+            for q in range(feats.shape[0] // columns):
+                feats[q * columns + there, which] = source[at : at + share, :]
+                cots[q * columns + there, which] = source[at + share : at + 2 * share, :]
+                at += 2 * share
     degree_rows = own[base : base + 16, :].astype(F32) + other[base : base + 16, :].astype(F32)
     for b in range(tiles):
         row = lax.rsqrt(1.0 + (degree_rows[2 * b : 2 * b + 1] + degree_rows[2 * b + 1 : 2 * b + 2]))
         for h in range(TILE // 128):
             at = b * TILE + h * 128
             scale[at : at + 128, :] = row_to_column(row[:, h * 128 : (h + 1) * 128])
-    for n, source in enumerate((own, other)):
-        column = (core if n == 0 else 1 - core) * ents
-        start = 0
-        for b in range(tiles):
-            for a in range(b, tiles):
-                piece = source[start : start + TILE, :]
-                full[a * TILE : (a + 1) * TILE, pl.ds(pl.multiple_of(column + b * TILE, TILE), TILE)] = piece
-                if a != b:
-                    full[b * TILE : (b + 1) * TILE, pl.ds(pl.multiple_of(column + a * TILE, TILE), TILE)] = piece.T
-                start += TILE
-
-    def es(at, size):
-        part = scale[at : at + size, :]
-        return jnp.concatenate([part] * (width // 128), axis=1)
-
-    def rows_of(stack, g):
-        return stack[g * per_group : (g + 1) * per_group].reshape(ent_dev, width)
-
-    for g in range(groups):
-        at = g * ent_dev
-        proj = dot(rows_of(feats, g), theta[...])
-        part = (es(at, ent_dev) * proj).astype(BF)
-        values[at : at + ent_dev, :] = part
-        values[ents + at : ents + at + ent_dev, :] = part
-    for g in range(groups):
-        at = g * ent_dev
-        preact = es(at, ent_dev) * dot(full[at : at + ent_dev, :], values[...])
+    square(other, rest)
+
+    def es(at, rows):
+        return jnp.concatenate([scale[at : at + rows, :]] * (width // 128), axis=1)
+
+    def product(value, at, rows):
+        return dot(full[at : at + rows, :], value[...]) + dot(rest[at : at + rows, :], value[...])
+
+    every = feats[...].reshape(ents, width)
+    for at in range(0, ents, TILE):
+        span = slice(at, at + TILE)
+        values[span, :] = (es(at, TILE) * dot(every[span, :], theta[...])).astype(BF)
+    for at in range(0, ents, TILE):
+        span = slice(at, at + TILE)
+        preact = es(at, TILE) * product(values, at, TILE)
         gate = jax.nn.sigmoid(preact)
-        acts[at : at + ent_dev, :] = (preact * gate).astype(BF)
-        grad = rows_of(cots, g).astype(F32) * gate * (1.0 + preact * (1.0 - gate))
-        part = (es(at, ent_dev) * grad).astype(BF)
-        backs[at : at + ent_dev, :] = part
-        backs[ents + at : ents + at + ent_dev, :] = part
+        acts[span, :] = (preact * gate).astype(BF)
+        cot = cots[at // ent_dev * per_group : (at + TILE) // ent_dev * per_group].reshape(TILE, width).astype(F32)
+        grad = cot * gate * (1.0 + preact * (1.0 - gate))
+        backs[span, :] = (es(at, TILE) * grad).astype(BF)
     own_rows = pl.ds(pl.multiple_of(mine * ent_dev, ent_dev), ent_dev)
     activated[...] = acts[own_rows, :]
-    total = jnp.zeros((width, width), F32)
-    for g in range(groups):
-        at = g * ent_dev
-        part = (es(at, ent_dev) * dot(full[at : at + ent_dev, :], backs[...])).astype(BF)
-        projs[at : at + ent_dev, :] = part
-        total = total + dot(rows_of(feats, g), part, TN)
-    grad_theta[...] = total
-    grad_features[...] = dot(projs[own_rows, :], theta[...], NT).astype(BF)
+    for at in range(0, ents, TILE):
+        acts[at : at + TILE, :] = (es(at, TILE) * product(backs, at, TILE)).astype(BF)
+    grad_theta[...] = dot(every, acts[...], TN)
+    grad_features[...] = dot(acts[own_rows, :], theta[...], NT).astype(BF)
     sections = incidence.shape[0]
-    for q in range(sections // 128):
-        piece = incidence[q * 128 : (q + 1) * 128, :]
-        ahead = dot(piece, values[0:ents, :])
-        back = dot(piece, backs[0:ents, :])
-        sums = column_to_row(jnp.sum(ahead * back, axis=1, keepdims=True))
-        lanes = slice(q * 128, (q + 1) * 128)
-        grad_weight[:, lanes] = sums * inverse[:, lanes]
+    for q in range(0, sections, TILE):
+        piece = incidence[q : q + TILE, :]
+        both = dot(piece, values[...]) * dot(piece, backs[...])
+        total = jnp.sum(both, axis=1, keepdims=True)
+        grad_weight[:, q : q + TILE] = column_to_row(total) * inverse[:, q : q + TILE]
 
 
 def dense_body(features, theta, section_weight, pair_rows, pair_cols, pair_counts, cotangent):
@@ -397,15 +403,14 @@
     share = ent_dev // (lax.axis_size("x") * CORES)
     height = CHUNKS * 16 + 8
     swap = [(0, 1), (1, 0)]
-    payload, shares, inverse = pl.pallas_call(
+    payload, inverse = pl.pallas_call(
         prep_kernel,
         out_shape=(
-            jax.ShapeDtypeStruct((height, 128), BF),
-            jax.ShapeDtypeStruct((layers * group, 2 * share, width), BF),
+            jax.ShapeDtypeStruct((height + 4 * share, 128), BF),
             jax.ShapeDtypeStruct((1, sec_dev), F32),
         ),
         in_specs=[hbm()] * 6,
-        out_specs=(vmem(), hbm(), vmem()),
+        out_specs=(vmem(), vmem()),
         scratch_shapes=[
             pltpu.SMEM((1, blocks), jnp.int32),
             pltpu.VMEM((blocks, slots), jnp.int32),
@@ -413,23 +418,14 @@
             pltpu.VMEM((1, sec_dev), F32),
             pltpu.VMEM((2 * share, width), BF),
             pltpu.SemaphoreType.DMA((6,)),
-            pltpu.SemaphoreType.DMA((layers * group,)),
         ],
         compiler_params=params(63),
         name="prep",
     )(pair_counts, pair_rows, pair_cols, section_weight.reshape(1, sec_dev), features, cotangent)
-    by_x = lax.ppermute(payload, "x", swap)
-    by_y = lax.ppermute(payload, "y", swap)
-    by_both = lax.ppermute(payload, ("y", "x"), [(i, i ^ 3) for i in range(4)])
-    incidence = pl.pallas_call(
-        own_kernel,
-        out_shape=jax.ShapeDtypeStruct((sec_dev, ents), BF),
-        in_specs=[vmem()],
-        out_specs=vmem(),
-        compiler_params=params(),
-        cost_estimate=pl.CostEstimate(flops=2 * sec_dev * ents * slots, bytes_accessed=2**20, transcendentals=0),
-        name="own_incidence",
-    )(payload)
+    def layer(d):
+        return lax.ppermute(payload, "z", [(i, i ^ d) for i in range(layers)])
+
+    by_layer = [layer(d) for d in range(1, layers)]
     held = pl.pallas_call(
         hold_kernel,
         out_shape=jax.ShapeDtypeStruct(payload.shape, BF),
@@ -445,14 +441,14 @@
         out_specs=vmem(),
         compiler_params=params(),
         name="collect",
-    )(held, by_x, by_y, by_both)
-
-    shares, near = lax.optimization_barrier((shares, near))
-
-    def across(d):
-        return lax.ppermute(near, "z", [(i, i ^ d) for i in range(layers)])
-
-    far = [near] + [across(d) for d in range(1, layers)]
+    )(held, *by_layer)
+
+    far = [
+        near,
+        lax.ppermute(near, "x", swap),
+        lax.ppermute(near, "y", swap),
+        lax.ppermute(near, ("y", "x"), [(i, i ^ 3) for i in range(group)]),
+    ]
     rows = column_rows(ents)[-1][1]
     scratch = [pltpu.VMEM((ents, group * sec_dev), BF), pltpu.VMEM((ents + 16, group * sec_dev), BF)]
 
@@ -475,11 +471,22 @@
     third, pair = lax.optimization_barrier((far[2], pair))
     single = step(first_kernel, (rows, TILE), F32, "gram_third", [third])
     fourth, single = lax.optimization_barrier((far[3], single))
-    own = step(last_kernel, (rows - 16 * tiles + 16, TILE), BF, "gram_last", [fourth, pair, single])
+    height = rows - 16 * tiles + 16 + layers * group * 2 * share
+    own = step(last_kernel, (height, TILE), BF, "gram_last", [fourth, pair, single, tuple(far[:2]), third])
     other = lax.ppermute(own, "core", swap)
-    own_share = lax.all_to_all(shares, ("z", "y", "x"), 0, 0, tiled=True)
-    other_share = lax.ppermute(own_share, "core", swap)
-    tail_in = (own, other, own_share, other_share, theta, incidence, inverse)
+    incidence, full = pl.pallas_call(
+        own_kernel,
+        out_shape=(
+            jax.ShapeDtypeStruct((sec_dev, ents), BF),
+            jax.ShapeDtypeStruct((ents, ents), BF),
+        ),
+        in_specs=[vmem(), vmem()],
+        out_specs=(vmem(), vmem()),
+        compiler_params=params(),
+        cost_estimate=pl.CostEstimate(flops=1000000000, bytes_accessed=1000, transcendentals=0),
+        name="own_square",
+    )(payload, own)
+    tail_in = (own, other, full, theta, incidence, inverse)
     activated, grad_features, grad_theta, grad_weight = pl.pallas_call(
         tail_kernel,
         out_shape=(
@@ -491,10 +498,9 @@
         in_specs=[vmem()] * len(tail_in),
         out_specs=(vmem(),) * 4,
         scratch_shapes=[
-            pltpu.VMEM((ents, 2 * ents), BF),
+            pltpu.VMEM((ents, ents), BF),
             pltpu.VMEM((ents, 128), F32),
-            pltpu.VMEM((2 * ents, width), BF),
-            pltpu.VMEM((2 * ents, width), BF),
+            pltpu.VMEM((ents, width), BF),
             pltpu.VMEM((ents, width), BF),
             pltpu.VMEM((ents, width), BF),
             pltpu.VMEM((layers * group, CORES, share, width), BF),

time: 48.4 us -> 42 us (0.87)
  starting transfers between devices: 14.5 us -> 9.38 us
  Pallas kernels: 25.1 us -> 23.5 us
    all_to_all x1 -> x0, starting transfers between devices: 4.98 us -> none  [dense_body(): own_share = lax.all_to_all(shares, ('z', 'y', 'x'), 0, 0, tiled=True)]
    pallas_call x1, Pallas kernels: 5.66 us -> 4.29 us  [dense_body(): pl.pallas_call(tail_kernel, out_shape=(jax.ShapeDtypeStruct((ent_dev, wid...]
    ppermute x1, waiting for transfers between devices: 2.08 us -> 3.2 us  [dense_body(): other = lax.ppermute(own, 'core', swap)]
    ppermute x7 -> x6, waiting for transfers between devices: 4.83 us -> 4.09 us  [the longest x3 3.74 us: layer(): return lax.ppermute(payload, 'z', [(i, i ^ d) for i in range(layers)])]
    ppermute x7 -> x6, starting transfers between devices: 9.49 us -> 9.31 us  [the longest x3 5.76 us: layer(): return lax.ppermute(payload, 'z', [(i, i ^ d) for i in range(layers)])]
  transfers between devices with their start and end apart: 9 -> 7, of which waited for: 4 -> 4; matrix products, arithmetic and copies ran while one was open for 0% -> 0% of each run, Pallas kernels for 35% -> 31%
where the time goes in v4:
time: 42 us; the launch traced here: 41.8 us
  Pallas kernels  23.5 us (56%)
  starting transfers between devices  9.38 us (22%)
  waiting for transfers between devices  7.29 us (17%)
  local copies, waits for them, and re-layouts  0.86 us (2%)
  between operations  0.74 us (2%)
    pallas_call x4, Pallas kernels, step(): pl.pallas_call(kernel, out_shape=jax.ShapeDtypeStruct(shape, kind), in_sp...  16.7 us
    ppermute x3, starting transfers between devices, layer(): return lax.ppermute(payload, 'z', [(i, i ^ d) for i in range(layers)])  5.76 us
    pallas_call x1, Pallas kernels, dense_body(): pl.pallas_call(tail_kernel, out_shape=(jax.ShapeDtypeStruct((ent_dev, wid...  4.29 us
    ppermute x3, waiting for transfers between devices, layer(): return lax.ppermute(payload, 'z', [(i, i ^ d) for i in range(layers)])  3.74 us
    ppermute x1, waiting for transfers between devices, dense_body(): other = lax.ppermute(own, 'core', swap)  3.2 us
    pallas_call x1, Pallas kernels, dense_body(): pl.pallas_call(prep_kernel, out_shape=(jax.ShapeDtypeStruct((height + 4 *...  1.87 us
    ppermute x1, starting transfers between devices, dense_body(): lax.ppermute(near, 'x', swap)  1.56 us
    ppermute x1, starting transfers between devices, dense_body(): lax.ppermute(near, 'y', swap)  1.52 us
  transfers between devices with their start and end apart: 7, of which 4 were waited for; matrix products, arithmetic and copies ran while one was open for 0% of the time, Pallas kernels for 31%

profile of v4, /device:TPU:0, one launch (start us, length us, event | category | flops | bytes accessed | tf_op | source)
XLA Modules:
  0.0 41.8 jit_solution(11254892662702615224)
XLA Ops:
  0.6 1.9 %prep.1 = (bf16[200,128]{1,0:T(8,128)(2,1)}, f32[1,512]{1,0:T(1,128)}) custom-call(s32[1,8]{1,0:T(1,128)} %counts.1, s32[1,8,512]{2,1,0:T(8,128)} %rows.1, s32[1,8,512]{2,1,0:T(8,128)} %cols.1, f32[1,512]{1,0:T(1,128)} %bitcast.2, bf16[128,256]{1,0:T(8,128)(2,1)} %features.1, bf16[128,256]{1,0:T(8,128)(2,1)} %cotangent.1), custom_call_target="tpu_custom_call" | custom-call | tf_op jit(solution)/shard_map/prep/pallas_call | solution.py:406
  2.5 5.1 %collective-permute-start.2 = (bf16[200,128]{1,0:T(8,128)(2,1)}, bf16[200,128]{1,0:T(8,128)(2,1)S(1)}, u32[]{:S(2)}, u32[]{:S(2)}) collective-permute-start(bf16[200,128]{1,0:T(8,128)(2,1)} %get-tuple-element.16.source.payload), channel_id=1, source_target_pairs={{0,24},{8,16},{16,8},{24,0},{1,25},{9,17},{17,9},{25,1},{2,26},{10... | collective-permute-start | bytes 153608 | tf_op jit(solution)/shard_map/ppermute | solution.py:426
  7.6 0.0 collective-permute-start.1
  7.6 0.6 %collective-permute-start = (bf16[200,128]{1,0:T(8,128)(2,1)}, bf16[200,128]{1,0:T(8,128)(2,1)S(1)}, u32[]{:S(2)}, u32[]{:S(2)}) collective-permute-start(bf16[200,128]{1,0:T(8,128)(2,1)} %get-tuple-element.16.source.payload), channel_id=1, source_target_pairs={{0,8},{8,0},{16,24},{24,16},{1,9},{9,1},{17,25},{25,17},{2,10},{10... | collective-permute-start | bytes 153608 | tf_op jit(solution)/shard_map/ppermute | solution.py:426
  8.3 0.0 copy-start.1
  8.3 0.8 %copy-done.1 = bf16[200,128]{1,0:T(8,128)(2,1)S(1)} copy-done((bf16[200,128]{1,0:T(8,128)(2,1)S(1)}, bf16[200,128]{1,0:T(8,128)(2,1)}, u32[]{:S(2)}) %copy-start.1) | copy-done | bytes 51224
  9.1 1.0 %collective-permute-done.2.third = bf16[200,128]{1,0:T(8,128)(2,1)S(1)} collective-permute-done((bf16[200,128]{1,0:T(8,128)(2,1)}, bf16[200,128]{1,0:T(8,128)(2,1)S(1)}, u32[]{:S(2)}, u32[]{:S(2)}) %collective-permute-start.2) | collective-permute-done | bytes 51232 | tf_op jit(solution)/shard_map/ppermute | solution.py:426
  10.1 2.7 %collective-permute-done.1.second = bf16[200,128]{1,0:T(8,128)(2,1)S(1)} collective-permute-done((bf16[200,128]{1,0:T(8,128)(2,1)}, bf16[200,128]{1,0:T(8,128)(2,1)S(1)}, u32[]{:S(2)}, u32[]{:S(2)}) %collective-permute-start.1) | collective-permute-done | bytes 51232 | tf_op jit(solution)/shard_map/ppermute | solution.py:426
  12.9 0.0 collective-permute-done.first
  12.9 1.6 %collective-permute-start.5 = (bf16[4,200,128]{2,1,0:T(8,128)(2,1)S(1)}, bf16[4,200,128]{2,1,0:T(8,128)(2,1)S(1)}, u32[]{:S(2)}, u32[]{:S(2)}) collective-permute-start(bf16[4,200,128]{2,1,0:T(8,128)(2,1)S(1)} %collect.1.lists.near_0_), channel_id=1, source_target_pairs={{0,2},{2,0},{1,3},{3,1},{4,6},{6,4},{5,7},{7,5},{8,10},{10,8},{9,1... | collective-permute-start | bytes 614408 | tf_op jit(solution)/shard_map/ppermute | solution.py:448
  14.4 1.5 %collective-permute-start.4 = (bf16[4,200,128]{2,1,0:T(8,128)(2,1)S(1)}, bf16[4,200,128]{2,1,0:T(8,128)(2,1)S(1)}, u32[]{:S(2)}, u32[]{:S(2)}) collective-permute-start(bf16[4,200,128]{2,1,0:T(8,128)(2,1)S(1)} %collect.1.lists.near_0_), channel_id=1, source_target_pairs={{0,4},{4,0},{1,5},{5,1},{2,6},{6,2},{3,7},{7,3},{8,12},{12,8},{9,1... | collective-permute-start | bytes 614408 | tf_op jit(solution)/shard_map/ppermute | solution.py:449
  16.0 0.5 %collective-permute-start.3 = (bf16[4,200,128]{2,1,0:T(8,128)(2,1)S(1)}, bf16[4,200,128]{2,1,0:T(8,128)(2,1)S(1)}, u32[]{:S(2)}, u32[]{:S(2)}) collective-permute-start(bf16[4,200,128]{2,1,0:T(8,128)(2,1)S(1)} %collect.1.lists.near_0_), channel_id=1, source_target_pairs={{0,6},{2,4},{4,2},{6,0},{1,7},{3,5},{5,3},{7,1},{8,14},{10,12},{12... | collective-permute-start | bytes 614408 | tf_op jit(solution)/shard_map/ppermute | solution.py:450
  16.4 4.1 %gram_first.1.before = f32[2624,256]{1,0:T(8,128)S(1)} custom-call(bf16[4,200,128]{2,1,0:T(8,128)(2,1)S(1)} %collect.1.lists.near_0_), custom_call_target="tpu_custom_call" | custom-call | flops 1000000000 | bytes 1000 | tf_op jit(solution)/shard_map/gram_first/pallas_call | solution.py:456
  20.5 0.4 collective-permute-done.5.lists.near_1_
  20.9 4.1 %gram_second.1.pair = f32[2624,256]{1,0:T(8,128)S(1)} custom-call(bf16[4,200,128]{2,1,0:T(8,128)(2,1)S(1)} %collective-permute-done.5.lists.near_1_, f32[2624,256]{1,0:T(8,128)S(1)} %gram_first.1.before), custom_call_target="tpu_custom_call" | custom-call | flops 1000000000 | bytes 1000 | tf_op jit(solution)/shard_map/gram_second/pallas_call | solution.py:456
  25.0 0.0 collective-permute-done.4.lists.third
  25.0 4.1 %gram_third.1.single = f32[2624,256]{1,0:T(8,128)S(1)} custom-call(bf16[4,200,128]{2,1,0:T(8,128)(2,1)S(1)} %collective-permute-done.4.lists.third), custom_call_target="tpu_custom_call" | custom-call | flops 1000000000 | bytes 1000 | tf_op jit(solution)/shard_map/gram_third/pallas_call | solution.py:456
  29.1 0.0 copy-start.2
  29.2 0.0 collective-permute-done.3.lists
  29.2 4.4 %gram_last.1.gram.own = bf16[3600,256]{1,0:T(8,128)(2,1)S(1)} custom-call(bf16[4,200,128]{2,1,0:T(8,128)(2,1)S(1)} %collective-permute-done.3.lists, f32[2624,256]{1,0:T(8,128)S(1)} %gram_second.1.pair, f32[2624,256]{1,0:T(8,128)S(1)} %gram_third.1.single, bf16[4,200,128]{2,1,0:T(8,128)(2,1)S(1)} %collect.1.lists.near_0_, ...), custom_call_target="tpu_custom_call" | custom-call | flops 1000000000 | bytes 1000 | tf_op jit(solution)/shard_map/gram_last/pallas_call | solution.py:456
  33.6 0.0 copy-start
  33.6 0.0 copy-start.3
  33.6 0.1 collective-permute-start.6
  33.7 0.0 copy-done.2
  33.7 0.6 %own_square.1 = (bf16[512,1024]{1,0:T(8,128)(2,1)S(1)}, bf16[1024,1024]{1,0:T(8,128)(2,1)S(1)}) custom-call(bf16[200,128]{1,0:T(8,128)(2,1)S(1)} %copy-done.2, bf16[3600,256]{1,0:T(8,128)(2,1)S(1)} %gram_last.1.gram.own), custom_call_target="tpu_custom_call" | custom-call | flops 1000000000 | bytes 1000 | tf_op jit(solution)/shard_map/own_square/pallas_call | solution.py:477
  34.3 3.2 %collective-permute-done.6.other = bf16[3600,256]{1,0:T(8,128)(2,1)S(1)} collective-permute-done((bf16[3600,256]{1,0:T(8,128)(2,1)S(1)}, bf16[3600,256]{1,0:T(8,128)(2,1)S(1)}, u32[]{:S(2)}, u32[]{:S(2)}) %collective-permute-start.6) | collective-permute-done | bytes 1843232 | tf_op jit(solution)/shard_map/ppermute | solution.py:476
  37.5 0.0 copy-done
  37.5 0.0 copy-done.3
  37.5 4.3 %tail.1 = (bf16[128,256]{1,0:T(8,128)(2,1)}, bf16[128,256]{1,0:T(8,128)(2,1)}, f32[256,256]{1,0:T(8,128)}, f32[1,512]{1,0:T(1,128)}) custom-call(bf16[3600,256]{1,0:T(8,128)(2,1)S(1)} %gram_last.1.gram.own, bf16[3600,256]{1,0:T(8,128)(2,1)S(1)} %collective-permute-done.6.other, bf16[1024,1024]{1,0:T(8,128)(2,1)S(1)} %get-tuple-element.21.full, ...), custom_call_target="tpu_custom_call" | custom-call | tf_op jit(solution)/shard_map/tail/pallas_call | solution.py:490
  (2 shorter events, 0.0 us)
Async XLA Ops:
  2.5 7.6 %collective-permute-start.2 = (bf16[200,128]{1,0:T(8,128)(2,1)}, bf16[200,128]{1,0:T(8,128)(2,1)S(1)}, u32[]{:S(2)}, u32[]{:S(2)}) collective-permute-start(bf16[200,128]{1,0:T(8,128)(2,1)} %get-tuple-element.16.source.payload), channel_id=1, source_target_pairs={{0,24},{8,16},{16,8},{24,0},{1,25},{9,17},{17,9},{25,1},{2,26},{10... | collective-permute-start | bytes 153608 | tf_op jit(solution)/shard_map/ppermute | solution.py:426
  7.6 5.2 %collective-permute-start.1 = (bf16[200,128]{1,0:T(8,128)(2,1)}, bf16[200,128]{1,0:T(8,128)(2,1)S(1)}, u32[]{:S(2)}, u32[]{:S(2)}) collective-permute-start(bf16[200,128]{1,0:T(8,128)(2,1)} %get-tuple-element.16.source.payload), channel_id=1, source_target_pairs={{0,16},{8,24},{16,0},{24,8},{1,17},{9,25},{17,1},{25,9},{2,18},{10... | collective-permute-start | bytes 153608 | tf_op jit(solution)/shard_map/ppermute | solution.py:426
  7.6 5.2 %collective-permute-start = (bf16[200,128]{1,0:T(8,128)(2,1)}, bf16[200,128]{1,0:T(8,128)(2,1)S(1)}, u32[]{:S(2)}, u32[]{:S(2)}) collective-permute-start(bf16[200,128]{1,0:T(8,128)(2,1)} %get-tuple-element.16.source.payload), channel_id=1, source_target_pairs={{0,8},{8,0},{16,24},{24,16},{1,9},{9,1},{17,25},{25,17},{2,10},{10... | collective-permute-start | bytes 153608 | tf_op jit(solution)/shard_map/ppermute | solution.py:426
  8.3 0.8 %copy-start.1 = (bf16[200,128]{1,0:T(8,128)(2,1)S(1)}, bf16[200,128]{1,0:T(8,128)(2,1)}, u32[]{:S(2)}) copy-start(bf16[200,128]{1,0:T(8,128)(2,1)} %get-tuple-element.16.source.payload) | copy-start | bytes 153604
  12.9 8.0 %collective-permute-start.5 = (bf16[4,200,128]{2,1,0:T(8,128)(2,1)S(1)}, bf16[4,200,128]{2,1,0:T(8,128)(2,1)S(1)}, u32[]{:S(2)}, u32[]{:S(2)}) collective-permute-start(bf16[4,200,128]{2,1,0:T(8,128)(2,1)S(1)} %collect.1.lists.near_0_), channel_id=1, source_target_pairs={{0,2},{2,0},{1,3},{3,1},{4,6},{6,4},{5,7},{7,5},{8,10},{10,8},{9,1... | collective-permute-start | bytes 614408 | tf_op jit(solution)/shard_map/ppermute | solution.py:448
  14.4 10.6 %collective-permute-start.4 = (bf16[4,200,128]{2,1,0:T(8,128)(2,1)S(1)}, bf16[4,200,128]{2,1,0:T(8,128)(2,1)S(1)}, u32[]{:S(2)}, u32[]{:S(2)}) collective-permute-start(bf16[4,200,128]{2,1,0:T(8,128)(2,1)S(1)} %collect.1.lists.near_0_), channel_id=1, source_target_pairs={{0,4},{4,0},{1,5},{5,1},{2,6},{6,2},{3,7},{7,3},{8,12},{12,8},{9,1... | collective-permute-start | bytes 614408 | tf_op jit(solution)/shard_map/ppermute | solution.py:449
  16.0 13.2 %collective-permute-start.3 = (bf16[4,200,128]{2,1,0:T(8,128)(2,1)S(1)}, bf16[4,200,128]{2,1,0:T(8,128)(2,1)S(1)}, u32[]{:S(2)}, u32[]{:S(2)}) collective-permute-start(bf16[4,200,128]{2,1,0:T(8,128)(2,1)S(1)} %collect.1.lists.near_0_), channel_id=1, source_target_pairs={{0,6},{2,4},{4,2},{6,0},{1,7},{3,5},{5,3},{7,1},{8,14},{10,12},{12... | collective-permute-start | bytes 614408 | tf_op jit(solution)/shard_map/ppermute | solution.py:450
  29.1 4.5 %copy-start.2 = (bf16[200,128]{1,0:T(8,128)(2,1)S(1)}, bf16[200,128]{1,0:T(8,128)(2,1)}, u32[]{:S(2)}) copy-start(bf16[200,128]{1,0:T(8,128)(2,1)} %get-tuple-element.16.source.payload) | copy-start | bytes 153604
  33.6 3.9 %copy-start = (bf16[256,256]{1,0:T(8,128)(2,1)S(1)}, bf16[256,256]{1,0:T(8,128)(2,1)}, u32[]{:S(2)}) copy-start(bf16[256,256]{1,0:T(8,128)(2,1)} %theta.1) | copy-start | bytes 393220
  33.6 3.9 %copy-start.3 = (f32[1,512]{1,0:T(1,128)S(1)}, f32[1,512]{1,0:T(1,128)}, u32[]{:S(2)}) copy-start(f32[1,512]{1,0:T(1,128)} %get-tuple-element.23.inverse) | copy-start | bytes 6148
  33.6 3.9 %collective-permute-start.6 = (bf16[3600,256]{1,0:T(8,128)(2,1)S(1)}, bf16[3600,256]{1,0:T(8,128)(2,1)S(1)}, u32[]{:S(2)}, u32[]{:S(2)}) collective-permute-start(bf16[3600,256]{1,0:T(8,128)(2,1)S(1)} %gram_last.1.gram.own), channel_id=1, source_target_pairs={{0,1},{1,0},{2,3},{3,2},{4,5},{5,4},{6,7},{7,6},{8,9},{9,8},{10,11... | collective-permute-start | bytes 5529608 | tf_op jit(solution)/shard_map/ppermute | solution.py:476

commit v5 on v4

--- a/solution.py
+++ b/solution.py
@@ -221,29 +221,45 @@
     target[...] = source[...]
 
 
-def square(gram, full):
+def square(firsts, others, full):
     ents = full.shape[0]
     start = 0
     for b in range(0, ents, TILE):
         for a in range(b, ents, TILE):
-            piece = gram[start : start + TILE, :]
+            refs, at = (firsts, a) if b == 0 else (others, start)
+            parts = [ref[at : at + TILE, :].astype(F32) for ref in refs]
+            piece = (parts[0] + parts[1]).astype(BF)
             full[a : a + TILE, b : b + TILE] = piece
             if a != b:
                 full[b : b + TILE, a : a + TILE] = piece.T
-            start += TILE
-
-
-def own_kernel(payload, gram, incidence, full):
+            start += TILE if b else 0
+
+
+def middle_kernel(payload, own_first, other_first, theta, incidence, feats, cots, projected):
     ents = incidence.shape[1]
     ent_dev = TILE // (incidence.shape[0] // TILE)
     chunks = CHUNKS
+    share = feats.shape[2]
+    core = lax.axis_index("core")
+    columns = lax.axis_size("y") * lax.axis_size("x")
+    column_here = lax.axis_index("y") * 2 + lax.axis_index("x")
+    for n, source in enumerate((own_first, other_first)):
+        which = core if n == 0 else 1 - core
+        at = ents
+        for d in range(columns):
+            there = jnp.bitwise_xor(column_here, d)
+            for q in range(feats.shape[0] // columns):
+                feats[q * columns + there, which] = source[at : at + share, :]
+                cots[q * columns + there, which] = source[at + share : at + 2 * share, :]
+                at += 2 * share
     for j in range(ents // ent_dev):
         block = dot(index_hot(payload, 8 + j, chunks), index_hot(payload, j, chunks), NT).astype(BF)
         for half in range(2):
             incidence[half * TILE : (half + 1) * TILE, j * ent_dev : (j + 1) * ent_dev] = block[
                 :, half * ent_dev : (half + 1) * ent_dev
             ]
-    square(gram, full)
+    every = feats[...].reshape(ents, theta.shape[0])
+    projected[...] = dot(every, theta[...])
 
 
 def collect_kernel(own, first, second, third, group):
@@ -299,23 +315,12 @@
         sums[start:end, :] = before[start:end, :] + column(b, table, scaled)
 
 
-def last_kernel(lists, pair, single, near, third, gram, table, scaled):
+def last_kernel(lists, pair, single, near, third, first, table, scaled):
     ents = table.shape[0]
-    spans = column_rows(ents)
     fill(lists, table, scaled)
-    at = 0
-    degrees = []
-    for b, (start, end) in enumerate(spans):
-        size = end - start - 16
-        total = pair[start:end, :] + (single[start:end, :] + column(b, table, scaled))
-        gram[at : at + size, :] = total[0:size].astype(BF)
-        at += size
-        degree = total[size : size + 1]
-        top = degree.astype(BF).astype(F32)
-        degrees += [top, degree - top]
-    degrees.append(jnp.zeros((16 - 2 * len(spans), TILE), F32))
-    gram[at : at + 16, :] = jnp.concatenate(degrees, axis=0).astype(BF)
-    at += 16
+    total = pair[0:ents, :] + (single[0:ents, :] + dot(scaled[0:ents, :], table[0:TILE, :], NT))
+    first[0:ents, :] = total.astype(BF)
+    at = ents
     for source in near + (third, lists):
         shards, height, _ = source.shape
         top = 16 * CHUNKS + 8
@@ -323,53 +328,61 @@
         for q in range(shards):
             for k in range(4):
                 rows = slice(at + k // 2 * share, at + (k // 2 + 1) * share)
-                gram[rows, k % 2 * 128 : k % 2 * 128 + 128] = source[q, top + k * share : top + (k + 1) * share, :]
+                first[rows, k % 2 * 128 : k % 2 * 128 + 128] = source[q, top + k * share : top + (k + 1) * share, :]
             at += 2 * share
 
 
+def others_kernel(table, scaled, pair, single, others):
+    ents = table.shape[0]
+    at = 0
+    degrees = []
+    for b, (start, end) in enumerate(column_rows(ents)):
+        size = end - start - 16
+        if b == 0:
+            start, size = end - 16, 0
+            product = dot(scaled[ents:, :], table[0:TILE, :], NT)
+        else:
+            product = column(b, table, scaled)
+        total = pair[start:end, :] + (single[start:end, :] + product)
+        if b:
+            others[at : at + size, :] = total[0:size].astype(BF)
+        at += size
+        degree = total[size : size + 1]
+        top = degree.astype(BF).astype(F32)
+        degrees += [top, degree - top]
+    degrees.append(jnp.zeros((16 - len(degrees), TILE), F32))
+    others[at : at + 16, :] = jnp.concatenate(degrees, axis=0).astype(BF)
+
+
 def tail_kernel(
-    own, other, full, theta, incidence, inverse,
+    own_first, own_others, other_first, other_others, feats, cots, projected, theta, incidence, inverse,
     activated, grad_features, grad_theta, grad_weight,
-    rest, scale, values, backs, acts, feats, cots,
+    full, scale, values, backs, acts,
 ):
     ents = full.shape[0]
     tiles = ents // TILE
     ent_dev = activated.shape[0]
     width = theta.shape[0]
-    share = feats.shape[2]
     per_group = feats.shape[0] // (ents // ent_dev)
-    core = lax.axis_index("core")
     mine = lax.axis_index("z") * 2 + lax.axis_index("y")
-    base = sum(ents - b * TILE for b in range(tiles))
-    columns = lax.axis_size("y") * lax.axis_size("x")
-    column_here = lax.axis_index("y") * 2 + lax.axis_index("x")
-    for n, source in enumerate((own, other)):
-        which = core if n == 0 else 1 - core
-        at = base + 16
-        for d in range(columns):
-            there = jnp.bitwise_xor(column_here, d)
-            for q in range(feats.shape[0] // columns):
-                feats[q * columns + there, which] = source[at : at + share, :]
-                cots[q * columns + there, which] = source[at + share : at + 2 * share, :]
-                at += 2 * share
-    degree_rows = own[base : base + 16, :].astype(F32) + other[base : base + 16, :].astype(F32)
+    base = own_others.shape[0] - 16
+    degree_rows = own_others[base:, :].astype(F32) + other_others[base:, :].astype(F32)
     for b in range(tiles):
         row = lax.rsqrt(1.0 + (degree_rows[2 * b : 2 * b + 1] + degree_rows[2 * b + 1 : 2 * b + 2]))
         for h in range(TILE // 128):
             at = b * TILE + h * 128
             scale[at : at + 128, :] = row_to_column(row[:, h * 128 : (h + 1) * 128])
-    square(other, rest)
+    square((own_first, other_first), (own_others, other_others), full)
 
     def es(at, rows):
         return jnp.concatenate([scale[at : at + rows, :]] * (width // 128), axis=1)
 
     def product(value, at, rows):
-        return dot(full[at : at + rows, :], value[...]) + dot(rest[at : at + rows, :], value[...])
-
-    every = feats[...].reshape(ents, width)
+        return dot(full[at : at + rows, :], value[...])
+
     for at in range(0, ents, TILE):
         span = slice(at, at + TILE)
-        values[span, :] = (es(at, TILE) * dot(every[span, :], theta[...])).astype(BF)
+        values[span, :] = (es(at, TILE) * projected[span, :]).astype(BF)
     for at in range(0, ents, TILE):
         span = slice(at, at + TILE)
         preact = es(at, TILE) * product(values, at, TILE)
@@ -382,7 +395,7 @@
     activated[...] = acts[own_rows, :]
     for at in range(0, ents, TILE):
         acts[at : at + TILE, :] = (es(at, TILE) * product(backs, at, TILE)).astype(BF)
-    grad_theta[...] = dot(every, acts[...], TN)
+    grad_theta[...] = dot(feats[...].reshape(ents, width), acts[...], TN)
     grad_features[...] = dot(acts[own_rows, :], theta[...], NT).astype(BF)
     sections = incidence.shape[0]
     for q in range(0, sections, TILE):
@@ -471,22 +484,40 @@
     third, pair = lax.optimization_barrier((far[2], pair))
     single = step(first_kernel, (rows, TILE), F32, "gram_third", [third])
     fourth, single = lax.optimization_barrier((far[3], single))
-    height = rows - 16 * tiles + 16 + layers * group * 2 * share
-    own = step(last_kernel, (height, TILE), BF, "gram_last", [fourth, pair, single, tuple(far[:2]), third])
-    other = lax.ppermute(own, "core", swap)
-    incidence, full = pl.pallas_call(
-        own_kernel,
-        out_shape=(
-            jax.ShapeDtypeStruct((sec_dev, ents), BF),
-            jax.ShapeDtypeStruct((ents, ents), BF),
-        ),
-        in_specs=[vmem(), vmem()],
-        out_specs=(vmem(), vmem()),
-        compiler_params=params(),
-        cost_estimate=pl.CostEstimate(flops=1000000000, bytes_accessed=1000, transcendentals=0),
-        name="own_square",
-    )(payload, own)
-    tail_in = (own, other, full, theta, incidence, inverse)
+    def plain(kernel, outs, name, inputs):
+        return pl.pallas_call(
+            kernel,
+            out_shape=[jax.ShapeDtypeStruct(shape, kind) for shape, kind in outs],
+            in_specs=jax.tree.map(lambda _: vmem(), list(inputs)),
+            out_specs=[vmem()] * len(outs),
+            compiler_params=params(),
+            cost_estimate=pl.CostEstimate(flops=1000000000, bytes_accessed=1000, transcendentals=0),
+            name=name,
+        )(*inputs)
+
+    own_first, table, scaled = plain(
+        last_kernel,
+        [
+            ((ents + layers * group * 2 * share, TILE), BF),
+            ((ents, group * sec_dev), BF),
+            ((ents + 16, group * sec_dev), BF),
+        ],
+        "gram_last",
+        [fourth, pair, single, tuple(far[:2]), third],
+    )
+    other_first = lax.ppermute(own_first, "core", swap)
+    (own_others,) = plain(
+        others_kernel, [((rows - 16 * tiles - ents + 16, TILE), BF)], "gram_others", [table, scaled, pair, single]
+    )
+    other_others = lax.ppermute(own_others, "core", swap)
+    stack = (layers * group, CORES, share, width)
+    incidence, feats, cots, projected = plain(
+        middle_kernel,
+        [((sec_dev, ents), BF), (stack, BF), (stack, BF), ((ents, width), F32)],
+        "middle",
+        [payload, own_first, other_first, theta],
+    )
+    tail_in = (own_first, own_others, other_first, other_others, feats, cots, projected, theta, incidence, inverse)
     activated, grad_features, grad_theta, grad_weight = pl.pallas_call(
         tail_kernel,
         out_shape=(
@@ -503,8 +534,6 @@
             pltpu.VMEM((ents, width), BF),
             pltpu.VMEM((ents, width), BF),
             pltpu.VMEM((ents, width), BF),
-            pltpu.VMEM((layers * group, CORES, share, width), BF),
-            pltpu.VMEM((layers * group, CORES, share, width), BF),
         ],
         compiler_params=params(),
         name="tail",

time: 42 us -> 40.5 us (0.964)
  waiting for transfers between devices: 7.29 us -> 5.35 us
  starting transfers between devices: 9.38 us -> 9.93 us
    pallas_call x1 -> x3, Pallas kernels: 0.57 us -> 5.95 us  [plain(): pl.pallas_call(kernel, out_shape=[jax.ShapeDtypeStruct(shape, kind) for s...]
    pallas_call x4 -> x3, Pallas kernels: 16.7 us -> 12.3 us  [step(): pl.pallas_call(kernel, out_shape=jax.ShapeDtypeStruct(shape, kind), in_sp...]
    ppermute x1 -> x2, waiting for transfers between devices: 3.2 us -> 1.25 us  [the longest x1 1.25 us: dense_body(): other_others = lax.ppermute(own_others, 'core', swap)]
    pallas_call x1, Pallas kernels: 4.29 us -> 3.23 us  [dense_body(): pl.pallas_call(tail_kernel, out_shape=(jax.ShapeDtypeStruct((ent_dev, wid...]
    ppermute x1 -> x2, starting transfers between devices: 0.07 us -> 0.62 us  [the longest x1 0.55 us: dense_body(): other_others = lax.ppermute(own_others, 'core', swap)]
    unnamed x8 -> x6, local copies, waits for them, and re-layouts: 0.86 us -> 0.85 us
  transfers between devices with their start and end apart: 7 -> 8, of which waited for: 4 -> 4; matrix products, arithmetic and copies ran while one was open for 0% -> 0% of each run, Pallas kernels for 31% -> 38%
where the time goes in v5:
time: 40.5 us; the launch traced here: 40.3 us
  Pallas kernels  23.4 us (58%)
  starting transfers between devices  9.93 us (25%)
  waiting for transfers between devices  5.35 us (13%)
  local copies, waits for them, and re-layouts  0.85 us (2%)
  between operations  0.73 us (2%)
    pallas_call x3, Pallas kernels, step(): pl.pallas_call(kernel, out_shape=jax.ShapeDtypeStruct(shape, kind), in_sp...  12.3 us
    pallas_call x3, Pallas kernels, plain(): pl.pallas_call(kernel, out_shape=[jax.ShapeDtypeStruct(shape, kind) for s...  5.95 us
    ppermute x3, starting transfers between devices, layer(): return lax.ppermute(payload, 'z', [(i, i ^ d) for i in range(layers)])  5.76 us
    ppermute x3, waiting for transfers between devices, layer(): return lax.ppermute(payload, 'z', [(i, i ^ d) for i in range(layers)])  3.74 us
    pallas_call x1, Pallas kernels, dense_body(): pl.pallas_call(tail_kernel, out_shape=(jax.ShapeDtypeStruct((ent_dev, wid...  3.23 us
    pallas_call x1, Pallas kernels, dense_body(): pl.pallas_call(prep_kernel, out_shape=(jax.ShapeDtypeStruct((height + 4 *...  1.87 us
    ppermute x1, starting transfers between devices, dense_body(): lax.ppermute(near, 'x', swap)  1.56 us
    ppermute x1, starting transfers between devices, dense_body(): lax.ppermute(near, 'y', swap)  1.52 us
  transfers between devices with their start and end apart: 8, of which 4 were waited for; matrix products, arithmetic and copies ran while one was open for 0% of the time, Pallas kernels for 38%

profile of v5, /device:TPU:0, one launch (start us, length us, event | category | flops | bytes accessed | tf_op | source)
XLA Modules:
  0.0 40.3 jit_solution(11772576227737223878)
XLA Ops:
  0.6 1.9 %prep.1 = (bf16[200,128]{1,0:T(8,128)(2,1)}, f32[1,512]{1,0:T(1,128)}) custom-call(s32[1,8]{1,0:T(1,128)} %counts.1, s32[1,8,512]{2,1,0:T(8,128)} %rows.1, s32[1,8,512]{2,1,0:T(8,128)} %cols.1, f32[1,512]{1,0:T(1,128)} %bitcast.2, bf16[128,256]{1,0:T(8,128)(2,1)} %features.1, bf16[128,256]{1,0:T(8,128)(2,1)} %cotangent.1), custom_call_target="tpu_custom_call" | custom-call | tf_op jit(solution)/shard_map/prep/pallas_call | solution.py:419
  2.5 5.1 %collective-permute-start.2 = (bf16[200,128]{1,0:T(8,128)(2,1)}, bf16[200,128]{1,0:T(8,128)(2,1)S(1)}, u32[]{:S(2)}, u32[]{:S(2)}) collective-permute-start(bf16[200,128]{1,0:T(8,128)(2,1)} %get-tuple-element.21.source.payload), channel_id=1, source_target_pairs={{0,24},{8,16},{16,8},{24,0},{1,25},{9,17},{17,9},{25,1},{2,26},{10... | collective-permute-start | bytes 153608 | tf_op jit(solution)/shard_map/ppermute | solution.py:439
  7.6 0.0 collective-permute-start.1
  7.6 0.6 %collective-permute-start = (bf16[200,128]{1,0:T(8,128)(2,1)}, bf16[200,128]{1,0:T(8,128)(2,1)S(1)}, u32[]{:S(2)}, u32[]{:S(2)}) collective-permute-start(bf16[200,128]{1,0:T(8,128)(2,1)} %get-tuple-element.21.source.payload), channel_id=1, source_target_pairs={{0,8},{8,0},{16,24},{24,16},{1,9},{9,1},{17,25},{25,17},{2,10},{10... | collective-permute-start | bytes 153608 | tf_op jit(solution)/shard_map/ppermute | solution.py:439
  8.3 0.0 copy-start.1
  8.3 0.8 %copy-done.1 = bf16[200,128]{1,0:T(8,128)(2,1)S(1)} copy-done((bf16[200,128]{1,0:T(8,128)(2,1)S(1)}, bf16[200,128]{1,0:T(8,128)(2,1)}, u32[]{:S(2)}) %copy-start.1) | copy-done | bytes 51224
  9.1 1.0 %collective-permute-done.2.third = bf16[200,128]{1,0:T(8,128)(2,1)S(1)} collective-permute-done((bf16[200,128]{1,0:T(8,128)(2,1)}, bf16[200,128]{1,0:T(8,128)(2,1)S(1)}, u32[]{:S(2)}, u32[]{:S(2)}) %collective-permute-start.2) | collective-permute-done | bytes 51232 | tf_op jit(solution)/shard_map/ppermute | solution.py:439
  10.1 2.7 %collective-permute-done.1.second = bf16[200,128]{1,0:T(8,128)(2,1)S(1)} collective-permute-done((bf16[200,128]{1,0:T(8,128)(2,1)}, bf16[200,128]{1,0:T(8,128)(2,1)S(1)}, u32[]{:S(2)}, u32[]{:S(2)}) %collective-permute-start.1) | collective-permute-done | bytes 51232 | tf_op jit(solution)/shard_map/ppermute | solution.py:439
  12.8 0.0 collective-permute-done.first
  12.9 1.6 %collective-permute-start.5 = (bf16[4,200,128]{2,1,0:T(8,128)(2,1)S(1)}, bf16[4,200,128]{2,1,0:T(8,128)(2,1)S(1)}, u32[]{:S(2)}, u32[]{:S(2)}) collective-permute-start(bf16[4,200,128]{2,1,0:T(8,128)(2,1)S(1)} %collect.1.lists.near_0_), channel_id=1, source_target_pairs={{0,2},{2,0},{1,3},{3,1},{4,6},{6,4},{5,7},{7,5},{8,10},{10,8},{9,1... | collective-permute-start | bytes 614408 | tf_op jit(solution)/shard_map/ppermute | solution.py:461
  14.4 1.5 %collective-permute-start.4 = (bf16[4,200,128]{2,1,0:T(8,128)(2,1)S(1)}, bf16[4,200,128]{2,1,0:T(8,128)(2,1)S(1)}, u32[]{:S(2)}, u32[]{:S(2)}) collective-permute-start(bf16[4,200,128]{2,1,0:T(8,128)(2,1)S(1)} %collect.1.lists.near_0_), channel_id=1, source_target_pairs={{0,4},{4,0},{1,5},{5,1},{2,6},{6,2},{3,7},{7,3},{8,12},{12,8},{9,1... | collective-permute-start | bytes 614408 | tf_op jit(solution)/shard_map/ppermute | solution.py:462
  16.0 0.5 %collective-permute-start.3 = (bf16[4,200,128]{2,1,0:T(8,128)(2,1)S(1)}, bf16[4,200,128]{2,1,0:T(8,128)(2,1)S(1)}, u32[]{:S(2)}, u32[]{:S(2)}) collective-permute-start(bf16[4,200,128]{2,1,0:T(8,128)(2,1)S(1)} %collect.1.lists.near_0_), channel_id=1, source_target_pairs={{0,6},{2,4},{4,2},{6,0},{1,7},{3,5},{5,3},{7,1},{8,14},{10,12},{12... | collective-permute-start | bytes 614408 | tf_op jit(solution)/shard_map/ppermute | solution.py:463
  16.4 4.1 %gram_first.1.before = f32[2624,256]{1,0:T(8,128)S(1)} custom-call(bf16[4,200,128]{2,1,0:T(8,128)(2,1)S(1)} %collect.1.lists.near_0_), custom_call_target="tpu_custom_call" | custom-call | flops 1000000000 | bytes 1000 | tf_op jit(solution)/shard_map/gram_first/pallas_call | solution.py:469
  20.5 0.3 collective-permute-done.5.lists.near_1_
  20.9 4.1 %gram_second.1.pair = f32[2624,256]{1,0:T(8,128)S(1)} custom-call(bf16[4,200,128]{2,1,0:T(8,128)(2,1)S(1)} %collective-permute-done.5.lists.near_1_, f32[2624,256]{1,0:T(8,128)S(1)} %gram_first.1.before), custom_call_target="tpu_custom_call" | custom-call | flops 1000000000 | bytes 1000 | tf_op jit(solution)/shard_map/gram_second/pallas_call | solution.py:469
  25.0 0.0 collective-permute-done.4.lists.third
  25.0 4.1 %gram_third.1.single = f32[2624,256]{1,0:T(8,128)S(1)} custom-call(bf16[4,200,128]{2,1,0:T(8,128)(2,1)S(1)} %collective-permute-done.4.lists.third), custom_call_target="tpu_custom_call" | custom-call | flops 1000000000 | bytes 1000 | tf_op jit(solution)/shard_map/gram_third/pallas_call | solution.py:469
  29.2 0.0 collective-permute-done.3.lists
  29.2 3.1 %gram_last.1 = (bf16[2048,256]{1,0:T(8,128)(2,1)S(1)}, bf16[1024,2048]{1,0:T(8,128)(2,1)S(1)}, bf16[1040,2048]{1,0:T(8,128)(2,1)S(1)}) custom-call(bf16[4,200,128]{2,1,0:T(8,128)(2,1)S(1)} %collective-permute-done.3.lists, f32[2624,256]{1,0:T(8,128)S(1)} %gram_second.1.pair, f32[2624,256]{1,0:T(8,128)S(1)} %gram_third.1.single, ...), custom_call_target="tpu_custom_call" | custom-call | flops 1000000000 | bytes 1000 | tf_op jit(solution)/shard_map/gram_last/pallas_call | solution.py:488
  32.3 0.1 collective-permute-start.6
  32.4 0.0 copy-start
  32.4 2.2 %gram_others.1.own_others = bf16[1552,256]{1,0:T(8,128)(2,1)S(1)} custom-call(bf16[1024,2048]{1,0:T(8,128)(2,1)S(1)} %get-tuple-element.27.table, bf16[1040,2048]{1,0:T(8,128)(2,1)S(1)} %get-tuple-element.28.scaled, f32[2624,256]{1,0:T(8,128)S(1)} %gram_second.1.pair, f32[2624,256]{1,0:T(8,128)S(1)} %gram_third.1.single), custom_call_target="tpu_custom_call" | custom-call | flops 1000000000 | bytes 1000 | tf_op jit(solution)/shard_map/gram_others/pallas_call | solution.py:488
  34.6 0.0 copy-start.2
  34.6 0.6 %collective-permute-start.7 = (bf16[1552,256]{1,0:T(8,128)(2,1)S(1)}, bf16[1552,256]{1,0:T(8,128)(2,1)S(1)}, u32[]{:S(2)}, u32[]{:S(2)}) collective-permute-start(bf16[1552,256]{1,0:T(8,128)(2,1)S(1)} %gram_others.1.own_others), channel_id=1, source_target_pairs={{0,1},{1,0},{2,3},{3,2},{4,5},{5,4},{6,7},{7,6},{8,9},{9,8},{10,11... | collective-permute-start | bytes 2383880 | tf_op jit(solution)/shard_map/ppermute | solution.py:512
  35.1 0.0 collective-permute-done.6.other_first
  35.1 0.0 copy-done
  35.1 0.7 %middle.1 = (bf16[512,1024]{1,0:T(8,128)(2,1)S(1)}, bf16[16,2,32,256]{3,2,1,0:T(8,128)(2,1)S(1)}, bf16[16,2,32,256]{3,2,1,0:T(8,128)(2,1)S(1)}, f32[1024,256]{1,0:T(8,128)S(1)}) custom-call(bf16[200,128]{1,0:T(8,128)(2,1)S(1)} %copy-done.1, bf16[2048,256]{1,0:T(8,128)(2,1)S(1)} %get-tuple-element.26.own_first, ...), custom_call_target="tpu_custom_call" | custom-call | flops 1000000000 | bytes 1000 | tf_op jit(solution)/shard_map/middle/pallas_call | solution.py:488
  35.8 1.3 %collective-permute-done.7.other_others = bf16[1552,256]{1,0:T(8,128)(2,1)S(1)} collective-permute-done((bf16[1552,256]{1,0:T(8,128)(2,1)S(1)}, bf16[1552,256]{1,0:T(8,128)(2,1)S(1)}, u32[]{:S(2)}, u32[]{:S(2)}) %collective-permute-start.7) | collective-permute-done | bytes 794656 | tf_op jit(solution)/shard_map/ppermute | solution.py:512
  37.1 0.0 copy-done.2
  37.1 3.2 %tail.1 = (bf16[128,256]{1,0:T(8,128)(2,1)}, bf16[128,256]{1,0:T(8,128)(2,1)}, f32[256,256]{1,0:T(8,128)}, f32[1,512]{1,0:T(1,128)}) custom-call(bf16[2048,256]{1,0:T(8,128)(2,1)S(1)} %get-tuple-element.26.own_first, bf16[1552,256]{1,0:T(8,128)(2,1)S(1)} %gram_others.1.own_others, bf16[2048,256]{1,0:T(8,128)(2,1)S(1)} %collective-permute-done.6.other_first, ...), custom_call_target="tpu_custom_call" | custom-call | tf_op jit(solution)/shard_map/tail/pallas_call | solution.py:521
  (2 shorter events, 0.0 us)
Async XLA Ops:
  2.5 7.6 %collective-permute-start.2 = (bf16[200,128]{1,0:T(8,128)(2,1)}, bf16[200,128]{1,0:T(8,128)(2,1)S(1)}, u32[]{:S(2)}, u32[]{:S(2)}) collective-permute-start(bf16[200,128]{1,0:T(8,128)(2,1)} %get-tuple-element.21.source.payload), channel_id=1, source_target_pairs={{0,24},{8,16},{16,8},{24,0},{1,25},{9,17},{17,9},{25,1},{2,26},{10... | collective-permute-start | bytes 153608 | tf_op jit(solution)/shard_map/ppermute | solution.py:439
  7.6 5.2 %collective-permute-start.1 = (bf16[200,128]{1,0:T(8,128)(2,1)}, bf16[200,128]{1,0:T(8,128)(2,1)S(1)}, u32[]{:S(2)}, u32[]{:S(2)}) collective-permute-start(bf16[200,128]{1,0:T(8,128)(2,1)} %get-tuple-element.21.source.payload), channel_id=1, source_target_pairs={{0,16},{8,24},{16,0},{24,8},{1,17},{9,25},{17,1},{25,9},{2,18},{10... | collective-permute-start | bytes 153608 | tf_op jit(solution)/shard_map/ppermute | solution.py:439
  7.6 5.2 %collective-permute-start = (bf16[200,128]{1,0:T(8,128)(2,1)}, bf16[200,128]{1,0:T(8,128)(2,1)S(1)}, u32[]{:S(2)}, u32[]{:S(2)}) collective-permute-start(bf16[200,128]{1,0:T(8,128)(2,1)} %get-tuple-element.21.source.payload), channel_id=1, source_target_pairs={{0,8},{8,0},{16,24},{24,16},{1,9},{9,1},{17,25},{25,17},{2,10},{10... | collective-permute-start | bytes 153608 | tf_op jit(solution)/shard_map/ppermute | solution.py:439
  8.3 0.8 %copy-start.1 = (bf16[200,128]{1,0:T(8,128)(2,1)S(1)}, bf16[200,128]{1,0:T(8,128)(2,1)}, u32[]{:S(2)}) copy-start(bf16[200,128]{1,0:T(8,128)(2,1)} %get-tuple-element.21.source.payload) | copy-start | bytes 153604
  12.9 8.0 %collective-permute-start.5 = (bf16[4,200,128]{2,1,0:T(8,128)(2,1)S(1)}, bf16[4,200,128]{2,1,0:T(8,128)(2,1)S(1)}, u32[]{:S(2)}, u32[]{:S(2)}) collective-permute-start(bf16[4,200,128]{2,1,0:T(8,128)(2,1)S(1)} %collect.1.lists.near_0_), channel_id=1, source_target_pairs={{0,2},{2,0},{1,3},{3,1},{4,6},{6,4},{5,7},{7,5},{8,10},{10,8},{9,1... | collective-permute-start | bytes 614408 | tf_op jit(solution)/shard_map/ppermute | solution.py:461
  14.4 10.6 %collective-permute-start.4 = (bf16[4,200,128]{2,1,0:T(8,128)(2,1)S(1)}, bf16[4,200,128]{2,1,0:T(8,128)(2,1)S(1)}, u32[]{:S(2)}, u32[]{:S(2)}) collective-permute-start(bf16[4,200,128]{2,1,0:T(8,128)(2,1)S(1)} %collect.1.lists.near_0_), channel_id=1, source_target_pairs={{0,4},{4,0},{1,5},{5,1},{2,6},{6,2},{3,7},{7,3},{8,12},{12,8},{9,1... | collective-permute-start | bytes 614408 | tf_op jit(solution)/shard_map/ppermute | solution.py:462
  16.0 13.2 %collective-permute-start.3 = (bf16[4,200,128]{2,1,0:T(8,128)(2,1)S(1)}, bf16[4,200,128]{2,1,0:T(8,128)(2,1)S(1)}, u32[]{:S(2)}, u32[]{:S(2)}) collective-permute-start(bf16[4,200,128]{2,1,0:T(8,128)(2,1)S(1)} %collect.1.lists.near_0_), channel_id=1, source_target_pairs={{0,6},{2,4},{4,2},{6,0},{1,7},{3,5},{5,3},{7,1},{8,14},{10,12},{12... | collective-permute-start | bytes 614408 | tf_op jit(solution)/shard_map/ppermute | solution.py:463
  32.3 2.8 %collective-permute-start.6 = (bf16[2048,256]{1,0:T(8,128)(2,1)S(1)}, bf16[2048,256]{1,0:T(8,128)(2,1)S(1)}, u32[]{:S(2)}, u32[]{:S(2)}) collective-permute-start(bf16[2048,256]{1,0:T(8,128)(2,1)S(1)} %get-tuple-element.26.own_first), channel_id=1, source_target_pairs={{0,1},{1,0},{2,3},{3,2},{4,5},{5,4},{6,7},{7,6},{8,9},{9,8},{10,11... | collective-permute-start | bytes 3145736 | tf_op jit(solution)/shard_map/ppermute | solution.py:508
  32.4 2.8 %copy-start = (bf16[256,256]{1,0:T(8,128)(2,1)S(1)}, bf16[256,256]{1,0:T(8,128)(2,1)}, u32[]{:S(2)}) copy-start(bf16[256,256]{1,0:T(8,128)(2,1)} %theta.3) | copy-start | bytes 393220
  34.6 2.5 %copy-start.2 = (f32[1,512]{1,0:T(1,128)S(1)}, f32[1,512]{1,0:T(1,128)}, u32[]{:S(2)}) copy-start(f32[1,512]{1,0:T(1,128)} %get-tuple-element.33.inverse) | copy-start | bytes 6148
  34.6 2.5 %collective-permute-start.7 = (bf16[1552,256]{1,0:T(8,128)(2,1)S(1)}, bf16[1552,256]{1,0:T(8,128)(2,1)S(1)}, u32[]{:S(2)}, u32[]{:S(2)}) collective-permute-start(bf16[1552,256]{1,0:T(8,128)(2,1)S(1)} %gram_others.1.own_others), channel_id=1, source_target_pairs={{0,1},{1,0},{2,3},{3,2},{4,5},{5,4},{6,7},{7,6},{8,9},{9,8},{10,11... | collective-permute-start | bytes 2383880 | tf_op jit(solution)/shard_map/ppermute | solution.py:512

commit v6 on v5

--- a/solution.py
+++ b/solution.py
@@ -277,15 +277,17 @@
     return spans
 
 
-def fill(lists, table, scaled):
-    shards = lists.shape[0]
+def members(group):
+    return [group.at[q] for q in range(group.shape[0])]
+
+
+def fill(shards, table, scaled):
     chunks = CHUNKS
     ents = table.shape[0]
-    sections = table.shape[1] // shards
+    sections = table.shape[1] // len(shards)
     ent_dev = TILE // (sections // TILE)
     scaled[ents:, :] = jnp.ones((scaled.shape[0] - ents, scaled.shape[1]), BF)
-    for q in range(shards):
-        indices = lists.at[q]
+    for q, indices in enumerate(shards):
         scale = jnp.concatenate(
             [indices[16 * chunks + c : 16 * chunks + c + 1, :] for c in range(chunks)], axis=1
         )
@@ -303,23 +305,46 @@
     return dot(scaled[b * TILE :, :], table[b * TILE : (b + 1) * TILE, :], NT)
 
 
-def first_kernel(lists, sums, table, scaled):
-    fill(lists, table, scaled)
+def shards_kernel(shards, sums, table, scaled):
+    fill(shards, table, scaled)
     for b, (start, end) in enumerate(column_rows(table.shape[0])):
         sums[start:end, :] = column(b, table, scaled)
 
 
-def second_kernel(lists, before, sums, table, scaled):
-    fill(lists, table, scaled)
+def own_kernel(payload, sums, table, scaled):
+    shards_kernel([payload], sums, table, scaled)
+
+
+def third_kernel(group, sums, table, scaled):
+    shards_kernel(members(group), sums, table, scaled)
+
+
+def layers_kernel(arrived, before, sums, table, scaled):
+    fill(arrived, table, scaled)
     for b, (start, end) in enumerate(column_rows(table.shape[0])):
         sums[start:end, :] = before[start:end, :] + column(b, table, scaled)
 
 
+def second_kernel(group, before, sums, table, scaled):
+    layers_kernel(members(group), before, sums, table, scaled)
+
+
+def degree_rows(*rows):
+    out = []
+    for row in rows:
+        top = row.astype(BF).astype(F32)
+        out += [top, row - top]
+    out.append(jnp.zeros((16 - len(out), TILE), F32))
+    return jnp.concatenate(out, axis=0).astype(BF)
+
+
 def last_kernel(lists, pair, single, near, third, first, table, scaled):
     ents = table.shape[0]
-    fill(lists, table, scaled)
-    total = pair[0:ents, :] + (single[0:ents, :] + dot(scaled[0:ents, :], table[0:TILE, :], NT))
-    first[0:ents, :] = total.astype(BF)
+    fill(members(lists), table, scaled)
+    start, end = column_rows(ents)[0]
+    total = pair[start:end, :] + (single[start:end, :] + column(0, table, scaled))
+    first[0:ents, :] = total[0:ents].astype(BF)
+    first[first.shape[0] - 16 :, :] = degree_rows(total[ents : ents + 1])
     at = ents
     for source in near + (third, lists):
         shards, height, _ = source.shape
@@ -337,21 +362,13 @@
     at = 0
     degrees = []
     for b, (start, end) in enumerate(column_rows(ents)):
-        size = end - start - 16
-        if b == 0:
-            start, size = end - 16, 0
-            product = dot(scaled[ents:, :], table[0:TILE, :], NT)
-        else:
-            product = column(b, table, scaled)
-        total = pair[start:end, :] + (single[start:end, :] + product)
         if b:
+            size = end - start - 16
+            total = pair[start:end, :] + (single[start:end, :] + column(b, table, scaled))
             others[at : at + size, :] = total[0:size].astype(BF)
-        at += size
-        degree = total[size : size + 1]
-        top = degree.astype(BF).astype(F32)
-        degrees += [top, degree - top]
-    degrees.append(jnp.zeros((16 - len(degrees), TILE), F32))
-    others[at : at + 16, :] = jnp.concatenate(degrees, axis=0).astype(BF)
+            at += size
+            degrees.append(total[size : size + 1])
+    others[at : at + 16, :] = degree_rows(*degrees)
 
 
 def tail_kernel(
@@ -365,10 +382,13 @@
     width = theta.shape[0]
     per_group = feats.shape[0] // (ents // ent_dev)
     mine = lax.axis_index("z") * 2 + lax.axis_index("y")
-    base = own_others.shape[0] - 16
-    degree_rows = own_others[base:, :].astype(F32) + other_others[base:, :].astype(F32)
+    degrees = []
+    for refs, count in (((own_first, other_first), 1), ((own_others, other_others), tiles - 1)):
+        base = refs[0].shape[0] - 16
+        parts = refs[0][base:, :].astype(F32) + refs[1][base:, :].astype(F32)
+        degrees += [parts[2 * n : 2 * n + 1] + parts[2 * n + 1 : 2 * n + 2] for n in range(count)]
     for b in range(tiles):
-        row = lax.rsqrt(1.0 + (degree_rows[2 * b : 2 * b + 1] + degree_rows[2 * b + 1 : 2 * b + 2]))
+        row = lax.rsqrt(1.0 + degrees[b])
         for h in range(TILE // 128):
             at = b * TILE + h * 128
             scale[at : at + 128, :] = row_to_column(row[:, h * 128 : (h + 1) * 128])
@@ -447,6 +467,22 @@
         compiler_params=params(),
         name="hold",
     )(payload)
+    rows = column_rows(ents)[-1][1]
+    def step(kernel, shards, name, inputs):
+        wide = shards * sec_dev
+        return pl.pallas_call(
+            kernel,
+            out_shape=jax.ShapeDtypeStruct((rows, TILE), F32),
+            in_specs=jax.tree.map(lambda _: vmem(), list(inputs)),
+            out_specs=vmem(),
+            scratch_shapes=[pltpu.VMEM((ents, wide), BF), pltpu.VMEM((ents + 16, wide), BF)],
+            compiler_params=params(),
+            cost_estimate=pl.CostEstimate(flops=1000000000, bytes_accessed=1000, transcendentals=0),
+            name=name,
+        )(*inputs)
+
+    sums = step(own_kernel, 1, "gram_own", [held])
+    sums, by_layer = lax.optimization_barrier((sums, by_layer))
     near = pl.pallas_call(
         collect_kernel,
         out_shape=jax.ShapeDtypeStruct((group,) + payload.shape, BF),
@@ -456,34 +492,16 @@
         name="collect",
     )(held, *by_layer)
 
-    far = [
-        near,
-        lax.ppermute(near, "x", swap),
-        lax.ppermute(near, "y", swap),
-        lax.ppermute(near, ("y", "x"), [(i, i ^ 3) for i in range(group)]),
-    ]
-    rows = column_rows(ents)[-1][1]
-    scratch = [pltpu.VMEM((ents, group * sec_dev), BF), pltpu.VMEM((ents + 16, group * sec_dev), BF)]
-
-    def step(kernel, shape, kind, name, inputs):
-        return pl.pallas_call(
-            kernel,
-            out_shape=jax.ShapeDtypeStruct(shape, kind),
-            in_specs=jax.tree.map(lambda _: vmem(), list(inputs)),
-            out_specs=vmem(),
-            scratch_shapes=scratch,
-            compiler_params=params(),
-            cost_estimate=pl.CostEstimate(
-                flops=1000000000, bytes_accessed=1000, transcendentals=0
-            ),
-            name=name,
-        )(*inputs)
-
-    sums = step(first_kernel, (rows, TILE), F32, "gram_first", [far[0]])
-    pair = step(second_kernel, (rows, TILE), F32, "gram_second", [far[1], sums])
+    by_x, by_y = lax.ppermute(near, "x", swap), lax.ppermute(near, "y", swap)
+    sums = step(layers_kernel, layers - 1, "gram_layers", [by_layer, sums])
+    later, sums = lax.optimization_barrier((near, sums))
+    by_both = lax.ppermute(later, ("y", "x"), [(i, i ^ 3) for i in range(group)])
+    far = [near, by_x, by_y, by_both]
+    pair = step(second_kernel, group, "gram_second", [far[1], sums])
     third, pair = lax.optimization_barrier((far[2], pair))
-    single = step(first_kernel, (rows, TILE), F32, "gram_third", [third])
+    single = step(third_kernel, group, "gram_third", [third])
     fourth, single = lax.optimization_barrier((far[3], single))
+
     def plain(kernel, outs, name, inputs):
         return pl.pallas_call(
             kernel,
@@ -498,7 +516,7 @@
     own_first, table, scaled = plain(
         last_kernel,
         [
-            ((ents + layers * group * 2 * share, TILE), BF),
+            ((ents + layers * group * 2 * share + 16, TILE), BF),
             ((ents, group * sec_dev), BF),
             ((ents + 16, group * sec_dev), BF),
         ],

time: 40.5 us -> 39.1 us (0.965)
  waiting for transfers between devices: 5.35 us -> 3.81 us
    ppermute x3, waiting for transfers between devices: 3.74 us -> 2.55 us  [layer(): return lax.ppermute(payload, 'z', [(i, i ^ d) for i in range(layers)])]
    pallas_call x3 -> x4, Pallas kernels: 12.3 us -> 12.6 us  [step(): pl.pallas_call(kernel, out_shape=jax.ShapeDtypeStruct((rows, TILE), F32),...]
  transfers between devices with their start and end apart: 8 -> 8, of which waited for: 4 -> 3; matrix products, arithmetic and copies ran while one was open for 0% -> 0% of each run, Pallas kernels for 38% -> 39%
where the time goes in v6:
time: 39.1 us; the launch traced here: 38.8 us
  Pallas kernels  23.4 us (60%)
  starting transfers between devices  10 us (26%)
  waiting for transfers between devices  3.81 us (10%)
  local copies, waits for them, and re-layouts  0.85 us (2%)
  between operations  0.75 us (2%)
    pallas_call x4, Pallas kernels, step(): pl.pallas_call(kernel, out_shape=jax.ShapeDtypeStruct((rows, TILE), F32),...  12.6 us
    ppermute x3, starting transfers between devices, layer(): return lax.ppermute(payload, 'z', [(i, i ^ d) for i in range(layers)])  5.76 us
    pallas_call x3, Pallas kernels, plain(): pl.pallas_call(kernel, out_shape=[jax.ShapeDtypeStruct(shape, kind) for s...  5.73 us
    pallas_call x1, Pallas kernels, dense_body(): pl.pallas_call(tail_kernel, out_shape=(jax.ShapeDtypeStruct((ent_dev, wid...  3.23 us
    ppermute x2, starting transfers between devices, dense_body(): by_x, by_y = (lax.ppermute(near, 'x', swap), lax.ppermute(near, 'y', swap))  3.08 us
    ppermute x3, waiting for transfers between devices, layer(): return lax.ppermute(payload, 'z', [(i, i ^ d) for i in range(layers)])  2.55 us
    pallas_call x1, Pallas kernels, dense_body(): pl.pallas_call(prep_kernel, out_shape=(jax.ShapeDtypeStruct((height + 4 *...  1.87 us
    ppermute x1, waiting for transfers between devices, dense_body(): other_others = lax.ppermute(own_others, 'core', swap)  1.07 us
  transfers between devices with their start and end apart: 8, of which 3 were waited for; matrix products, arithmetic and copies ran while one was open for 0% of the time, Pallas kernels for 39%

profile of v6, /device:TPU:0, one launch (start us, length us, event | category | flops | bytes accessed | tf_op | source)
XLA Modules:
  0.0 38.8 jit_solution(17622585298070988247)
XLA Ops:
  0.6 1.9 %prep.1 = (bf16[200,128]{1,0:T(8,128)(2,1)}, f32[1,512]{1,0:T(1,128)}) custom-call(s32[1,8]{1,0:T(1,128)} %counts.1, s32[1,8,512]{2,1,0:T(8,128)} %rows.1, s32[1,8,512]{2,1,0:T(8,128)} %cols.1, f32[1,512]{1,0:T(1,128)} %bitcast.2, bf16[128,256]{1,0:T(8,128)(2,1)} %features.1, bf16[128,256]{1,0:T(8,128)(2,1)} %cotangent.1), custom_call_target="tpu_custom_call" | custom-call | tf_op jit(solution)/shard_map/prep/pallas_call | solution.py:439
  2.5 5.1 %collective-permute-start.2 = (bf16[200,128]{1,0:T(8,128)(2,1)}, bf16[200,128]{1,0:T(8,128)(2,1)S(1)}, u32[]{:S(2)}, u32[]{:S(2)}) collective-permute-start(bf16[200,128]{1,0:T(8,128)(2,1)} %get-tuple-element.27.source.payload), channel_id=1, source_target_pairs={{0,24},{8,16},{16,8},{24,0},{1,25},{9,17},{17,9},{25,1},{2,26},{10... | collective-permute-start | bytes 153608 | tf_op jit(solution)/shard_map/ppermute | solution.py:459
  7.6 0.0 collective-permute-start.1
  7.6 0.6 %collective-permute-start = (bf16[200,128]{1,0:T(8,128)(2,1)}, bf16[200,128]{1,0:T(8,128)(2,1)S(1)}, u32[]{:S(2)}, u32[]{:S(2)}) collective-permute-start(bf16[200,128]{1,0:T(8,128)(2,1)} %get-tuple-element.27.source.payload), channel_id=1, source_target_pairs={{0,8},{8,0},{16,24},{24,16},{1,9},{9,1},{17,25},{25,17},{2,10},{10... | collective-permute-start | bytes 153608 | tf_op jit(solution)/shard_map/ppermute | solution.py:459
  8.3 0.0 copy-start.1
  8.3 0.8 %copy-done.1 = bf16[200,128]{1,0:T(8,128)(2,1)S(1)} copy-done((bf16[200,128]{1,0:T(8,128)(2,1)S(1)}, bf16[200,128]{1,0:T(8,128)(2,1)}, u32[]{:S(2)}) %copy-start.1) | copy-done | bytes 51224
  9.1 1.2 %gram_own.1.before = f32[2624,256]{1,0:T(8,128)S(1)} custom-call(bf16[200,128]{1,0:T(8,128)(2,1)S(1)} %hold.1.payload.own), custom_call_target="tpu_custom_call" | custom-call | flops 1000000000 | bytes 1000 | tf_op jit(solution)/shard_map/gram_own/pallas_call | solution.py:473
  10.3 0.0 collective-permute-done.2.third.arrived_2_
  10.3 2.5 %collective-permute-done.1.second.arrived_1_ = bf16[200,128]{1,0:T(8,128)(2,1)S(1)} collective-permute-done((bf16[200,128]{1,0:T(8,128)(2,1)}, bf16[200,128]{1,0:T(8,128)(2,1)S(1)}, u32[]{:S(2)}, u32[]{:S(2)}) %collective-permute-start.1) | collective-permute-done | bytes 51232 | tf_op jit(solution)/shard_map/ppermute | solution.py:459
  12.8 0.0 collective-permute-done.first.arrived_0_
  12.9 1.6 %collective-permute-start.5 = (bf16[4,200,128]{2,1,0:T(8,128)(2,1)S(1)}, bf16[4,200,128]{2,1,0:T(8,128)(2,1)S(1)}, u32[]{:S(2)}, u32[]{:S(2)}) collective-permute-start(bf16[4,200,128]{2,1,0:T(8,128)(2,1)S(1)} %collect.1.near_0_), channel_id=1, source_target_pairs={{0,2},{2,0},{1,3},{3,1},{4,6},{6,4},{5,7},{7,5},{8,10},{10,8},{9,1... | collective-permute-start | bytes 614408 | tf_op jit(solution)/shard_map/ppermute | solution.py:495
  14.4 1.5 %collective-permute-start.4 = (bf16[4,200,128]{2,1,0:T(8,128)(2,1)S(1)}, bf16[4,200,128]{2,1,0:T(8,128)(2,1)S(1)}, u32[]{:S(2)}, u32[]{:S(2)}) collective-permute-start(bf16[4,200,128]{2,1,0:T(8,128)(2,1)S(1)} %collect.1.near_0_), channel_id=1, source_target_pairs={{0,4},{4,0},{1,5},{5,1},{2,6},{6,2},{3,7},{7,3},{8,12},{12,8},{9,1... | collective-permute-start | bytes 614408 | tf_op jit(solution)/shard_map/ppermute | solution.py:495
  16.0 3.1 %gram_layers.1.before = f32[2624,256]{1,0:T(8,128)S(1)} custom-call(bf16[200,128]{1,0:T(8,128)(2,1)S(1)} %collective-permute-done.first.arrived_0_, bf16[200,128]{1,0:T(8,128)(2,1)S(1)} %collective-permute-done.1.second.arrived_1_, bf16[200,128]{1,0:T(8,128)(2,1)S(1)} %collective-permute-done.2.third.arrived_2_, f32[2624,256]{1,0:T(8,128)S(1)} %gram_own.1.before), custom_call_target="tpu_custom_call" | custom-call | flops 1000000000 | bytes 1000 | tf_op jit(solution)/shard_map/gram_layers/pallas_call | solution.py:473
  19.1 0.6 %collective-permute-start.3 = (bf16[4,200,128]{2,1,0:T(8,128)(2,1)S(1)}, bf16[4,200,128]{2,1,0:T(8,128)(2,1)S(1)}, u32[]{:S(2)}, u32[]{:S(2)}) collective-permute-start(bf16[4,200,128]{2,1,0:T(8,128)(2,1)S(1)} %collect.1.near_0_), channel_id=1, source_target_pairs={{0,6},{2,4},{4,2},{6,0},{1,7},{3,5},{5,3},{7,1},{8,14},{10,12},{12... | collective-permute-start | bytes 614408 | tf_op jit(solution)/shard_map/ppermute | solution.py:498
  19.7 0.0 collective-permute-done.5.group.near_1_
  19.7 4.1 %gram_second.1.pair = f32[2624,256]{1,0:T(8,128)S(1)} custom-call(bf16[4,200,128]{2,1,0:T(8,128)(2,1)S(1)} %collective-permute-done.5.group.near_1_, f32[2624,256]{1,0:T(8,128)S(1)} %gram_layers.1.before), custom_call_target="tpu_custom_call" | custom-call | flops 1000000000 | bytes 1000 | tf_op jit(solution)/shard_map/gram_second/pallas_call | solution.py:473
  23.8 0.0 collective-permute-done.4.group.third
  23.8 4.1 %gram_third.1.single = f32[2624,256]{1,0:T(8,128)S(1)} custom-call(bf16[4,200,128]{2,1,0:T(8,128)(2,1)S(1)} %collective-permute-done.4.group.third), custom_call_target="tpu_custom_call" | custom-call | flops 1000000000 | bytes 1000 | tf_op jit(solution)/shard_map/gram_third/pallas_call | solution.py:473
  27.9 0.0 collective-permute-done.3.lists
  27.9 3.2 %gram_last.1 = (bf16[2064,256]{1,0:T(8,128)(2,1)S(1)}, bf16[1024,2048]{1,0:T(8,128)(2,1)S(1)}, bf16[1040,2048]{1,0:T(8,128)(2,1)S(1)}) custom-call(bf16[4,200,128]{2,1,0:T(8,128)(2,1)S(1)} %collective-permute-done.3.lists, f32[2624,256]{1,0:T(8,128)S(1)} %gram_second.1.pair, f32[2624,256]{1,0:T(8,128)S(1)} %gram_third.1.single, ...), custom_call_target="tpu_custom_call" | custom-call | flops 1000000000 | bytes 1000 | tf_op jit(solution)/shard_map/gram_last/pallas_call | solution.py:506
  31.1 0.1 collective-permute-start.6
  31.2 0.0 copy-start
  31.2 1.9 %gram_others.1.own_others = bf16[1552,256]{1,0:T(8,128)(2,1)S(1)} custom-call(bf16[1024,2048]{1,0:T(8,128)(2,1)S(1)} %get-tuple-element.39.table, bf16[1040,2048]{1,0:T(8,128)(2,1)S(1)} %get-tuple-element.40.scaled, f32[2624,256]{1,0:T(8,128)S(1)} %gram_second.1.pair, f32[2624,256]{1,0:T(8,128)S(1)} %gram_third.1.single), custom_call_target="tpu_custom_call" | custom-call | flops 1000000000 | bytes 1000 | tf_op jit(solution)/shard_map/gram_others/pallas_call | solution.py:506
  33.1 0.0 copy-start.2
  33.1 0.6 %collective-permute-start.7 = (bf16[1552,256]{1,0:T(8,128)(2,1)S(1)}, bf16[1552,256]{1,0:T(8,128)(2,1)S(1)}, u32[]{:S(2)}, u32[]{:S(2)}) collective-permute-start(bf16[1552,256]{1,0:T(8,128)(2,1)S(1)} %gram_others.1.own_others), channel_id=1, source_target_pairs={{0,1},{1,0},{2,3},{3,2},{4,5},{5,4},{6,7},{7,6},{8,9},{9,8},{10,11... | collective-permute-start | bytes 2383880 | tf_op jit(solution)/shard_map/ppermute | solution.py:530
  33.7 0.2 collective-permute-done.6.other_first
  33.8 0.0 copy-done
  33.8 0.7 %middle.1 = (bf16[512,1024]{1,0:T(8,128)(2,1)S(1)}, bf16[16,2,32,256]{3,2,1,0:T(8,128)(2,1)S(1)}, bf16[16,2,32,256]{3,2,1,0:T(8,128)(2,1)S(1)}, f32[1024,256]{1,0:T(8,128)S(1)}) custom-call(bf16[200,128]{1,0:T(8,128)(2,1)S(1)} %copy-done.1, bf16[2064,256]{1,0:T(8,128)(2,1)S(1)} %get-tuple-element.38.own_first, ...), custom_call_target="tpu_custom_call" | custom-call | flops 1000000000 | bytes 1000 | tf_op jit(solution)/shard_map/middle/pallas_call | solution.py:506
  34.5 1.1 %collective-permute-done.7.other_others = bf16[1552,256]{1,0:T(8,128)(2,1)S(1)} collective-permute-done((bf16[1552,256]{1,0:T(8,128)(2,1)S(1)}, bf16[1552,256]{1,0:T(8,128)(2,1)S(1)}, u32[]{:S(2)}, u32[]{:S(2)}) %collective-permute-start.7) | collective-permute-done | bytes 794656 | tf_op jit(solution)/shard_map/ppermute | solution.py:530
  35.6 0.0 copy-done.2
  35.6 3.2 %tail.1 = (bf16[128,256]{1,0:T(8,128)(2,1)}, bf16[128,256]{1,0:T(8,128)(2,1)}, f32[256,256]{1,0:T(8,128)}, f32[1,512]{1,0:T(1,128)}) custom-call(bf16[2064,256]{1,0:T(8,128)(2,1)S(1)} %get-tuple-element.38.own_first, bf16[1552,256]{1,0:T(8,128)(2,1)S(1)} %gram_others.1.own_others, bf16[2064,256]{1,0:T(8,128)(2,1)S(1)} %collective-permute-done.6.other_first, ...), custom_call_target="tpu_custom_call" | custom-call | tf_op jit(solution)/shard_map/tail/pallas_call | solution.py:539
  (2 shorter events, 0.0 us)
Async XLA Ops:
  2.5 7.8 %collective-permute-start.2 = (bf16[200,128]{1,0:T(8,128)(2,1)}, bf16[200,128]{1,0:T(8,128)(2,1)S(1)}, u32[]{:S(2)}, u32[]{:S(2)}) collective-permute-start(bf16[200,128]{1,0:T(8,128)(2,1)} %get-tuple-element.27.source.payload), channel_id=1, source_target_pairs={{0,24},{8,16},{16,8},{24,0},{1,25},{9,17},{17,9},{25,1},{2,26},{10... | collective-permute-start | bytes 153608 | tf_op jit(solution)/shard_map/ppermute | solution.py:459
  7.6 5.2 %collective-permute-start.1 = (bf16[200,128]{1,0:T(8,128)(2,1)}, bf16[200,128]{1,0:T(8,128)(2,1)S(1)}, u32[]{:S(2)}, u32[]{:S(2)}) collective-permute-start(bf16[200,128]{1,0:T(8,128)(2,1)} %get-tuple-element.27.source.payload), channel_id=1, source_target_pairs={{0,16},{8,24},{16,0},{24,8},{1,17},{9,25},{17,1},{25,9},{2,18},{10... | collective-permute-start | bytes 153608 | tf_op jit(solution)/shard_map/ppermute | solution.py:459
  7.6 5.2 %collective-permute-start = (bf16[200,128]{1,0:T(8,128)(2,1)}, bf16[200,128]{1,0:T(8,128)(2,1)S(1)}, u32[]{:S(2)}, u32[]{:S(2)}) collective-permute-start(bf16[200,128]{1,0:T(8,128)(2,1)} %get-tuple-element.27.source.payload), channel_id=1, source_target_pairs={{0,8},{8,0},{16,24},{24,16},{1,9},{9,1},{17,25},{25,17},{2,10},{10... | collective-permute-start | bytes 153608 | tf_op jit(solution)/shard_map/ppermute | solution.py:459
  8.3 0.8 %copy-start.1 = (bf16[200,128]{1,0:T(8,128)(2,1)S(1)}, bf16[200,128]{1,0:T(8,128)(2,1)}, u32[]{:S(2)}) copy-start(bf16[200,128]{1,0:T(8,128)(2,1)} %get-tuple-element.27.source.payload) | copy-start | bytes 153604
  12.9 6.8 %collective-permute-start.5 = (bf16[4,200,128]{2,1,0:T(8,128)(2,1)S(1)}, bf16[4,200,128]{2,1,0:T(8,128)(2,1)S(1)}, u32[]{:S(2)}, u32[]{:S(2)}) collective-permute-start(bf16[4,200,128]{2,1,0:T(8,128)(2,1)S(1)} %collect.1.near_0_), channel_id=1, source_target_pairs={{0,2},{2,0},{1,3},{3,1},{4,6},{6,4},{5,7},{7,5},{8,10},{10,8},{9,1... | collective-permute-start | bytes 614408 | tf_op jit(solution)/shard_map/ppermute | solution.py:495
  14.4 9.4 %collective-permute-start.4 = (bf16[4,200,128]{2,1,0:T(8,128)(2,1)S(1)}, bf16[4,200,128]{2,1,0:T(8,128)(2,1)S(1)}, u32[]{:S(2)}, u32[]{:S(2)}) collective-permute-start(bf16[4,200,128]{2,1,0:T(8,128)(2,1)S(1)} %collect.1.near_0_), channel_id=1, source_target_pairs={{0,4},{4,0},{1,5},{5,1},{2,6},{6,2},{3,7},{7,3},{8,12},{12,8},{9,1... | collective-permute-start | bytes 614408 | tf_op jit(solution)/shard_map/ppermute | solution.py:495
  19.1 8.8 %collective-permute-start.3 = (bf16[4,200,128]{2,1,0:T(8,128)(2,1)S(1)}, bf16[4,200,128]{2,1,0:T(8,128)(2,1)S(1)}, u32[]{:S(2)}, u32[]{:S(2)}) collective-permute-start(bf16[4,200,128]{2,1,0:T(8,128)(2,1)S(1)} %collect.1.near_0_), channel_id=1, source_target_pairs={{0,6},{2,4},{4,2},{6,0},{1,7},{3,5},{5,3},{7,1},{8,14},{10,12},{12... | collective-permute-start | bytes 614408 | tf_op jit(solution)/shard_map/ppermute | solution.py:498
  31.1 2.7 %collective-permute-start.6 = (bf16[2064,256]{1,0:T(8,128)(2,1)S(1)}, bf16[2064,256]{1,0:T(8,128)(2,1)S(1)}, u32[]{:S(2)}, u32[]{:S(2)}) collective-permute-start(bf16[2064,256]{1,0:T(8,128)(2,1)S(1)} %get-tuple-element.38.own_first), channel_id=1, source_target_pairs={{0,1},{1,0},{2,3},{3,2},{4,5},{5,4},{6,7},{7,6},{8,9},{9,8},{10,11... | collective-permute-start | bytes 3170312 | tf_op jit(solution)/shard_map/ppermute | solution.py:526
  31.2 2.7 %copy-start = (bf16[256,256]{1,0:T(8,128)(2,1)S(1)}, bf16[256,256]{1,0:T(8,128)(2,1)}, u32[]{:S(2)}) copy-start(bf16[256,256]{1,0:T(8,128)(2,1)} %theta.3) | copy-start | bytes 393220
  33.1 2.5 %copy-start.2 = (f32[1,512]{1,0:T(1,128)S(1)}, f32[1,512]{1,0:T(1,128)}, u32[]{:S(2)}) copy-start(f32[1,512]{1,0:T(1,128)} %get-tuple-element.45.inverse) | copy-start | bytes 6148
  33.1 2.5 %collective-permute-start.7 = (bf16[1552,256]{1,0:T(8,128)(2,1)S(1)}, bf16[1552,256]{1,0:T(8,128)(2,1)S(1)}, u32[]{:S(2)}, u32[]{:S(2)}) collective-permute-start(bf16[1552,256]{1,0:T(8,128)(2,1)S(1)} %gram_others.1.own_others), channel_id=1, source_target_pairs={{0,1},{1,0},{2,3},{3,2},{4,5},{5,4},{6,7},{7,6},{8,9},{9,8},{10,11... | collective-permute-start | bytes 2383880 | tf_op jit(solution)/shard_map/ppermute | solution.py:530

commit v7 on v6

--- a/solution.py
+++ b/solution.py
@@ -194,13 +194,14 @@
     part = lax.shift_right_logical(row_ids, SHIFT)
     high = jnp.where(live, part * ent_dev + cols_here[...], -1).astype(F32)
     low = jnp.where(live, row_ids & (TILE - 1), -1).astype(F32)
-    part = part.astype(F32)
-    degree = jnp.zeros((16, TILE), F32)
+    chunk = lax.shift_right_logical(row_ids, 7).astype(F32)
+    place = jnp.where(live, row_ids & 127, -1).astype(F32)
+    degree = jnp.zeros((16, 128), F32)
     for j in range(blocks):
         degree = degree + dot(
-            one_hot(part[j : j + 1].astype(BF), 16), one_hot(low[j : j + 1].astype(BF)), NT
+            one_hot(chunk[j : j + 1].astype(BF), 16), one_hot(place[j : j + 1].astype(BF), 128), NT
         )
-    degree = jnp.concatenate([degree[0:1], degree[1:2]], axis=1)
+    degree = jnp.concatenate([degree[c : c + 1] for c in range(weight.shape[1] // 128)], axis=1)
     inverse[...] = 1.0 / (1.0 + degree)
     scale = weight_here[...] / (1.0 + degree)
     indices = jnp.concatenate([high, low], axis=0).astype(BF)

time: 39.1 us -> 38.9 us (level)
  no operation moved by 1% of the time
where the time goes in v7:
time: 38.9 us; the launch traced here: 38.7 us
  Pallas kernels  23.3 us (60%)
  starting transfers between devices  10 us (26%)
  waiting for transfers between devices  3.81 us (10%)
  local copies, waits for them, and re-layouts  0.85 us (2%)
  between operations  0.75 us (2%)
    pallas_call x4, Pallas kernels, step(): pl.pallas_call(kernel, out_shape=jax.ShapeDtypeStruct((rows, TILE), F32),...  12.6 us
    ppermute x3, starting transfers between devices, layer(): return lax.ppermute(payload, 'z', [(i, i ^ d) for i in range(layers)])  5.76 us
    pallas_call x3, Pallas kernels, plain(): pl.pallas_call(kernel, out_shape=[jax.ShapeDtypeStruct(shape, kind) for s...  5.73 us
    pallas_call x1, Pallas kernels, dense_body(): pl.pallas_call(tail_kernel, out_shape=(jax.ShapeDtypeStruct((ent_dev, wid...  3.23 us
    ppermute x2, starting transfers between devices, dense_body(): by_x, by_y = (lax.ppermute(near, 'x', swap), lax.ppermute(near, 'y', swap))  3.08 us
    ppermute x3, waiting for transfers between devices, layer(): return lax.ppermute(payload, 'z', [(i, i ^ d) for i in range(layers)])  2.55 us
    pallas_call x1, Pallas kernels, dense_body(): pl.pallas_call(prep_kernel, out_shape=(jax.ShapeDtypeStruct((height + 4 *...  1.74 us
    ppermute x1, waiting for transfers between devices, dense_body(): other_others = lax.ppermute(own_others, 'core', swap)  1.07 us
  transfers between devices with their start and end apart: 8, of which 3 were waited for; matrix products, arithmetic and copies ran while one was open for 0% of the time, Pallas kernels for 39%

profile of v7, /device:TPU:0, one launch (start us, length us, event | category | flops | bytes accessed | tf_op | source)
XLA Modules:
  0.0 38.7 jit_solution(5390505176399564739)
XLA Ops:
  0.6 1.7 %prep.1 = (bf16[200,128]{1,0:T(8,128)(2,1)}, f32[1,512]{1,0:T(1,128)}) custom-call(s32[1,8]{1,0:T(1,128)} %counts.1, s32[1,8,512]{2,1,0:T(8,128)} %rows.1, s32[1,8,512]{2,1,0:T(8,128)} %cols.1, f32[1,512]{1,0:T(1,128)} %bitcast.2, bf16[128,256]{1,0:T(8,128)(2,1)} %features.1, bf16[128,256]{1,0:T(8,128)(2,1)} %cotangent.1), custom_call_target="tpu_custom_call" | custom-call | tf_op jit(solution)/shard_map/prep/pallas_call | solution.py:440
  2.4 5.1 %collective-permute-start.2 = (bf16[200,128]{1,0:T(8,128)(2,1)}, bf16[200,128]{1,0:T(8,128)(2,1)S(1)}, u32[]{:S(2)}, u32[]{:S(2)}) collective-permute-start(bf16[200,128]{1,0:T(8,128)(2,1)} %get-tuple-element.27.source.payload), channel_id=1, source_target_pairs={{0,24},{8,16},{16,8},{24,0},{1,25},{9,17},{17,9},{25,1},{2,26},{10... | collective-permute-start | bytes 153608 | tf_op jit(solution)/shard_map/ppermute | solution.py:460
  7.5 0.0 collective-permute-start.1
  7.5 0.6 %collective-permute-start = (bf16[200,128]{1,0:T(8,128)(2,1)}, bf16[200,128]{1,0:T(8,128)(2,1)S(1)}, u32[]{:S(2)}, u32[]{:S(2)}) collective-permute-start(bf16[200,128]{1,0:T(8,128)(2,1)} %get-tuple-element.27.source.payload), channel_id=1, source_target_pairs={{0,8},{8,0},{16,24},{24,16},{1,9},{9,1},{17,25},{25,17},{2,10},{10... | collective-permute-start | bytes 153608 | tf_op jit(solution)/shard_map/ppermute | solution.py:460
  8.1 0.0 copy-start.1
  8.1 0.8 %copy-done.1 = bf16[200,128]{1,0:T(8,128)(2,1)S(1)} copy-done((bf16[200,128]{1,0:T(8,128)(2,1)S(1)}, bf16[200,128]{1,0:T(8,128)(2,1)}, u32[]{:S(2)}) %copy-start.1) | copy-done | bytes 51224
  9.0 1.2 %gram_own.1.before = f32[2624,256]{1,0:T(8,128)S(1)} custom-call(bf16[200,128]{1,0:T(8,128)(2,1)S(1)} %hold.1.payload.own), custom_call_target="tpu_custom_call" | custom-call | flops 1000000000 | bytes 1000 | tf_op jit(solution)/shard_map/gram_own/pallas_call | solution.py:474
  10.2 0.0 collective-permute-done.2.third.arrived_2_
  10.2 2.5 %collective-permute-done.1.second.arrived_1_ = bf16[200,128]{1,0:T(8,128)(2,1)S(1)} collective-permute-done((bf16[200,128]{1,0:T(8,128)(2,1)}, bf16[200,128]{1,0:T(8,128)(2,1)S(1)}, u32[]{:S(2)}, u32[]{:S(2)}) %collective-permute-start.1) | collective-permute-done | bytes 51232 | tf_op jit(solution)/shard_map/ppermute | solution.py:460
  12.7 0.0 collective-permute-done.first.arrived_0_
  12.8 1.6 %collective-permute-start.5 = (bf16[4,200,128]{2,1,0:T(8,128)(2,1)S(1)}, bf16[4,200,128]{2,1,0:T(8,128)(2,1)S(1)}, u32[]{:S(2)}, u32[]{:S(2)}) collective-permute-start(bf16[4,200,128]{2,1,0:T(8,128)(2,1)S(1)} %collect.1.near_0_), channel_id=1, source_target_pairs={{0,2},{2,0},{1,3},{3,1},{4,6},{6,4},{5,7},{7,5},{8,10},{10,8},{9,1... | collective-permute-start | bytes 614408 | tf_op jit(solution)/shard_map/ppermute | solution.py:496
  14.3 1.5 %collective-permute-start.4 = (bf16[4,200,128]{2,1,0:T(8,128)(2,1)S(1)}, bf16[4,200,128]{2,1,0:T(8,128)(2,1)S(1)}, u32[]{:S(2)}, u32[]{:S(2)}) collective-permute-start(bf16[4,200,128]{2,1,0:T(8,128)(2,1)S(1)} %collect.1.near_0_), channel_id=1, source_target_pairs={{0,4},{4,0},{1,5},{5,1},{2,6},{6,2},{3,7},{7,3},{8,12},{12,8},{9,1... | collective-permute-start | bytes 614408 | tf_op jit(solution)/shard_map/ppermute | solution.py:496
  15.8 3.1 %gram_layers.1.before = f32[2624,256]{1,0:T(8,128)S(1)} custom-call(bf16[200,128]{1,0:T(8,128)(2,1)S(1)} %collective-permute-done.first.arrived_0_, bf16[200,128]{1,0:T(8,128)(2,1)S(1)} %collective-permute-done.1.second.arrived_1_, bf16[200,128]{1,0:T(8,128)(2,1)S(1)} %collective-permute-done.2.third.arrived_2_, f32[2624,256]{1,0:T(8,128)S(1)} %gram_own.1.before), custom_call_target="tpu_custom_call" | custom-call | flops 1000000000 | bytes 1000 | tf_op jit(solution)/shard_map/gram_layers/pallas_call | solution.py:474
  19.0 0.5 %collective-permute-start.3 = (bf16[4,200,128]{2,1,0:T(8,128)(2,1)S(1)}, bf16[4,200,128]{2,1,0:T(8,128)(2,1)S(1)}, u32[]{:S(2)}, u32[]{:S(2)}) collective-permute-start(bf16[4,200,128]{2,1,0:T(8,128)(2,1)S(1)} %collect.1.near_0_), channel_id=1, source_target_pairs={{0,6},{2,4},{4,2},{6,0},{1,7},{3,5},{5,3},{7,1},{8,14},{10,12},{12... | collective-permute-start | bytes 614408 | tf_op jit(solution)/shard_map/ppermute | solution.py:499
  19.5 0.0 collective-permute-done.5.group.near_1_
  19.5 4.1 %gram_second.1.pair = f32[2624,256]{1,0:T(8,128)S(1)} custom-call(bf16[4,200,128]{2,1,0:T(8,128)(2,1)S(1)} %collective-permute-done.5.group.near_1_, f32[2624,256]{1,0:T(8,128)S(1)} %gram_layers.1.before), custom_call_target="tpu_custom_call" | custom-call | flops 1000000000 | bytes 1000 | tf_op jit(solution)/shard_map/gram_second/pallas_call | solution.py:474
  23.7 0.0 collective-permute-done.4.group.third
  23.7 4.1 %gram_third.1.single = f32[2624,256]{1,0:T(8,128)S(1)} custom-call(bf16[4,200,128]{2,1,0:T(8,128)(2,1)S(1)} %collective-permute-done.4.group.third), custom_call_target="tpu_custom_call" | custom-call | flops 1000000000 | bytes 1000 | tf_op jit(solution)/shard_map/gram_third/pallas_call | solution.py:474
  27.8 0.0 collective-permute-done.3.lists
  27.8 3.2 %gram_last.1 = (bf16[2064,256]{1,0:T(8,128)(2,1)S(1)}, bf16[1024,2048]{1,0:T(8,128)(2,1)S(1)}, bf16[1040,2048]{1,0:T(8,128)(2,1)S(1)}) custom-call(bf16[4,200,128]{2,1,0:T(8,128)(2,1)S(1)} %collective-permute-done.3.lists, f32[2624,256]{1,0:T(8,128)S(1)} %gram_second.1.pair, f32[2624,256]{1,0:T(8,128)S(1)} %gram_third.1.single, ...), custom_call_target="tpu_custom_call" | custom-call | flops 1000000000 | bytes 1000 | tf_op jit(solution)/shard_map/gram_last/pallas_call | solution.py:507
  31.0 0.1 collective-permute-start.6
  31.1 0.0 copy-start
  31.1 1.9 %gram_others.1.own_others = bf16[1552,256]{1,0:T(8,128)(2,1)S(1)} custom-call(bf16[1024,2048]{1,0:T(8,128)(2,1)S(1)} %get-tuple-element.39.table, bf16[1040,2048]{1,0:T(8,128)(2,1)S(1)} %get-tuple-element.40.scaled, f32[2624,256]{1,0:T(8,128)S(1)} %gram_second.1.pair, f32[2624,256]{1,0:T(8,128)S(1)} %gram_third.1.single), custom_call_target="tpu_custom_call" | custom-call | flops 1000000000 | bytes 1000 | tf_op jit(solution)/shard_map/gram_others/pallas_call | solution.py:507
  33.0 0.0 copy-start.2
  33.0 0.6 %collective-permute-start.7 = (bf16[1552,256]{1,0:T(8,128)(2,1)S(1)}, bf16[1552,256]{1,0:T(8,128)(2,1)S(1)}, u32[]{:S(2)}, u32[]{:S(2)}) collective-permute-start(bf16[1552,256]{1,0:T(8,128)(2,1)S(1)} %gram_others.1.own_others), channel_id=1, source_target_pairs={{0,1},{1,0},{2,3},{3,2},{4,5},{5,4},{6,7},{7,6},{8,9},{9,8},{10,11... | collective-permute-start | bytes 2383880 | tf_op jit(solution)/shard_map/ppermute | solution.py:531
  33.5 0.2 collective-permute-done.6.other_first
  33.7 0.0 copy-done
  33.7 0.7 %middle.1 = (bf16[512,1024]{1,0:T(8,128)(2,1)S(1)}, bf16[16,2,32,256]{3,2,1,0:T(8,128)(2,1)S(1)}, bf16[16,2,32,256]{3,2,1,0:T(8,128)(2,1)S(1)}, f32[1024,256]{1,0:T(8,128)S(1)}) custom-call(bf16[200,128]{1,0:T(8,128)(2,1)S(1)} %copy-done.1, bf16[2064,256]{1,0:T(8,128)(2,1)S(1)} %get-tuple-element.38.own_first, ...), custom_call_target="tpu_custom_call" | custom-call | flops 1000000000 | bytes 1000 | tf_op jit(solution)/shard_map/middle/pallas_call | solution.py:507
  34.4 1.1 %collective-permute-done.7.other_others = bf16[1552,256]{1,0:T(8,128)(2,1)S(1)} collective-permute-done((bf16[1552,256]{1,0:T(8,128)(2,1)S(1)}, bf16[1552,256]{1,0:T(8,128)(2,1)S(1)}, u32[]{:S(2)}, u32[]{:S(2)}) %collective-permute-start.7) | collective-permute-done | bytes 794656 | tf_op jit(solution)/shard_map/ppermute | solution.py:531
  35.5 0.0 copy-done.2
  35.5 3.2 %tail.1 = (bf16[128,256]{1,0:T(8,128)(2,1)}, bf16[128,256]{1,0:T(8,128)(2,1)}, f32[256,256]{1,0:T(8,128)}, f32[1,512]{1,0:T(1,128)}) custom-call(bf16[2064,256]{1,0:T(8,128)(2,1)S(1)} %get-tuple-element.38.own_first, bf16[1552,256]{1,0:T(8,128)(2,1)S(1)} %gram_others.1.own_others, bf16[2064,256]{1,0:T(8,128)(2,1)S(1)} %collective-permute-done.6.other_first, ...), custom_call_target="tpu_custom_call" | custom-call | tf_op jit(solution)/shard_map/tail/pallas_call | solution.py:540
  (2 shorter events, 0.0 us)
Async XLA Ops:
  2.4 7.8 %collective-permute-start.2 = (bf16[200,128]{1,0:T(8,128)(2,1)}, bf16[200,128]{1,0:T(8,128)(2,1)S(1)}, u32[]{:S(2)}, u32[]{:S(2)}) collective-permute-start(bf16[200,128]{1,0:T(8,128)(2,1)} %get-tuple-element.27.source.payload), channel_id=1, source_target_pairs={{0,24},{8,16},{16,8},{24,0},{1,25},{9,17},{17,9},{25,1},{2,26},{10... | collective-permute-start | bytes 153608 | tf_op jit(solution)/shard_map/ppermute | solution.py:460
  7.5 5.2 %collective-permute-start.1 = (bf16[200,128]{1,0:T(8,128)(2,1)}, bf16[200,128]{1,0:T(8,128)(2,1)S(1)}, u32[]{:S(2)}, u32[]{:S(2)}) collective-permute-start(bf16[200,128]{1,0:T(8,128)(2,1)} %get-tuple-element.27.source.payload), channel_id=1, source_target_pairs={{0,16},{8,24},{16,0},{24,8},{1,17},{9,25},{17,1},{25,9},{2,18},{10... | collective-permute-start | bytes 153608 | tf_op jit(solution)/shard_map/ppermute | solution.py:460
  7.5 5.2 %collective-permute-start = (bf16[200,128]{1,0:T(8,128)(2,1)}, bf16[200,128]{1,0:T(8,128)(2,1)S(1)}, u32[]{:S(2)}, u32[]{:S(2)}) collective-permute-start(bf16[200,128]{1,0:T(8,128)(2,1)} %get-tuple-element.27.source.payload), channel_id=1, source_target_pairs={{0,8},{8,0},{16,24},{24,16},{1,9},{9,1},{17,25},{25,17},{2,10},{10... | collective-permute-start | bytes 153608 | tf_op jit(solution)/shard_map/ppermute | solution.py:460
  8.1 0.8 %copy-start.1 = (bf16[200,128]{1,0:T(8,128)(2,1)S(1)}, bf16[200,128]{1,0:T(8,128)(2,1)}, u32[]{:S(2)}) copy-start(bf16[200,128]{1,0:T(8,128)(2,1)} %get-tuple-element.27.source.payload) | copy-start | bytes 153604
  12.8 6.8 %collective-permute-start.5 = (bf16[4,200,128]{2,1,0:T(8,128)(2,1)S(1)}, bf16[4,200,128]{2,1,0:T(8,128)(2,1)S(1)}, u32[]{:S(2)}, u32[]{:S(2)}) collective-permute-start(bf16[4,200,128]{2,1,0:T(8,128)(2,1)S(1)} %collect.1.near_0_), channel_id=1, source_target_pairs={{0,2},{2,0},{1,3},{3,1},{4,6},{6,4},{5,7},{7,5},{8,10},{10,8},{9,1... | collective-permute-start | bytes 614408 | tf_op jit(solution)/shard_map/ppermute | solution.py:496
  14.3 9.4 %collective-permute-start.4 = (bf16[4,200,128]{2,1,0:T(8,128)(2,1)S(1)}, bf16[4,200,128]{2,1,0:T(8,128)(2,1)S(1)}, u32[]{:S(2)}, u32[]{:S(2)}) collective-permute-start(bf16[4,200,128]{2,1,0:T(8,128)(2,1)S(1)} %collect.1.near_0_), channel_id=1, source_target_pairs={{0,4},{4,0},{1,5},{5,1},{2,6},{6,2},{3,7},{7,3},{8,12},{12,8},{9,1... | collective-permute-start | bytes 614408 | tf_op jit(solution)/shard_map/ppermute | solution.py:496
  19.0 8.8 %collective-permute-start.3 = (bf16[4,200,128]{2,1,0:T(8,128)(2,1)S(1)}, bf16[4,200,128]{2,1,0:T(8,128)(2,1)S(1)}, u32[]{:S(2)}, u32[]{:S(2)}) collective-permute-start(bf16[4,200,128]{2,1,0:T(8,128)(2,1)S(1)} %collect.1.near_0_), channel_id=1, source_target_pairs={{0,6},{2,4},{4,2},{6,0},{1,7},{3,5},{5,3},{7,1},{8,14},{10,12},{12... | collective-permute-start | bytes 614408 | tf_op jit(solution)/shard_map/ppermute | solution.py:499
  31.0 2.7 %collective-permute-start.6 = (bf16[2064,256]{1,0:T(8,128)(2,1)S(1)}, bf16[2064,256]{1,0:T(8,128)(2,1)S(1)}, u32[]{:S(2)}, u32[]{:S(2)}) collective-permute-start(bf16[2064,256]{1,0:T(8,128)(2,1)S(1)} %get-tuple-element.38.own_first), channel_id=1, source_target_pairs={{0,1},{1,0},{2,3},{3,2},{4,5},{5,4},{6,7},{7,6},{8,9},{9,8},{10,11... | collective-permute-start | bytes 3170312 | tf_op jit(solution)/shard_map/ppermute | solution.py:527
  31.1 2.7 %copy-start = (bf16[256,256]{1,0:T(8,128)(2,1)S(1)}, bf16[256,256]{1,0:T(8,128)(2,1)}, u32[]{:S(2)}) copy-start(bf16[256,256]{1,0:T(8,128)(2,1)} %theta.3) | copy-start | bytes 393220
  33.0 2.5 %copy-start.2 = (f32[1,512]{1,0:T(1,128)S(1)}, f32[1,512]{1,0:T(1,128)}, u32[]{:S(2)}) copy-start(f32[1,512]{1,0:T(1,128)} %get-tuple-element.45.inverse) | copy-start | bytes 6148
  33.0 2.5 %collective-permute-start.7 = (bf16[1552,256]{1,0:T(8,128)(2,1)S(1)}, bf16[1552,256]{1,0:T(8,128)(2,1)S(1)}, u32[]{:S(2)}, u32[]{:S(2)}) collective-permute-start(bf16[1552,256]{1,0:T(8,128)(2,1)S(1)} %gram_others.1.own_others), channel_id=1, source_target_pairs={{0,1},{1,0},{2,3},{3,2},{4,5},{5,4},{6,7},{7,6},{8,9},{9,8},{10,11... | collective-permute-start | bytes 2383880 | tf_op jit(solution)/shard_map/ppermute | solution.py:531
